TPU v7x, 256 devices: a whole 4x4x8 slice. The times are simulated.
256 devices in a mesh: ctx: 16 (over y_lo, z), fsdp: 16 (over y_hi, x, core).
Axes of the slice: x: 4, y: 4 (y_hi: 2, y_lo: 2; y = y_hi * 2 + y_lo), z: 8, core: 2. Of those that a mesh axis runs over, the one named last changes fastest.
Arguments:
- hidden_in: bfloat16 [16, 2048, 8192], P('fsdp', 'ctx'), may hold values from -600 to 600
- queries: bfloat16 [16, 2048, 4096], P('fsdp', 'ctx'), may hold values from -100 to 100
- kv_weight: bfloat16 [8192, 1024], P('fsdp'), may hold values from -0.0625 to 0.0625
- kv_bias: float32 [1024], replicated, may hold values from -3 to 3
- norm_gain: float32 [8192], replicated, may hold values from 0.1 to 1.9
- block_mask: int32 [16, 16, 16], P('fsdp'), may hold values from 0 to 1, as said below
Outputs:
- attended: bfloat16 [16, 2048, 4096], P('fsdp', 'ctx')
Inputs may be any that keep to these rules, and one draw needn't show every extreme that they name: block_mask is 1 on the diagonal and 0 above it; the first block of a pack is visible to every block.
All inputs are finite; a program needn't handle non-finite values.
Results may differ from a plain program's by a relative error of at most 0.0056.
Values may be sent and summed in bfloat16 or wider, within the bound.
No kernel may reach another device: no remote copies, remote signals or barrier semaphores. Data moves between devices by JAX's collectives and lax.ppermute only.
A program may use at most 64 MiB of HBM per device.

v0:
```python
import math

import jax
import jax.numpy as jnp
from jax import lax
from jax.sharding import PartitionSpec as P

H = 32
KVH = 4
HD = 128
BLK = 128


neg_floor = -1e30


def rotary(raw_keys, positions):
    key_count = raw_keys.shape[0]
    shaped = raw_keys.reshape(key_count, KVH, HD)
    half_dim = HD // 2
    inv_freq = jnp.exp(jnp.arange(half_dim, dtype=jnp.float32) * (-2.0 * math.log(1000000.0) / HD))
    angle = positions.astype(jnp.float32)[:, None] * inv_freq[None, :]
    cosine = jnp.cos(angle)[:, None, :]
    sine_part = jnp.sin(angle)[:, None, :]
    first_half = shaped[..., :half_dim]
    second_half = shaped[..., half_dim:]
    turned = jnp.concatenate(
        [
            first_half * cosine - second_half * sine_part,
            second_half * cosine + first_half * sine_part,
        ],
        axis=-1,
    )
    return turned.reshape(key_count, KVH * HD)


def attend_block(running, query_rows, query_start, key_rows, value_rows, key_start, mask_table):
    query_count = query_rows.shape[0]
    key_count = key_rows.shape[0]
    per_group = H // KVH
    block_ids = jnp.arange(mask_table.shape[0], dtype=jnp.int32)
    query_pos = query_start + jnp.arange(query_count, dtype=jnp.int32)
    key_pos = key_start + jnp.arange(key_count, dtype=jnp.int32)
    query_onehot = (query_pos[:, None] // BLK == block_ids[None, :]).astype(jnp.float32)
    key_onehot = (key_pos[:, None] // BLK == block_ids[None, :]).astype(jnp.float32)
    linked = jnp.dot(
        jnp.dot(query_onehot, mask_table, precision=lax.Precision.HIGHEST),
        key_onehot.T,
        precision=lax.Precision.HIGHEST,
    )
    visible = (linked > 0.5) & (key_pos[None, :] <= query_pos[:, None])
    top_seen, totals, summed = running
    scores = jnp.einsum(
        "tkgd,nkd->kgtn",
        query_rows.reshape(query_count, KVH, per_group, HD),
        key_rows.reshape(key_count, KVH, HD),
        preferred_element_type=jnp.float32,
    ) / math.sqrt(HD)
    masked = jnp.where(visible[None, None], scores, neg_floor)
    new_top = jnp.maximum(top_seen, jnp.max(masked, axis=-1))
    weights = jnp.where(visible[None, None], jnp.exp(scores - new_top[..., None]), 0.0)
    factor = jnp.exp(top_seen - new_top)
    totals = totals * factor + jnp.sum(weights, axis=-1)
    summed = summed * factor[..., None] + jnp.einsum(
        "kgtn,nkd->kgtd",
        weights.astype(jnp.bfloat16),
        value_rows.reshape(key_count, KVH, HD),
        preferred_element_type=jnp.float32,
    )
    return (new_top, totals, summed)


def attend(running, query_rows, query_start, key_rows, value_rows, key_start, mask_table):
    key_count = key_rows.shape[0]
    block_width = 512
    for low_end in range(0, key_count, block_width):
        high_end = min(key_count, low_end + block_width)
        running = attend_block(
            running,
            query_rows,
            query_start,
            key_rows[low_end:high_end],
            value_rows[low_end:high_end],
            key_start + low_end,
            mask_table,
        )
    return running


def attend_packs(running, query_all, query_start, key_all, value_all, key_start, mask_tables):
    state_one = (running[0][0], running[1][0], running[2][0])
    results = [
        attend(
            state_one,
            query_all[0],
            query_start,
            key_all[0],
            value_all[0],
            key_start,
            mask_tables[0],
        )
    ]
    return (
        jnp.stack([item[0] for item in results]),
        jnp.stack([item[1] for item in results]),
        jnp.stack([item[2] for item in results]),
    )


def on_device(hidden_in, queries, kv_weight, kv_bias, norm_gain, block_mask):
    pack_count = hidden_in.shape[0]
    tokens_here = hidden_in.shape[1]
    all_rows = pack_count * tokens_here
    hidden_rows = hidden_in.reshape(all_rows, hidden_in.shape[2])
    wide_rows = hidden_rows.astype(jnp.float32)
    inv_rms = lax.rsqrt(jnp.mean(wide_rows * wide_rows, axis=-1, keepdims=True) + 1e-06)
    normed = (wide_rows * inv_rms * norm_gain).astype(jnp.bfloat16)
    projected = jnp.dot(
        normed,
        lax.all_gather(kv_weight, "fsdp", axis=0, tiled=True),
        preferred_element_type=jnp.float32,
    )
    projected = projected + kv_bias
    ctx_index = lax.axis_index("ctx")
    my_start = ctx_index * tokens_here
    positions = jnp.tile(my_start + jnp.arange(tokens_here, dtype=jnp.int32), pack_count)
    key_rows = (
        rotary(projected[:, : KVH * HD], positions)
        .astype(jnp.bfloat16)
        .reshape(pack_count, tokens_here, KVH * HD)
    )
    value_rows = (
        projected[:, KVH * HD :].astype(jnp.bfloat16).reshape(pack_count, tokens_here, KVH * HD)
    )
    mask_tables = block_mask.astype(jnp.float32)
    per_group = H // KVH
    start_state = (
        jnp.full((pack_count, KVH, per_group, tokens_here), neg_floor, jnp.float32),
        jnp.zeros((pack_count, KVH, per_group, tokens_here), jnp.float32),
        jnp.zeros((pack_count, KVH, per_group, tokens_here, HD), jnp.float32),
    )
    top_seen, totals, summed = attend_packs(
        start_state,
        queries,
        my_start,
        lax.all_gather(key_rows, "ctx", axis=1, tiled=True),
        lax.all_gather(value_rows, "ctx", axis=1, tiled=True),
        jnp.int32(0),
        mask_tables,
    )
    attended = (
        (summed / totals[..., None])
        .transpose(0, 3, 1, 2, 4)
        .reshape(pack_count, tokens_here, H * HD)
        .astype(jnp.bfloat16)
    )
    return attended


def solution(mesh):
    return jax.shard_map(
        on_device,
        mesh=mesh,
        in_specs=(
            P("fsdp", "ctx", None),
            P("fsdp", "ctx", None),
            P("fsdp", None),
            P(),
            P(),
            P("fsdp", None, None),
        ),
        out_specs=P("fsdp", "ctx", None),
        check_vma=False,
    )
```

profile of v0, /device:TPU:32, one launch (start us, length us, event | category | flops | bytes accessed | tf_op | source)
XLA Modules:
  0.0 323.5 jit_solution(10495896230145384770)
XLA Ops:
  6.5 0.7 all-gather.5.cloned.1.call-update
  7.3 0.0 all-gather.9.cloned.1.call-start
  7.3 2.1 fusion.20
  9.4 0.0 copy-start.2
  9.4 0.0 copy-start
  9.4 118.7 %all-gather.5.cloned.1.call-done = bf16[8192,1024]{1,0:T(8,128)(2,1)} async-done(((bf16[512,1024]{1,0:T(8,128)(2,1)}), bf16[8192,1024]{1,0:T(8,128)(2,1)}) %all-gather.5.cloned.1.call-update) | async-done | bytes 16777232 | tf_op jit(solution)/shard_map/all_gather | solution.py:120
  128.1 8.8 %fusion.54 = f32[128,1024]{1,0:T(8,128)S(1)} fusion(bf16[8192,1024]{1,0:T(8,128)(2,1)} %all-gather.5.cloned.1.call-done, bf16[1,128,8192]{2,1,0:T(8,128)(2,1)} %param.6, f32[8192]{0:T(1024)} %param.10, f32[128]{0:T(128)S(1)} %add_rsqrt_fusion, f32[1024]{0:T(1024)} %param.9), kind=kOutput, calls=%fused_computation.58 | convolution fusion | flops 2151809024 | bytes 19436032 | tf_op jit(solution)/shard_map/dot_general | solution.py:118
  136.9 0.7 slice.74
  137.6 0.0 all-gather.9.cloned.1.call-update
  137.6 0.2 all-gather.7.cloned.1.call-start
  137.9 0.3 multiply_cosine_fusion
  138.2 0.1 reshape.436
  138.3 0.3 subtract_convert_fusion
  138.6 0.2 pad_maximum_fusion
  138.8 0.8 copy.25
  139.5 0.0 all-gather.7.cloned.1.call-update
  139.6 0.2 fusion.73
  139.8 0.5 fusion.60
  140.3 0.2 copy.40
  140.5 0.4 fusion.59
  140.9 0.2 copy.35
  141.1 0.4 fusion.58
  141.5 0.2 copy.30
  141.7 0.4 fusion.57
  142.1 0.2 copy.24
  142.3 0.2 copy.70
  142.5 63.5 %all-gather.9.cloned.1.call-done = bf16[2048,512]{1,0:T(8,128)(2,1)} async-done(((bf16[128,512]{1,0:T(8,128)(2,1)}), bf16[2048,512]{1,0:T(8,128)(2,1)}) %all-gather.9.cloned.1.call-update) | async-done | bytes 2097168 | tf_op jit(solution)/shard_map/all_gather | solution.py:147
  206.0 1.7 fusion.101
  207.7 1.0 copy.60
  208.7 0.2 copy.69
  208.9 0.2 copy.66
  209.1 0.2 copy.63
  209.3 68.8 %all-gather.7.cloned.1.call-done = bf16[1,2048,512]{1,2,0:T(8,128)(2,1)} async-done(((bf16[1,128,512]{1,2,0:T(8,128)(2,1)}), bf16[1,2048,512]{1,2,0:T(8,128)(2,1)}) %all-gather.7.cloned.1.call-update) | async-done | bytes 2097168 | tf_op jit(solution)/shard_map/all_gather | solution.py:146
  278.1 1.7 fusion.102
  279.8 2.0 fusion.6
  281.8 2.0 fusion.3
  283.9 5.3 %fusion = (f32[4,8,128]{2,1,0:T(8,128)S(1)}, f32[4,512,128,8]{2,1,3,0:T(8,128)}) fusion(pred[128,512]{0,1:T(8,128)(4,1)S(1)} %copy.40, bf16[512,4,128,1]{0,2,3,1:T(8,128)(2,1)S(1)} %bitcast.139, bf16[128,4,8,128]{3,2,1,0:T(8,128)(2,1)S(1)} %bitcast.136), kind=kOutput, calls=%fused_computation.2 | convolution fusion | flops 543158272 | bytes 10043392 | tf_op jit(solution)/shard_map/tkgd,nkd->kgtn/dot_general | solution.py:53
  289.1 2.0 fusion.9
  291.2 5.3 %fusion.18 = f32[4,8,128]{2,1,0:T(8,128)S(1)} fusion(f32[4,512,128,8]{2,1,3,0:T(8,128)} %get-tuple-element.27, f32[4,8,128]{2,1,0:T(8,128)S(1)} %get-tuple-element.9, pred[128,512]{0,1:T(8,128)(4,1)S(1)} %copy.40), kind=kLoop, calls=%fused_computation.26 | loop fusion | flops 8384512 | bytes 8486912 | tf_op jit(solution)/shard_map/reduce_sum | solution.py:63
  296.5 6.5 %fusion.23 = f32[4,8,128,128]{2,3,1,0:T(8,128)} fusion(bf16[512,4,128,1]{0,2,3,1:T(8,128)(2,1)S(1)} %bitcast.148, f32[4,512,128,8]{2,1,3,0:T(8,128)} %get-tuple-element.27, f32[4,8,128]{2,1,0:T(8,128)S(1)} %get-tuple-element.9, pred[128,512]{0,1:T(8,128)(4,1)S(1)} %copy.40), kind=kOutput, calls=%fused_computation.33 | convolution fusion | flops 545259520 | bytes 11091968 | tf_op jit(solution)/shard_map/kgtn,nkd->kgtd/dot_general | solution.py:64
  303.0 1.8 fusion.16
  304.8 3.1 fusion.25
  307.9 1.8 fusion.14
  309.7 0.0 copy-start.1
  309.7 1.7 fusion.27
  311.4 1.8 fusion.12
  313.3 2.4 divide_convert_fusion
  315.7 1.3 copy.45
  (19 shorter events, 0.1 us)
Async XLA Ops:
  6.5 121.6 %all-gather.5.cloned.1.call-start = ((), (), s32[]{:S(2)}) async-start(), calls=%async_computation | async-start | bytes 17825792 | tf_op jit(solution)/shard_map/all_gather | solution.py:120
  7.3 198.8 %all-gather.9.cloned.1.call-start = ((), (), s32[]{:S(2)}) async-start(), calls=%async_computation.2 | async-start | bytes 2228224 | tf_op jit(solution)/shard_map/all_gather | solution.py:147
  9.4 130.2 %copy-start.2 = (s32[1,16,16]{2,1,0:T(8,128)S(1)}, s32[1,16,16]{2,1,0:T(8,128)}, u32[]{:S(2)}) copy-start(s32[1,16,16]{2,1,0:T(8,128)} %param.11) | copy-start | bytes 3076
  9.4 132.8 %copy-start = (bf16[1,128,4096]{2,1,0:T(8,128)(2,1)S(1)}, bf16[1,128,4096]{2,1,0:T(8,128)(2,1)}, u32[]{:S(2)}) copy-start(bf16[1,128,4096]{2,1,0:T(8,128)(2,1)} %param.7) | copy-start | bytes 3145732
  137.6 140.5 %all-gather.7.cloned.1.call-start = ((), (), s32[]{:S(2)}) async-start(), calls=%async_computation.1 | async-start | bytes 2228224 | tf_op jit(solution)/shard_map/all_gather | solution.py:146
  309.7 3.6 %copy-start.1 = (bf16[1,512,512]{1,2,0:T(8,128)(2,1)S(1)}, bf16[1,512,512]{1,2,0:T(8,128)(2,1)}, u32[]{:S(2)}) copy-start(bf16[1,512,512]{1,2,0:T(8,128)(2,1)} %copy.60) | copy-start | bytes 1572868
  309.7 3.6 %copy-start.3 = (f32[4,8,128,128]{2,3,1,0:T(8,128)S(1)}, f32[4,8,128,128]{2,3,1,0:T(8,128)}, u32[]{:S(2)}) copy-start(f32[4,8,128,128]{2,3,1,0:T(8,128)} %fusion.23) | copy-start | bytes 6291460
  309.7 3.6 %copy-start.4 = (f32[4,8,128,128]{2,3,1,0:T(8,128)S(1)}, f32[4,8,128,128]{2,3,1,0:T(8,128)}, u32[]{:S(2)}) copy-start(f32[4,8,128,128]{2,3,1,0:T(8,128)} %fusion.25) | copy-start | bytes 6291460
Sparse Core Ops, SparseCore 0:
  10.1 117.9 all-gather.4
  137.7 68.2 all-gather.8
  207.7 70.3 all-gather.6
where the time goes:
time: 324 us
  waiting for transfers between devices  252 us (78%)
  matrix products  35.8 us (11%)
  other arithmetic  13.6 us (4%)
  between operations  13.4 us (4%)
  local copies, waits for them, and re-layouts  8.76 us (3%)
    all_gather x1, waiting for transfers between devices, on_device(): lax.all_gather(kv_weight, 'fsdp', axis=0, tiled=True)  119 us
    all_gather x1, waiting for transfers between devices, on_device(): lax.all_gather(key_rows, 'ctx', axis=1, tiled=True)  68.8 us
    all_gather x1, waiting for transfers between devices, on_device(): lax.all_gather(value_rows, 'ctx', axis=1, tiled=True)  63.5 us
    dot_general x4, matrix products, attend_block(): jnp.einsum('kgtn,nkd->kgtd', weights.astype(jnp.bfloat16), value_rows.res...  13.7 us
    dot_general x4, matrix products, attend_block(): jnp.einsum('tkgd,nkd->kgtn', query_rows.reshape(query_count, KVH, per_gro...  11.4 us
    reduce_sum x4, other arithmetic, attend_block(): totals = totals * factor + jnp.sum(weights, axis=-1)  10.6 us
    dot_general x1, matrix products, on_device(): jnp.dot(normed, lax.all_gather(kv_weight, 'fsdp', axis=0, tiled=True), pr...  8.8 us
  transfers between devices with their start and end apart: 3, of which 3 were waited for; matrix products, arithmetic and copies ran while one was open for 3% of the time, Pallas kernels for 0%

commit v1 on v0

v1 whole, which is shorter than its diff:
```python
import math

import jax
import jax.numpy as jnp
from jax import lax
from jax.experimental import pallas as pl
from jax.experimental.pallas import tpu as pltpu
from jax.sharding import PartitionSpec as P

H = 32
KVH = 4
HD = 128
BLK = 128
D = 8192
GW = (H // KVH) * HD
LOW = -1e30
SCALE = math.log2(math.e) / math.sqrt(HD)
BF = jnp.bfloat16
F32 = jnp.float32


def x_pairs(k):
    return [(f, (f & 8) | ((((f >> 1) + k) & 3) << 1) | (f & 1)) for f in range(16)]


CORE_PAIRS = [(f, f ^ 1) for f in range(16)]
DIAG_PAIRS = [(i, i ^ (8 * 16) ^ 8) for i in range(256)]


def member_pairs(k):
    flip = ((k >> 1) << 3) | (k & 1)
    return [(c, c ^ flip) for c in range(16)]


def z_pairs(k):
    return [(c, (c & 8) | ((c + k) & 7)) for c in range(16)]


def norm_kernel(pos_ref, x_ref, gain_ref, *outs):
    xi, yhi, core = pos_ref[0], pos_ref[1], pos_ref[2]
    total = None
    for j in range(8):
        part = x_ref[:, j * 1024 : (j + 1) * 1024].astype(F32)
        part = part * part
        for i in range(8):
            piece = part[:, i * 128 : (i + 1) * 128]
            total = piece if total is None else total + piece
    inv = lax.rsqrt(jnp.sum(total, axis=-1, keepdims=True) / D + 1e-06)
    for k in range(4):
        for a in range(2):
            for b in range(2):
                src = (yhi ^ a) * 4096 + ((xi + k) & 3) * 1024 + (core ^ b) * 512
                cols = pl.ds(pl.multiple_of(src, 512), 512)
                wide = x_ref[:, cols].astype(F32)
                dst = (a * 2 + b) * 512
                outs[k][:, dst : dst + 512] = (wide * inv * gain_ref[:, cols]).astype(BF)


def norm_call(pos, hidden, gain):
    rows = hidden.shape[0]
    step = 32
    return pl.pallas_call(
        norm_kernel,
        grid_spec=pltpu.PrefetchScalarGridSpec(
            num_scalar_prefetch=1,
            grid=(rows // step,),
            in_specs=[
                pl.BlockSpec((step, D), lambda i, p: (i, 0)),
                pl.BlockSpec((1, D), lambda i, p: (0, 0)),
            ],
            out_specs=[pl.BlockSpec((step, D // 4), lambda i, p: (i, 0))] * 4,
        ),
        out_shape=[jax.ShapeDtypeStruct((rows, D // 4), BF)] * 4,
        compiler_params=pltpu.CompilerParams(vmem_limit_bytes=16 * 1024 * 1024),
        cost_estimate=pl.CostEstimate(flops=4 << 20, bytes_accessed=4 << 20, transcendentals=0),
        name="norm",
    )(pos, hidden, gain)


def kv_kernel(j_ref, own_ref, r1_ref, r2_ref, r3_ref, bias_ref, cos_ref, sin_ref, *outs):
    j = j_ref[0]

    def part(col):
        cols = pl.ds(pl.multiple_of(col, 128), 128)
        back = r1_ref[:, cols].astype(F32) + r2_ref[:, cols].astype(F32) + r3_ref[:, cols].astype(F32)
        return own_ref[:, cols] + back + bias_ref[:, cols]

    for k in range(4):
        head = j ^ k
        key = part(head * HD)
        turned = key * cos_ref[...] + pltpu.roll(key, HD // 2, 1) * sin_ref[...]
        outs[k][:, :HD] = turned.astype(BF)
        outs[k][:, HD:] = part(KVH * HD + head * HD).astype(BF)


def kv_call(j, own, r1, r2, r3, bias, cos, sin):
    vm = pl.BlockSpec(memory_space=pltpu.VMEM)
    return pl.pallas_call(
        kv_kernel,
        in_specs=[pl.BlockSpec(memory_space=pltpu.SMEM)] + [vm] * 7,
        out_specs=[vm] * 4,
        out_shape=[jax.ShapeDtypeStruct((own.shape[0], 2 * HD), BF)] * 4,
        compiler_params=pltpu.CompilerParams(vmem_limit_bytes=8 * 1024 * 1024),
        cost_estimate=pl.CostEstimate(flops=1 << 20, bytes_accessed=2 << 20, transcendentals=0),
        name="keys_values",
    )(j, own, r1, r2, r3, bias, cos, sin)


def attn_kernel(flag_ref, q_ref, *refs):
    kv_refs, out_ref, kv_all, top, acc = refs[:-4], refs[-4], refs[-3], refs[-2], refs[-1]
    qi = pl.program_id(0)
    chunks = kv_all.shape[0]
    heads = H // KVH

    @pl.when(qi == 0)
    def _():
        at = 0
        for ref in kv_refs:
            for i in range(ref.shape[0] // 256):
                kv_all[at] = ref[i * 256 : (i + 1) * 256, :]
                at += 1

    top[...] = jnp.full_like(top, LOW)
    acc[...] = jnp.zeros_like(acc)
    ones = jnp.ones((256, HD), BF)

    def update(c, valid):
        keys = kv_all[c, :, :HD]
        values = jnp.concatenate([kv_all[c, :, HD:], ones], axis=1)
        for h in range(heads):
            q = q_ref[0, :, h * HD : (h + 1) * HD]
            s = lax.dot_general(q, keys, (((1,), (1,)), ((), ())), preferred_element_type=F32)
            if valid is not None:
                s = jnp.where(valid, s, LOW)
            old = top[h]
            new = jnp.maximum(old, jnp.max(s, axis=-1, keepdims=True))
            top[h] = new
            shift = new * SCALE
            factor = jnp.exp2(old * SCALE - shift)
            p = jnp.exp2(s * SCALE - jnp.concatenate([shift, shift], axis=1))
            if valid is not None:
                p = jnp.where(valid, p, 0.0)
            add = jnp.dot(p.astype(BF), values, preferred_element_type=F32)
            acc[h] = acc[h] * jnp.concatenate([factor, factor], axis=1) + add

    def step(c, carry):
        f0 = flag_ref[qi, c * 2]
        f1 = flag_ref[qi, c * 2 + 1]
        plain = (f0 == 1) & (f1 == 1)

        @pl.when(plain)
        def _():
            update(c, None)

        @pl.when(jnp.logical_not(plain) & ((f0 + f1) > 0))
        def _():
            row = lax.broadcasted_iota(jnp.int32, (BLK, BLK), 0)
            col = lax.broadcasted_iota(jnp.int32, (BLK, BLK), 1)
            reach0 = jnp.where(f0 == 2, row, jnp.where(f0 == 1, BLK, -1))
            reach1 = jnp.where(f1 == 2, row, jnp.where(f1 == 1, BLK, -1))
            reach = jnp.concatenate([reach0, reach1], axis=1)
            update(c, jnp.concatenate([col, col], axis=1) <= reach)

        return carry

    lax.fori_loop(0, chunks, step, 0)
    for h in range(heads):
        out_ref[0, :, h * HD : (h + 1) * HD] = (acc[h, :, :HD] / acc[h, :, HD:]).astype(BF)


def attn_call(flags, q4, parts):
    chunks = sum(p.shape[0] for p in parts) // 256
    return pl.pallas_call(
        attn_kernel,
        grid_spec=pltpu.PrefetchScalarGridSpec(
            num_scalar_prefetch=1,
            grid=(4,),
            in_specs=[pl.BlockSpec((1, BLK, GW), lambda i, f: (i, 0, 0))]
            + [pl.BlockSpec(p.shape, lambda i, f: (0, 0)) for p in parts],
            out_specs=pl.BlockSpec((1, BLK, GW), lambda i, f: (i, 0, 0)),
            scratch_shapes=[
                pltpu.VMEM((chunks, 256, 2 * HD), BF),
                pltpu.VMEM((H // KVH, BLK, HD), F32),
                pltpu.VMEM((H // KVH, BLK, 2 * HD), F32),
            ],
        ),
        out_shape=jax.ShapeDtypeStruct((4, BLK, GW), BF),
        compiler_params=pltpu.CompilerParams(vmem_limit_bytes=24 * 1024 * 1024),
        cost_estimate=pl.CostEstimate(flops=6 << 30, bytes_accessed=4 << 20, transcendentals=8 << 20),
        name="attend",
    )(flags, q4, *parts)


def place_kernel(j_ref, *refs):
    out_ref = refs[-1]
    for k in range(4):
        cols = pl.ds(pl.multiple_of((j_ref[0] ^ k) * GW, GW), GW)
        out_ref[:, cols] = refs[k][...]


def place_call(j, parts):
    vm = pl.BlockSpec(memory_space=pltpu.VMEM)
    return pl.pallas_call(
        place_kernel,
        in_specs=[pl.BlockSpec(memory_space=pltpu.SMEM)] + [vm] * 4,
        out_specs=vm,
        out_shape=jax.ShapeDtypeStruct((BLK, H * HD), BF),
        compiler_params=pltpu.CompilerParams(vmem_limit_bytes=8 * 1024 * 1024),
        name="place",
    )(j, *parts)


def rotary_tables(start, count):
    half_dim = HD // 2
    positions = start + jnp.arange(count, dtype=jnp.int32)
    inv_freq = jnp.exp(jnp.arange(half_dim, dtype=F32) * (-2.0 * math.log(1000000.0) / HD))
    angle = positions.astype(F32)[:, None] * inv_freq[None, :]
    cosine, sine = jnp.cos(angle), jnp.sin(angle)
    return jnp.concatenate([cosine, cosine], 1), jnp.concatenate([-sine, sine], 1)


def on_device(hidden_in, queries, kv_weight, kv_bias, norm_gain, block_mask):
    f = lax.axis_index("fsdp")
    c = lax.axis_index("ctx")
    core, xi, yhi = f & 1, (f >> 1) & 3, f >> 3
    z, ylo = c & 7, c >> 3
    j = ylo * 2 + (z & 1)
    zq = z >> 1
    hidden = hidden_in.reshape(BLK, D)
    q = queries.reshape(BLK, H * HD)
    j1 = jnp.reshape(j, (1,))

    w_core = lax.ppermute(kv_weight, "fsdp", CORE_PAIRS)
    w_y = lax.ppermute(kv_weight, ("ctx", "fsdp"), DIAG_PAIRS)

    normed = norm_call(jnp.stack([xi, yhi, core]), hidden, norm_gain.reshape(1, D))
    n1 = lax.ppermute(normed[1], "fsdp", x_pairs(1))
    n3 = lax.ppermute(normed[3], "fsdp", x_pairs(3))
    n2 = lax.ppermute(normed[2], "fsdp", x_pairs(2))
    w_yc = lax.ppermute(w_y, "fsdp", CORE_PAIRS)

    q_parts = []
    for k in range(4):
        piece = lax.dynamic_slice(q, (0, (j ^ k) * GW), (BLK, GW))
        q_parts.append(piece if k == 0 else lax.ppermute(piece, "ctx", member_pairs(k)))
    q4 = jnp.stack(q_parts)

    weight = jnp.concatenate([kv_weight, w_core, w_y, w_yc], axis=0)
    own = jnp.dot(normed[0], weight, preferred_element_type=F32)
    back = []
    for got, k in ((n1, 3), (n3, 1), (n2, 2)):
        product = jnp.dot(got, weight, preferred_element_type=F32).astype(BF)
        back.append(lax.ppermute(product, "fsdp", x_pairs(k)))

    cos, sin = rotary_tables(c * BLK, BLK)
    kvs = kv_call(j1, own, back[0], back[1], back[2], kv_bias.reshape(1, -1), cos, sin)
    group = jnp.concatenate([kvs[0]] + [lax.ppermute(kvs[k], "ctx", member_pairs(k)) for k in (1, 2, 3)], axis=0)

    up = lax.ppermute(group, "ctx", z_pairs(2))
    down = lax.ppermute(group, "ctx", z_pairs(-2))
    far0 = lax.ppermute(up[:256], "ctx", z_pairs(2))
    far1 = lax.ppermute(down[256:], "ctx", z_pairs(-2))

    members = j ^ jnp.arange(4, dtype=jnp.int32)
    block_of = lambda at: (members >> 1) * 8 + 2 * at + (members & 1)
    q_ids = block_of(zq)
    u_ids = jnp.concatenate([q_ids, block_of((zq + 3) & 3), block_of((zq + 1) & 3), block_of((zq + 2) & 3)])
    table = block_mask.reshape(16, 16)
    seen = jnp.take(jnp.take(table, q_ids, axis=0), u_ids, axis=1) == 1
    order = q_ids[:, None] - u_ids[None, :]
    flags = jnp.where(order == 0, 2, jnp.where(order > 0, 1, 0)) * seen.astype(jnp.int32)

    out4 = attn_call(flags.astype(jnp.int32), q4, [group, up, down, far0, far1])
    parts = [out4[0]] + [lax.ppermute(out4[k], "ctx", member_pairs(k)) for k in (1, 2, 3)]
    return place_call(j1, parts).reshape(1, BLK, H * HD)


def solution(mesh):
    return jax.shard_map(
        on_device,
        mesh=mesh,
        in_specs=(
            P("fsdp", "ctx", None),
            P("fsdp", "ctx", None),
            P("fsdp", None),
            P(),
            P(),
            P("fsdp", None, None),
        ),
        out_specs=P("fsdp", "ctx", None),
        check_vma=False,
    )
```

time: 324 us -> 117 us (0.36)
  the two profiles are of different devices: /device:TPU:32 before, /device:TPU:210 now
where the time goes in v1:
time: 117 us
  waiting for transfers between devices  54.1 us (46%)
  starting transfers between devices  26.4 us (23%)
  Pallas kernels  21.1 us (18%)
  local copies, waits for them, and re-layouts  8.59 us (7%)
  matrix products  6 us (5%)
    pallas_call x1, Pallas kernels, attn_call(): pl.pallas_call(attn_kernel, grid_spec=pltpu.PrefetchScalarGridSpec(num_sc...  18 us
    ppermute x1, waiting for transfers between devices, on_device(): w_y = lax.ppermute(kv_weight, ('ctx', 'fsdp'), DIAG_PAIRS)  15.3 us
    ppermute x3, waiting for transfers between devices, on_device(): lax.ppermute(out4[k], 'ctx', member_pairs(k))  10.5 us
    ppermute x3, waiting for transfers between devices, on_device(): lax.ppermute(kvs[k], 'ctx', member_pairs(k))  7.36 us
    ppermute x3, waiting for transfers between devices, on_device(): back.append(lax.ppermute(product, 'fsdp', x_pairs(k)))  6.29 us
    ppermute x1, waiting for transfers between devices, on_device(): up = lax.ppermute(group, 'ctx', z_pairs(2))  5.66 us
    ppermute x3, starting transfers between devices, on_device(): lax.ppermute(out4[k], 'ctx', member_pairs(k))  5.37 us
    dot_general x3, matrix products, on_device(): product = jnp.dot(got, weight, preferred_element_type=F32).astype(BF)  5.27 us
  transfers between devices with their start and end apart: 22, of which 12 were waited for; matrix products, arithmetic and copies ran while one was open for 11% of the time, Pallas kernels for 2%

profile of v1, /device:TPU:210, one launch (start us, length us, event | category | flops | bytes accessed | tf_op | source)
XLA Modules:
  0.0 117.4 jit_solution(2032772379936603964)
XLA Ops:
  0.0 0.4 collective-permute-start.4
  0.5 1.6 %copy-done.1 = bf16[1,128,8192]{2,1,0:T(8,128)(2,1)S(1)} copy-done((bf16[1,128,8192]{2,1,0:T(8,128)(2,1)S(1)}, bf16[1,128,8192]{2,1,0:T(8,128)(2,1)}, u32[]{:S(2)}) %copy-start.1) | copy-done | bytes 2097176
  2.1 0.8 copy-done.2
  2.9 1.7 %norm.1 = (bf16[128,2048]{1,0:T(8,128)(2,1)S(1)}, bf16[128,2048]{1,0:T(8,128)(2,1)S(1)}, bf16[128,2048]{1,0:T(8,128)(2,1)S(1)}, bf16[128,2048]{1,0:T(8,128)(2,1)S(1)}) custom-call(s32[3]{0:T(128)S(1)} %pad_add_fusion.1.pos_ref, bf16[128,8192]{1,0:T(8,128)(2,1)S(1)} %bitcast.48, f32[1,8192]{1,0:T(1,128)S(1)} %bitcast.49), custom_call_target="tpu_custom_call" | custom-call | flops 4194304 | bytes 4194304 | tf_op jit(solution)/shard_map/norm/pallas_call | solution.py:62
  4.6 2.2 %collective-permute-start.10 = (bf16[128,2048]{1,0:T(8,128)(2,1)S(1)}, bf16[128,2048]{1,0:T(8,128)(2,1)}, u32[]{:S(2)}, u32[]{:S(2)}) collective-permute-start(bf16[128,2048]{1,0:T(8,128)(2,1)S(1)} %get-tuple-element.16), channel_id=1, source_target_pairs={{0,4},{1,5},{2,6},{3,7},{4,0},{5,1},{6,2},{7,3},{8,12},{9,13},{10,... | collective-permute-start | bytes 1572872 | tf_op jit(solution)/shard_map/ppermute | solution.py:239
  6.9 2.0 %collective-permute-start.8 = (bf16[128,2048]{1,0:T(8,128)(2,1)S(1)}, bf16[128,2048]{1,0:T(8,128)(2,1)}, u32[]{:S(2)}, u32[]{:S(2)}) collective-permute-start(bf16[128,2048]{1,0:T(8,128)(2,1)S(1)} %get-tuple-element.15), channel_id=1, source_target_pairs={{0,6},{1,7},{2,0},{3,1},{4,2},{5,3},{6,4},{7,5},{8,14},{9,15},{10,... | collective-permute-start | bytes 1572872 | tf_op jit(solution)/shard_map/ppermute | solution.py:238
  8.9 0.6 gather_fusion
  9.6 0.3 fusion
  9.9 15.3 %collective-permute-done.4 = bf16[512,1024]{1,0:T(8,128)(2,1)} collective-permute-done((bf16[512,1024]{1,0:T(8,128)(2,1)}, bf16[512,1024]{1,0:T(8,128)(2,1)}, u32[]{:S(2)}, u32[]{:S(2)}) %collective-permute-start.4) | collective-permute-done | bytes 1048608 | tf_op jit(solution)/shard_map/ppermute | solution.py:234
  25.2 0.1 pad_maximum_fusion.1
  25.3 2.1 %constant_dynamic-slice_fusion = (bf16[1,128,1024]{2,1,0:T(8,128)(2,1)S(1)}, bf16[128,1024]{1,0:T(8,128)(2,1)}, bf16[128,1024]{1,0:T(8,128)(2,1)}, bf16[128,1024]{1,0:T(8,128)(2,1)}) fusion(bf16[1,128,4096]{2,1,0:T(8,128)(2,1)} %param.7, s32[]{:T(128)S(6)} %select_n.68, s32[]{:T(128)S(6)} %select_n.69, s32[]{:T(128)S(6)} %select_n.71, s32[]{:T(128)S(6)} %select_n.70), kind=kLoop, calls=%fused_computation.40 | loop fusion | bytes 2097168 | tf_op jit(solution)/shard_map/dynamic_slice | solution.py:244
  27.6 1.1 collective-permute-start
  28.7 1.3 %constant_dynamic-update-slice_fusion.2 = bf16[2048,1024]{1,0:T(8,128)(2,1)S(1)} fusion(bf16[2048,1024]{1,0:T(8,128)(2,1)S(1)} %constant_dynamic-update-slice_fusion.3, bf16[512,1024]{1,0:T(8,128)(2,1)} %collective-permute-done.3), kind=kLoop, calls=%fused_computation.20 | loop fusion | bytes 2097152
  30.0 1.3 %constant_dynamic-update-slice_fusion.1 = bf16[2048,1024]{1,0:T(8,128)(2,1)S(1)} fusion(bf16[2048,1024]{1,0:T(8,128)(2,1)S(1)} %constant_dynamic-update-slice_fusion.2, bf16[512,1024]{1,0:T(8,128)(2,1)} %collective-permute-done.4), kind=kLoop, calls=%fused_computation.19 | loop fusion | bytes 2097152
  31.3 2.6 %collective-permute-start.1 = (bf16[128,1024]{1,0:T(8,128)(2,1)}, bf16[128,1024]{1,0:T(8,128)(2,1)S(1)}, u32[]{:S(2)}, u32[]{:S(2)}) collective-permute-start(bf16[128,1024]{1,0:T(8,128)(2,1)} %get-tuple-element.32), channel_id=1, source_target_pairs={{0,128},{16,144},{32,160},{48,176},{64,192},{80,208},{96,224},{112... | collective-permute-start | bytes 786440 | tf_op jit(solution)/shard_map/ppermute | solution.py:245
  34.0 1.8 %convolution_convert_fusion = bf16[128,1024]{1,0:T(8,128)(2,1)S(1)} fusion(bf16[128,2048]{1,0:T(8,128)(2,1)} %collective-permute-done.10, bf16[2048,1024]{1,0:T(8,128)(2,1)S(1)} %constant_dynamic-update-slice_fusion), kind=kOutput, calls=%fused_computation.2 | convolution fusion | flops 537001984 | bytes 4980736 | tf_op jit(solution)/shard_map/dot_general | solution.py:252
  35.7 2.2 %collective-permute-start.11 = (bf16[128,1024]{1,0:T(8,128)(2,1)S(1)}, bf16[128,1024]{1,0:T(8,128)(2,1)S(1)}, u32[]{:S(2)}, u32[]{:S(2)}) collective-permute-start(bf16[128,1024]{1,0:T(8,128)(2,1)S(1)} %convolution_convert_fusion), channel_id=1, source_target_pairs={{0,4},{1,5},{2,6},{3,7},{4,0},{5,1},{6,2},{7,3},{8,12},{9,13},{10,... | collective-permute-start | bytes 786440 | tf_op jit(solution)/shard_map/ppermute | solution.py:253
  38.0 1.8 %convolution_convert_fusion.2 = bf16[128,1024]{1,0:T(8,128)(2,1)S(1)} fusion(bf16[128,2048]{1,0:T(8,128)(2,1)} %collective-permute-done.6, bf16[2048,1024]{1,0:T(8,128)(2,1)S(1)} %constant_dynamic-update-slice_fusion), kind=kOutput, calls=%fused_computation.4 | convolution fusion | flops 537001984 | bytes 4980736 | tf_op jit(solution)/shard_map/dot_general | solution.py:252
  39.7 1.5 %collective-permute-start.7 = (bf16[128,1024]{1,0:T(8,128)(2,1)S(1)}, bf16[128,1024]{1,0:T(8,128)(2,1)S(1)}, u32[]{:S(2)}, u32[]{:S(2)}) collective-permute-start(bf16[128,1024]{1,0:T(8,128)(2,1)S(1)} %convolution_convert_fusion.2), channel_id=1, source_target_pairs={{0,6},{1,7},{2,0},{3,1},{4,2},{5,3},{6,4},{7,5},{8,14},{9,15},{10,... | collective-permute-start | bytes 786440 | tf_op jit(solution)/shard_map/ppermute | solution.py:253
  41.2 1.8 %convolution_convert_fusion.1 = bf16[128,1024]{1,0:T(8,128)(2,1)S(1)} fusion(bf16[128,2048]{1,0:T(8,128)(2,1)} %collective-permute-done.8, bf16[2048,1024]{1,0:T(8,128)(2,1)S(1)} %constant_dynamic-update-slice_fusion), kind=kOutput, calls=%fused_computation.3 | convolution fusion | flops 537001984 | bytes 4980736 | tf_op jit(solution)/shard_map/dot_general | solution.py:252
  43.0 0.7 collective-permute-start.9
  43.7 0.7 fusion.5.own_ref
  44.4 2.1 %collective-permute-done.11.r3_ref = bf16[128,1024]{1,0:T(8,128)(2,1)S(1)} collective-permute-done((bf16[128,1024]{1,0:T(8,128)(2,1)S(1)}, bf16[128,1024]{1,0:T(8,128)(2,1)S(1)}, u32[]{:S(2)}, u32[]{:S(2)}) %collective-permute-start.11) | collective-permute-done | bytes 262176 | tf_op jit(solution)/shard_map/ppermute | solution.py:253
  46.6 0.4 collective-permute-start.2
  47.0 4.1 %collective-permute-done.7.r1_ref = bf16[128,1024]{1,0:T(8,128)(2,1)S(1)} collective-permute-done((bf16[128,1024]{1,0:T(8,128)(2,1)S(1)}, bf16[128,1024]{1,0:T(8,128)(2,1)S(1)}, u32[]{:S(2)}, u32[]{:S(2)}) %collective-permute-start.7) | collective-permute-done | bytes 262176 | tf_op jit(solution)/shard_map/ppermute | solution.py:253
  51.1 0.4 keys_values.1
  51.5 1.3 %collective-permute-start.12 = (bf16[128,256]{1,0:T(8,128)(2,1)S(1)}, bf16[128,256]{1,0:T(8,128)(2,1)S(1)}, u32[]{:S(2)}, u32[]{:S(2)}) collective-permute-start(bf16[128,256]{1,0:T(8,128)(2,1)S(1)} %get-tuple-element.18), channel_id=1, source_target_pairs={{0,16},{16,0},{32,48},{48,32},{64,80},{80,64},{96,112},{112,96},{1... | collective-permute-start | bytes 196616 | tf_op jit(solution)/shard_map/ppermute | solution.py:257
  52.8 0.3 collective-permute-start.13
  53.1 3.0 %collective-permute-done.12 = bf16[128,256]{1,0:T(8,128)(2,1)S(1)} collective-permute-done((bf16[128,256]{1,0:T(8,128)(2,1)S(1)}, bf16[128,256]{1,0:T(8,128)(2,1)S(1)}, u32[]{:S(2)}, u32[]{:S(2)}) %collective-permute-start.12) | collective-permute-done | bytes 65568 | tf_op jit(solution)/shard_map/ppermute | solution.py:257
  56.0 0.7 collective-permute-start.14
  56.8 0.3 collective-permute-done.13
  57.0 4.1 %collective-permute-done.14 = bf16[128,256]{1,0:T(8,128)(2,1)S(1)} collective-permute-done((bf16[128,256]{1,0:T(8,128)(2,1)S(1)}, bf16[128,256]{1,0:T(8,128)(2,1)S(1)}, u32[]{:S(2)}, u32[]{:S(2)}) %collective-permute-start.14) | collective-permute-done | bytes 65568 | tf_op jit(solution)/shard_map/ppermute | solution.py:257
  61.2 2.9 %collective-permute-start.16 = (bf16[512,256]{1,0:T(8,128)(2,1)S(1)}, bf16[512,256]{1,0:T(8,128)(2,1)S(1)}, u32[]{:S(2)}, u32[]{:S(2)}) collective-permute-start(bf16[512,256]{1,0:T(8,128)(2,1)S(1)} %constant_dynamic-update-slice_fusion.4.refs_0_), channel_id=1, source_target_pairs={{0,96},{16,112},{32,0},{48,16},{64,32},{80,48},{96,64},{112,80},{1... | collective-permute-start | bytes 786440 | tf_op jit(solution)/shard_map/ppermute | solution.py:260
  64.2 0.1 copy.7
  64.3 0.6 gather_fusion.1
  65.0 5.7 %collective-permute-done.15.refs_1_ = bf16[512,256]{1,0:T(8,128)(2,1)S(1)} collective-permute-done((bf16[512,256]{1,0:T(8,128)(2,1)S(1)}, bf16[512,256]{1,0:T(8,128)(2,1)S(1)}, u32[]{:S(2)}, u32[]{:S(2)}) %collective-permute-start.15) | collective-permute-done | bytes 262176 | tf_op jit(solution)/shard_map/ppermute | solution.py:259
  70.7 1.2 %collective-permute-start.17 = (bf16[256,256]{1,0:T(8,128)(2,1)S(1)}, bf16[256,256]{1,0:T(8,128)(2,1)S(1)}, u32[]{:S(2)}, u32[]{:S(2)}) collective-permute-start(bf16[256,256]{1,0:T(8,128)(2,1)S(1)} %slice.28), channel_id=1, source_target_pairs={{0,32},{16,48},{32,64},{48,80},{64,96},{80,112},{96,0},{112,16},{1... | collective-permute-start | bytes 393224 | tf_op jit(solution)/shard_map/ppermute | solution.py:261
  71.8 3.1 %collective-permute-done.16.refs_2_ = bf16[512,256]{1,0:T(8,128)(2,1)S(1)} collective-permute-done((bf16[512,256]{1,0:T(8,128)(2,1)S(1)}, bf16[512,256]{1,0:T(8,128)(2,1)S(1)}, u32[]{:S(2)}, u32[]{:S(2)}) %collective-permute-start.16) | collective-permute-done | bytes 262176 | tf_op jit(solution)/shard_map/ppermute | solution.py:260
  74.9 1.4 %collective-permute-start.18 = (bf16[256,256]{1,0:T(8,128)(2,1)S(1)}, bf16[256,256]{1,0:T(8,128)(2,1)S(1)}, u32[]{:S(2)}, u32[]{:S(2)}) collective-permute-start(bf16[256,256]{1,0:T(8,128)(2,1)S(1)} %slice.29), channel_id=1, source_target_pairs={{0,96},{16,112},{32,0},{48,16},{64,32},{80,48},{96,64},{112,80},{1... | collective-permute-start | bytes 393224 | tf_op jit(solution)/shard_map/ppermute | solution.py:262
  76.4 0.1 pad_maximum_fusion.q_ref
  76.5 3.5 %collective-permute-done.17.refs_3_ = bf16[256,256]{1,0:T(8,128)(2,1)S(1)} collective-permute-done((bf16[256,256]{1,0:T(8,128)(2,1)S(1)}, bf16[256,256]{1,0:T(8,128)(2,1)S(1)}, u32[]{:S(2)}, u32[]{:S(2)}) %collective-permute-start.17) | collective-permute-done | bytes 131104 | tf_op jit(solution)/shard_map/ppermute | solution.py:261
  80.0 2.5 %collective-permute-done.18.refs_4_ = bf16[256,256]{1,0:T(8,128)(2,1)S(1)} collective-permute-done((bf16[256,256]{1,0:T(8,128)(2,1)S(1)}, bf16[256,256]{1,0:T(8,128)(2,1)S(1)}, u32[]{:S(2)}, u32[]{:S(2)}) %collective-permute-start.18) | collective-permute-done | bytes 131104 | tf_op jit(solution)/shard_map/ppermute | solution.py:262
  82.5 18.0 %attend.1 = bf16[4,128,1024]{2,1,0:T(8,128)(2,1)S(1)} custom-call(s32[4,16]{1,0:T(4,128)S(1)} %select_select_fusion.flag_ref, bf16[4,128,1024]{2,1,0:T(8,128)(2,1)S(1)} %pad_maximum_fusion.q_ref, bf16[512,256]{1,0:T(8,128)(2,1)S(1)} %constant_dynamic-update-slice_fusion.4.refs_0_, bf16[512,256]{1,0:T(8,128)(2,1)S(1)} %collective-permute-done.15.refs_1_, ...), custom_call_target="tpu_custom_call" | custom-call | flops 6442450944 | bytes 4194304 | tf_op jit(solution)/shard_map/attend/pallas_call | solution.py:173
  100.5 3.8 %collective-permute-start.19 = (bf16[128,1024]{1,0:T(8,128)(2,1)S(1)}, bf16[128,1024]{1,0:T(8,128)(2,1)S(1)}, u32[]{:S(2)}, u32[]{:S(2)}) collective-permute-start(bf16[128,1024]{1,0:T(8,128)(2,1)S(1)} %get-tuple-element.27), channel_id=1, source_target_pairs={{0,16},{16,0},{32,48},{48,32},{64,80},{80,64},{96,112},{112,96},{1... | collective-permute-start | bytes 786440 | tf_op jit(solution)/shard_map/ppermute | solution.py:274
  104.3 1.6 %collective-permute-start.21 = (bf16[128,1024]{1,0:T(8,128)(2,1)S(1)}, bf16[128,1024]{1,0:T(8,128)(2,1)S(1)}, u32[]{:S(2)}, u32[]{:S(2)}) collective-permute-start(bf16[128,1024]{1,0:T(8,128)(2,1)S(1)} %get-tuple-element.25), channel_id=1, source_target_pairs={{0,144},{16,128},{32,176},{48,160},{64,208},{80,192},{96,240},{112... | collective-permute-start | bytes 786440 | tf_op jit(solution)/shard_map/ppermute | solution.py:274
  105.9 5.7 %collective-permute-done.19.refs_1_ = bf16[128,1024]{1,0:T(8,128)(2,1)S(1)} collective-permute-done((bf16[128,1024]{1,0:T(8,128)(2,1)S(1)}, bf16[128,1024]{1,0:T(8,128)(2,1)S(1)}, u32[]{:S(2)}, u32[]{:S(2)}) %collective-permute-start.19) | collective-permute-done | bytes 262176 | tf_op jit(solution)/shard_map/ppermute | solution.py:274
  111.6 4.8 %collective-permute-done.20.refs_2_ = bf16[128,1024]{1,0:T(8,128)(2,1)S(1)} collective-permute-done((bf16[128,1024]{1,0:T(8,128)(2,1)S(1)}, bf16[128,1024]{1,0:T(8,128)(2,1)S(1)}, u32[]{:S(2)}, u32[]{:S(2)}) %collective-permute-start.20) | collective-permute-done | bytes 262176 | tf_op jit(solution)/shard_map/ppermute | solution.py:274
  116.4 1.0 place.1
  (47 shorter events, 0.9 us)
Async XLA Ops:
  0.0 8.9 %copy-start = (s32[1,16,16]{2,1,0:T(8,128)S(1)}, s32[1,16,16]{2,1,0:T(8,128)}, u32[]{:S(2)}) copy-start(s32[1,16,16]{2,1,0:T(8,128)} %param.11) | copy-start | bytes 3076
  0.0 25.2 %collective-permute-start.4 = (bf16[512,1024]{1,0:T(8,128)(2,1)}, bf16[512,1024]{1,0:T(8,128)(2,1)}, u32[]{:S(2)}, u32[]{:S(2)}) collective-permute-start(bf16[512,1024]{1,0:T(8,128)(2,1)} %param.8), channel_id=1, source_target_pairs={{0,136},{1,137},{2,138},{3,139},{4,140},{5,141},{6,142},{7,143},{8... | collective-permute-start | bytes 3145736 | tf_op jit(solution)/shard_map/ppermute | solution.py:234
  0.5 27.2 %collective-permute-start.3 = (bf16[512,1024]{1,0:T(8,128)(2,1)}, bf16[512,1024]{1,0:T(8,128)(2,1)}, u32[]{:S(2)}, u32[]{:S(2)}) collective-permute-start(bf16[512,1024]{1,0:T(8,128)(2,1)} %param.8), channel_id=1, source_target_pairs={{0,1},{1,0},{2,3},{3,2},{4,5},{5,4},{6,7},{7,6},{8,9},{9,8},{10,11... | collective-permute-start | bytes 3145736 | tf_op jit(solution)/shard_map/ppermute | solution.py:233
  0.5 1.6 %copy-start.1 = (bf16[1,128,8192]{2,1,0:T(8,128)(2,1)S(1)}, bf16[1,128,8192]{2,1,0:T(8,128)(2,1)}, u32[]{:S(2)}) copy-start(bf16[1,128,8192]{2,1,0:T(8,128)(2,1)} %param.6) | copy-start | bytes 6291460
  2.1 0.8 copy-start.2
  2.9 24.6 %copy-start.4 = (bf16[512,1024]{1,0:T(8,128)(2,1)S(1)}, bf16[512,1024]{1,0:T(8,128)(2,1)}, u32[]{:S(2)}) copy-start(bf16[512,1024]{1,0:T(8,128)(2,1)} %param.8) | copy-start | bytes 3145732
  4.6 29.3 %collective-permute-start.10 = (bf16[128,2048]{1,0:T(8,128)(2,1)S(1)}, bf16[128,2048]{1,0:T(8,128)(2,1)}, u32[]{:S(2)}, u32[]{:S(2)}) collective-permute-start(bf16[128,2048]{1,0:T(8,128)(2,1)S(1)} %get-tuple-element.16), channel_id=1, source_target_pairs={{0,4},{1,5},{2,6},{3,7},{4,0},{5,1},{6,2},{7,3},{8,12},{9,13},{10,... | collective-permute-start | bytes 1572872 | tf_op jit(solution)/shard_map/ppermute | solution.py:239
  6.9 31.1 %collective-permute-start.6 = (bf16[128,2048]{1,0:T(8,128)(2,1)S(1)}, bf16[128,2048]{1,0:T(8,128)(2,1)}, u32[]{:S(2)}, u32[]{:S(2)}) collective-permute-start(bf16[128,2048]{1,0:T(8,128)(2,1)S(1)} %get-tuple-element.14), channel_id=1, source_target_pairs={{0,2},{1,3},{2,4},{3,5},{4,6},{5,7},{6,0},{7,1},{8,10},{9,11},{10,... | collective-permute-start | bytes 1572872 | tf_op jit(solution)/shard_map/ppermute | solution.py:237
  6.9 34.4 %collective-permute-start.8 = (bf16[128,2048]{1,0:T(8,128)(2,1)S(1)}, bf16[128,2048]{1,0:T(8,128)(2,1)}, u32[]{:S(2)}, u32[]{:S(2)}) collective-permute-start(bf16[128,2048]{1,0:T(8,128)(2,1)S(1)} %get-tuple-element.15), channel_id=1, source_target_pairs={{0,6},{1,7},{2,0},{3,1},{4,2},{5,3},{6,4},{7,5},{8,14},{9,15},{10,... | collective-permute-start | bytes 1572872 | tf_op jit(solution)/shard_map/ppermute | solution.py:238
  25.2 6.1 %collective-permute-start.5 = (bf16[512,1024]{1,0:T(8,128)(2,1)}, bf16[512,1024]{1,0:T(8,128)(2,1)S(1)}, u32[]{:S(2)}, u32[]{:S(2)}) collective-permute-start(bf16[512,1024]{1,0:T(8,128)(2,1)} %collective-permute-done.4), channel_id=1, source_target_pairs={{0,1},{1,0},{2,3},{3,2},{4,5},{5,4},{6,7},{7,6},{8,9},{9,8},{10,11... | collective-permute-start | bytes 3145736 | tf_op jit(solution)/shard_map/ppermute | solution.py:240
  27.6 48.8 %collective-permute-start = (bf16[128,1024]{1,0:T(8,128)(2,1)}, bf16[128,1024]{1,0:T(8,128)(2,1)S(1)}, u32[]{:S(2)}, u32[]{:S(2)}) collective-permute-start(bf16[128,1024]{1,0:T(8,128)(2,1)} %get-tuple-element.30), channel_id=1, source_target_pairs={{0,16},{16,0},{32,48},{48,32},{64,80},{80,64},{96,112},{112,96},{1... | collective-permute-start | bytes 786440 | tf_op jit(solution)/shard_map/ppermute | solution.py:245
  31.3 45.1 %collective-permute-start.1 = (bf16[128,1024]{1,0:T(8,128)(2,1)}, bf16[128,1024]{1,0:T(8,128)(2,1)S(1)}, u32[]{:S(2)}, u32[]{:S(2)}) collective-permute-start(bf16[128,1024]{1,0:T(8,128)(2,1)} %get-tuple-element.32), channel_id=1, source_target_pairs={{0,128},{16,144},{32,160},{48,176},{64,192},{80,208},{96,224},{112... | collective-permute-start | bytes 786440 | tf_op jit(solution)/shard_map/ppermute | solution.py:245
  35.7 10.8 %collective-permute-start.11 = (bf16[128,1024]{1,0:T(8,128)(2,1)S(1)}, bf16[128,1024]{1,0:T(8,128)(2,1)S(1)}, u32[]{:S(2)}, u32[]{:S(2)}) collective-permute-start(bf16[128,1024]{1,0:T(8,128)(2,1)S(1)} %convolution_convert_fusion), channel_id=1, source_target_pairs={{0,4},{1,5},{2,6},{3,7},{4,0},{5,1},{6,2},{7,3},{8,12},{9,13},{10,... | collective-permute-start | bytes 786440 | tf_op jit(solution)/shard_map/ppermute | solution.py:253
  39.7 11.4 %copy-start.3 = (f32[1024]{0:T(1024)S(1)}, f32[1024]{0:T(1024)}, u32[]{:S(2)}) copy-start(f32[1024]{0:T(1024)} %param.9) | copy-start | bytes 12292
  39.7 11.4 %collective-permute-start.7 = (bf16[128,1024]{1,0:T(8,128)(2,1)S(1)}, bf16[128,1024]{1,0:T(8,128)(2,1)S(1)}, u32[]{:S(2)}, u32[]{:S(2)}) collective-permute-start(bf16[128,1024]{1,0:T(8,128)(2,1)S(1)} %convolution_convert_fusion.2), channel_id=1, source_target_pairs={{0,6},{1,7},{2,0},{3,1},{4,2},{5,3},{6,4},{7,5},{8,14},{9,15},{10,... | collective-permute-start | bytes 786440 | tf_op jit(solution)/shard_map/ppermute | solution.py:253
  43.0 8.1 %collective-permute-start.9 = (bf16[128,1024]{1,0:T(8,128)(2,1)S(1)}, bf16[128,1024]{1,0:T(8,128)(2,1)S(1)}, u32[]{:S(2)}, u32[]{:S(2)}) collective-permute-start(bf16[128,1024]{1,0:T(8,128)(2,1)S(1)} %convolution_convert_fusion.1), channel_id=1, source_target_pairs={{0,2},{1,3},{2,4},{3,5},{4,6},{5,7},{6,0},{7,1},{8,10},{9,11},{10,... | collective-permute-start | bytes 786440 | tf_op jit(solution)/shard_map/ppermute | solution.py:253
  46.6 29.8 %collective-permute-start.2 = (bf16[128,1024]{1,0:T(8,128)(2,1)}, bf16[128,1024]{1,0:T(8,128)(2,1)S(1)}, u32[]{:S(2)}, u32[]{:S(2)}) collective-permute-start(bf16[128,1024]{1,0:T(8,128)(2,1)} %get-tuple-element.31), channel_id=1, source_target_pairs={{0,144},{16,128},{32,176},{48,160},{64,208},{80,192},{96,240},{112... | collective-permute-start | bytes 786440 | tf_op jit(solution)/shard_map/ppermute | solution.py:245
  51.5 4.5 %collective-permute-start.12 = (bf16[128,256]{1,0:T(8,128)(2,1)S(1)}, bf16[128,256]{1,0:T(8,128)(2,1)S(1)}, u32[]{:S(2)}, u32[]{:S(2)}) collective-permute-start(bf16[128,256]{1,0:T(8,128)(2,1)S(1)} %get-tuple-element.18), channel_id=1, source_target_pairs={{0,16},{16,0},{32,48},{48,32},{64,80},{80,64},{96,112},{112,96},{1... | collective-permute-start | bytes 196616 | tf_op jit(solution)/shard_map/ppermute | solution.py:257
  52.8 4.3 %collective-permute-start.13 = (bf16[128,256]{1,0:T(8,128)(2,1)S(1)}, bf16[128,256]{1,0:T(8,128)(2,1)S(1)}, u32[]{:S(2)}, u32[]{:S(2)}) collective-permute-start(bf16[128,256]{1,0:T(8,128)(2,1)S(1)} %get-tuple-element.19), channel_id=1, source_target_pairs={{0,128},{16,144},{32,160},{48,176},{64,192},{80,208},{96,224},{112... | collective-permute-start | bytes 196616 | tf_op jit(solution)/shard_map/ppermute | solution.py:257
  56.0 5.2 %collective-permute-start.14 = (bf16[128,256]{1,0:T(8,128)(2,1)S(1)}, bf16[128,256]{1,0:T(8,128)(2,1)S(1)}, u32[]{:S(2)}, u32[]{:S(2)}) collective-permute-start(bf16[128,256]{1,0:T(8,128)(2,1)S(1)} %get-tuple-element.20), channel_id=1, source_target_pairs={{0,144},{16,128},{32,176},{48,160},{64,208},{80,192},{96,240},{112... | collective-permute-start | bytes 196616 | tf_op jit(solution)/shard_map/ppermute | solution.py:257
  61.2 9.5 %collective-permute-start.15 = (bf16[512,256]{1,0:T(8,128)(2,1)S(1)}, bf16[512,256]{1,0:T(8,128)(2,1)S(1)}, u32[]{:S(2)}, u32[]{:S(2)}) collective-permute-start(bf16[512,256]{1,0:T(8,128)(2,1)S(1)} %constant_dynamic-update-slice_fusion.4.refs_0_), channel_id=1, source_target_pairs={{0,32},{16,48},{32,64},{48,80},{64,96},{80,112},{96,0},{112,16},{1... | collective-permute-start | bytes 786440 | tf_op jit(solution)/shard_map/ppermute | solution.py:259
  61.2 13.7 %collective-permute-start.16 = (bf16[512,256]{1,0:T(8,128)(2,1)S(1)}, bf16[512,256]{1,0:T(8,128)(2,1)S(1)}, u32[]{:S(2)}, u32[]{:S(2)}) collective-permute-start(bf16[512,256]{1,0:T(8,128)(2,1)S(1)} %constant_dynamic-update-slice_fusion.4.refs_0_), channel_id=1, source_target_pairs={{0,96},{16,112},{32,0},{48,16},{64,32},{80,48},{96,64},{112,80},{1... | collective-permute-start | bytes 786440 | tf_op jit(solution)/shard_map/ppermute | solution.py:260
  70.7 9.3 %collective-permute-start.17 = (bf16[256,256]{1,0:T(8,128)(2,1)S(1)}, bf16[256,256]{1,0:T(8,128)(2,1)S(1)}, u32[]{:S(2)}, u32[]{:S(2)}) collective-permute-start(bf16[256,256]{1,0:T(8,128)(2,1)S(1)} %slice.28), channel_id=1, source_target_pairs={{0,32},{16,48},{32,64},{48,80},{64,96},{80,112},{96,0},{112,16},{1... | collective-permute-start | bytes 393224 | tf_op jit(solution)/shard_map/ppermute | solution.py:261
  74.9 7.5 %collective-permute-start.18 = (bf16[256,256]{1,0:T(8,128)(2,1)S(1)}, bf16[256,256]{1,0:T(8,128)(2,1)S(1)}, u32[]{:S(2)}, u32[]{:S(2)}) collective-permute-start(bf16[256,256]{1,0:T(8,128)(2,1)S(1)} %slice.29), channel_id=1, source_target_pairs={{0,96},{16,112},{32,0},{48,16},{64,32},{80,48},{96,64},{112,80},{1... | collective-permute-start | bytes 393224 | tf_op jit(solution)/shard_map/ppermute | solution.py:262
  100.5 11.0 %collective-permute-start.19 = (bf16[128,1024]{1,0:T(8,128)(2,1)S(1)}, bf16[128,1024]{1,0:T(8,128)(2,1)S(1)}, u32[]{:S(2)}, u32[]{:S(2)}) collective-permute-start(bf16[128,1024]{1,0:T(8,128)(2,1)S(1)} %get-tuple-element.27), channel_id=1, source_target_pairs={{0,16},{16,0},{32,48},{48,32},{64,80},{80,64},{96,112},{112,96},{1... | collective-permute-start | bytes 786440 | tf_op jit(solution)/shard_map/ppermute | solution.py:274
  104.3 12.0 %collective-permute-start.20 = (bf16[128,1024]{1,0:T(8,128)(2,1)S(1)}, bf16[128,1024]{1,0:T(8,128)(2,1)S(1)}, u32[]{:S(2)}, u32[]{:S(2)}) collective-permute-start(bf16[128,1024]{1,0:T(8,128)(2,1)S(1)} %get-tuple-element.26), channel_id=1, source_target_pairs={{0,128},{16,144},{32,160},{48,176},{64,192},{80,208},{96,224},{112... | collective-permute-start | bytes 786440 | tf_op jit(solution)/shard_map/ppermute | solution.py:274
  104.3 12.0 %collective-permute-start.21 = (bf16[128,1024]{1,0:T(8,128)(2,1)S(1)}, bf16[128,1024]{1,0:T(8,128)(2,1)S(1)}, u32[]{:S(2)}, u32[]{:S(2)}) collective-permute-start(bf16[128,1024]{1,0:T(8,128)(2,1)S(1)} %get-tuple-element.25), channel_id=1, source_target_pairs={{0,144},{16,128},{32,176},{48,160},{64,208},{80,192},{96,240},{112... | collective-permute-start | bytes 786440 | tf_op jit(solution)/shard_map/ppermute | solution.py:274

commit v2 on v1

--- a/solution.py
+++ b/solution.py
@@ -39,12 +39,10 @@
 def norm_kernel(pos_ref, x_ref, gain_ref, *outs):
     xi, yhi, core = pos_ref[0], pos_ref[1], pos_ref[2]
     total = None
-    for j in range(8):
-        part = x_ref[:, j * 1024 : (j + 1) * 1024].astype(F32)
+    for j in range(D // 128):
+        part = x_ref[:, j * 128 : (j + 1) * 128].astype(F32)
         part = part * part
-        for i in range(8):
-            piece = part[:, i * 128 : (i + 1) * 128]
-            total = piece if total is None else total + piece
+        total = part if total is None else total + part
     inv = lax.rsqrt(jnp.sum(total, axis=-1, keepdims=True) / D + 1e-06)
     for k in range(4):
         for a in range(2):
@@ -71,10 +69,43 @@
             out_specs=[pl.BlockSpec((step, D // 4), lambda i, p: (i, 0))] * 4,
         ),
         out_shape=[jax.ShapeDtypeStruct((rows, D // 4), BF)] * 4,
-        compiler_params=pltpu.CompilerParams(vmem_limit_bytes=16 * 1024 * 1024),
+        compiler_params=pltpu.CompilerParams(vmem_limit_bytes=60 * 1024 * 1024),
         cost_estimate=pl.CostEstimate(flops=4 << 20, bytes_accessed=4 << 20, transcendentals=0),
         name="norm",
     )(pos, hidden, gain)
+
+
+def product_kernel(count, *refs):
+    rows, weights, outs = refs[:count], refs[count : -count], refs[-count:]
+    tokens = rows[0].shape[0]
+    for n in range(4):
+        cols = slice(n * 256, (n + 1) * 256)
+        total = None
+        at = 0
+        for w_ref in weights:
+            depth = w_ref.shape[0]
+            left = jnp.concatenate([r[:, at : at + depth] for r in rows], axis=0)
+            part = jnp.dot(left, w_ref[:, cols], preferred_element_type=F32)
+            total = part if total is None else total + part
+            at += depth
+        for i in range(count):
+            outs[i][:, cols] = total[i * tokens : (i + 1) * tokens].astype(outs[i].dtype)
+
+
+def product_call(rows, weights, dtype, name):
+    vm = pl.BlockSpec(memory_space=pltpu.VMEM)
+    count, tokens = len(rows), rows[0].shape[0]
+    return pl.pallas_call(
+        lambda *refs: product_kernel(count, *refs),
+        in_specs=[vm] * (count + len(weights)),
+        out_specs=[vm] * count,
+        out_shape=[jax.ShapeDtypeStruct((tokens, 1024), dtype)] * count,
+        compiler_params=pltpu.CompilerParams(vmem_limit_bytes=24 * 1024 * 1024),
+        cost_estimate=pl.CostEstimate(
+            flops=count * tokens * 2048 * 2048, bytes_accessed=4 << 20, transcendentals=0
+        ),
+        name=name,
+    )(*rows, *weights)
 
 
 def kv_kernel(j_ref, own_ref, r1_ref, r2_ref, r3_ref, bias_ref, cos_ref, sin_ref, *outs):
@@ -106,89 +137,97 @@
     )(j, own, r1, r2, r3, bias, cos, sin)
 
 
-def attn_kernel(flag_ref, q_ref, *refs):
-    kv_refs, out_ref, kv_all, top, acc = refs[:-4], refs[-4], refs[-3], refs[-2], refs[-1]
-    qi = pl.program_id(0)
-    chunks = kv_all.shape[0]
+def attend_chunks(flag_ref, base, qi, q_ref, kv_refs, top, acc):
     heads = H // KVH
-
-    @pl.when(qi == 0)
-    def _():
-        at = 0
-        for ref in kv_refs:
-            for i in range(ref.shape[0] // 256):
-                kv_all[at] = ref[i * 256 : (i + 1) * 256, :]
-                at += 1
-
-    top[...] = jnp.full_like(top, LOW)
-    acc[...] = jnp.zeros_like(acc)
     ones = jnp.ones((256, HD), BF)
 
-    def update(c, valid):
-        keys = kv_all[c, :, :HD]
-        values = jnp.concatenate([kv_all[c, :, HD:], ones], axis=1)
+    def update(ref, low, valid):
+        keys = ref[low : low + 256, :HD]
+        values = jnp.concatenate([ref[low : low + 256, HD:], ones], axis=1)
         for h in range(heads):
-            q = q_ref[0, :, h * HD : (h + 1) * HD]
+            q = q_ref[qi, :, h * HD : (h + 1) * HD]
             s = lax.dot_general(q, keys, (((1,), (1,)), ((), ())), preferred_element_type=F32)
             if valid is not None:
                 s = jnp.where(valid, s, LOW)
             old = top[h]
             new = jnp.maximum(old, jnp.max(s, axis=-1, keepdims=True))
             top[h] = new
-            shift = new * SCALE
-            factor = jnp.exp2(old * SCALE - shift)
-            p = jnp.exp2(s * SCALE - jnp.concatenate([shift, shift], axis=1))
+            factor = jnp.exp2((old - new) * SCALE)
+            p = jnp.exp2((s - jnp.concatenate([new, new], axis=1)) * SCALE)
             if valid is not None:
                 p = jnp.where(valid, p, 0.0)
             add = jnp.dot(p.astype(BF), values, preferred_element_type=F32)
             acc[h] = acc[h] * jnp.concatenate([factor, factor], axis=1) + add
 
-    def step(c, carry):
-        f0 = flag_ref[qi, c * 2]
-        f1 = flag_ref[qi, c * 2 + 1]
-        plain = (f0 == 1) & (f1 == 1)
-
-        @pl.when(plain)
-        def _():
-            update(c, None)
-
-        @pl.when(jnp.logical_not(plain) & ((f0 + f1) > 0))
-        def _():
-            row = lax.broadcasted_iota(jnp.int32, (BLK, BLK), 0)
-            col = lax.broadcasted_iota(jnp.int32, (BLK, BLK), 1)
-            reach0 = jnp.where(f0 == 2, row, jnp.where(f0 == 1, BLK, -1))
-            reach1 = jnp.where(f1 == 2, row, jnp.where(f1 == 1, BLK, -1))
-            reach = jnp.concatenate([reach0, reach1], axis=1)
-            update(c, jnp.concatenate([col, col], axis=1) <= reach)
-
+    c = base
+    for ref in kv_refs:
+        for low in range(0, ref.shape[0], 256):
+            f0 = flag_ref[qi, c * 2]
+            f1 = flag_ref[qi, c * 2 + 1]
+            c += 1
+            plain = (f0 == 1) & (f1 == 1)
+
+            @pl.when(plain)
+            def _(ref=ref, low=low):
+                update(ref, low, None)
+
+            @pl.when(jnp.logical_not(plain) & ((f0 + f1) > 0))
+            def _(ref=ref, low=low, f0=f0, f1=f1):
+                row = lax.broadcasted_iota(jnp.int32, (BLK, BLK), 0)
+                col = lax.broadcasted_iota(jnp.int32, (BLK, BLK), 1)
+                reach0 = jnp.where(f0 == 2, row, jnp.where(f0 == 1, BLK, -1))
+                reach1 = jnp.where(f1 == 2, row, jnp.where(f1 == 1, BLK, -1))
+                reach = jnp.concatenate([reach0, reach1], axis=1)
+                update(ref, low, jnp.concatenate([col, col], axis=1) <= reach)
+
+
+def attend_first_kernel(flag_ref, q_ref, kv_ref, top, acc):
+    def step(qi, carry):
+        top[qi] = jnp.full(top.shape[1:], LOW, F32)
+        acc[qi] = jnp.zeros(acc.shape[1:], F32)
+        attend_chunks(flag_ref, 0, qi, q_ref, [kv_ref], top.at[qi], acc.at[qi])
         return carry
 
-    lax.fori_loop(0, chunks, step, 0)
-    for h in range(heads):
-        out_ref[0, :, h * HD : (h + 1) * HD] = (acc[h, :, :HD] / acc[h, :, HD:]).astype(BF)
-
-
-def attn_call(flags, q4, parts):
-    chunks = sum(p.shape[0] for p in parts) // 256
-    return pl.pallas_call(
-        attn_kernel,
-        grid_spec=pltpu.PrefetchScalarGridSpec(
-            num_scalar_prefetch=1,
-            grid=(4,),
-            in_specs=[pl.BlockSpec((1, BLK, GW), lambda i, f: (i, 0, 0))]
-            + [pl.BlockSpec(p.shape, lambda i, f: (0, 0)) for p in parts],
-            out_specs=pl.BlockSpec((1, BLK, GW), lambda i, f: (i, 0, 0)),
-            scratch_shapes=[
-                pltpu.VMEM((chunks, 256, 2 * HD), BF),
-                pltpu.VMEM((H // KVH, BLK, HD), F32),
-                pltpu.VMEM((H // KVH, BLK, 2 * HD), F32),
-            ],
-        ),
-        out_shape=jax.ShapeDtypeStruct((4, BLK, GW), BF),
+    lax.fori_loop(0, 4, step, 0)
+
+
+def attend_more_kernel(flag_ref, q_ref, up_ref, down_ref, top_in, acc_in, top, acc):
+    def step(qi, carry):
+        attend_chunks(flag_ref, 2, qi, q_ref, [up_ref, down_ref], top.at[qi], acc.at[qi])
+        return carry
+
+    lax.fori_loop(0, 4, step, 0)
+
+
+def attend_last_kernel(blocks, flag_ref, q_ref, far0_ref, far1_ref, top_in, acc_in, *refs):
+    outs, (top, acc) = refs[:-2], refs[-2:]
+    for i, qi in enumerate(blocks):
+        top[...] = top_in[qi]
+        acc[...] = acc_in[qi]
+        attend_chunks(flag_ref, 6, qi, q_ref, [far0_ref, far1_ref], top, acc)
+        for h in range(H // KVH):
+            outs[i][:, h * HD : (h + 1) * HD] = (acc[h, :, :HD] / acc[h, :, HD:]).astype(BF)
+
+
+STATE = [
+    jax.ShapeDtypeStruct((4, H // KVH, BLK, HD), F32),
+    jax.ShapeDtypeStruct((4, H // KVH, BLK, 2 * HD), F32),
+]
+
+
+def attend_call(kernel, flags, arrays, outs, scratch=(), aliases=None, share=1, name="attend"):
+    vm = pl.BlockSpec(memory_space=pltpu.VMEM)
+    return pl.pallas_call(
+        kernel,
+        in_specs=[pl.BlockSpec(memory_space=pltpu.SMEM)] + [vm] * len(arrays),
+        out_specs=[vm] * len(outs),
+        out_shape=outs,
+        scratch_shapes=list(scratch),
+        input_output_aliases=aliases or {},
         compiler_params=pltpu.CompilerParams(vmem_limit_bytes=24 * 1024 * 1024),
-        cost_estimate=pl.CostEstimate(flops=6 << 30, bytes_accessed=4 << 20, transcendentals=8 << 20),
-        name="attend",
-    )(flags, q4, *parts)
+        cost_estimate=pl.CostEstimate(flops=share << 30, bytes_accessed=4 << 20, transcendentals=share << 20),
+        name=name,
+    )(flags, *arrays)
 
 
 def place_kernel(j_ref, *refs):
@@ -234,9 +273,9 @@
     w_y = lax.ppermute(kv_weight, ("ctx", "fsdp"), DIAG_PAIRS)
 
     normed = norm_call(jnp.stack([xi, yhi, core]), hidden, norm_gain.reshape(1, D))
+    n2 = lax.ppermute(normed[2], "fsdp", x_pairs(2))
     n1 = lax.ppermute(normed[1], "fsdp", x_pairs(1))
     n3 = lax.ppermute(normed[3], "fsdp", x_pairs(3))
-    n2 = lax.ppermute(normed[2], "fsdp", x_pairs(2))
     w_yc = lax.ppermute(w_y, "fsdp", CORE_PAIRS)
 
     q_parts = []
@@ -245,12 +284,10 @@
         q_parts.append(piece if k == 0 else lax.ppermute(piece, "ctx", member_pairs(k)))
     q4 = jnp.stack(q_parts)
 
-    weight = jnp.concatenate([kv_weight, w_core, w_y, w_yc], axis=0)
-    own = jnp.dot(normed[0], weight, preferred_element_type=F32)
-    back = []
-    for got, k in ((n1, 3), (n3, 1), (n2, 2)):
-        product = jnp.dot(got, weight, preferred_element_type=F32).astype(BF)
-        back.append(lax.ppermute(product, "fsdp", x_pairs(k)))
+    weights = [kv_weight, w_core, w_y, w_yc]
+    products = product_call([n1, n3, n2], weights, BF, "products")
+    back = [lax.ppermute(p, "fsdp", x_pairs(k)) for p, k in zip(products, (3, 1, 2))]
+    (own,) = product_call([normed[0]], weights, F32, "own_product")
 
     cos, sin = rotary_tables(c * BLK, BLK)
     kvs = kv_call(j1, own, back[0], back[1], back[2], kv_bias.reshape(1, -1), cos, sin)
@@ -270,8 +307,26 @@
     order = q_ids[:, None] - u_ids[None, :]
     flags = jnp.where(order == 0, 2, jnp.where(order > 0, 1, 0)) * seen.astype(jnp.int32)
 
-    out4 = attn_call(flags.astype(jnp.int32), q4, [group, up, down, far0, far1])
-    parts = [out4[0]] + [lax.ppermute(out4[k], "ctx", member_pairs(k)) for k in (1, 2, 3)]
+    flags = flags.astype(jnp.int32)
+
+    top, acc = attend_call(attend_first_kernel, flags, [q4, group], STATE, share=1, name="attend_first")
+    top, acc = attend_call(
+        attend_more_kernel, flags, [q4, up, down, top, acc], STATE, aliases={4: 0, 5: 1}, share=3, name="attend_more"
+    )
+
+    def finish(blocks, name):
+        return attend_call(
+            lambda *refs: attend_last_kernel(blocks, *refs),
+            flags,
+            [q4, far0, far1, top, acc],
+            [jax.ShapeDtypeStruct((BLK, GW), BF)] * len(blocks),
+            scratch=[pltpu.VMEM(STATE[0].shape[1:], F32), pltpu.VMEM(STATE[1].shape[1:], F32)],
+            name=name,
+        )
+
+    out3, out2 = finish((3, 2), "attend_others")
+    out1, out0 = finish((1, 0), "attend_own")
+    parts = [out0] + [lax.ppermute(o, "ctx", member_pairs(k)) for k, o in ((1, out1), (2, out2), (3, out3))]
     return place_call(j1, parts).reshape(1, BLK, H * HD)
 
 

time: 117 us -> 110 us (0.940)
  the two profiles are of different devices: /device:TPU:210 before, /device:TPU:32 now
where the time goes in v2:
time: 110 us; the launch traced here: 108 us
  waiting for transfers between devices  50.6 us (46%)
  starting transfers between devices  30.4 us (28%)
  Pallas kernels  22.6 us (21%)
  local copies, waits for them, and re-layouts  2.62 us (2%)
  other arithmetic  1.51 us (1%)
    ppermute x1, waiting for transfers between devices, on_device(): w_y = lax.ppermute(kv_weight, ('ctx', 'fsdp'), DIAG_PAIRS)  12.1 us
    pallas_call x4, Pallas kernels, attend_call(): pl.pallas_call(kernel, in_specs=[pl.BlockSpec(memory_space=pltpu.SMEM)] +...  10.7 us
    ppermute x3, waiting for transfers between devices, on_device(): lax.ppermute(p, 'fsdp', x_pairs(k))  9.28 us
    ppermute x3, waiting for transfers between devices, on_device(): lax.ppermute(kvs[k], 'ctx', member_pairs(k))  7.78 us
    ppermute x3, waiting for transfers between devices, on_device(): lax.ppermute(o, 'ctx', member_pairs(k))  6.15 us
    ppermute x1, waiting for transfers between devices, on_device(): n3 = lax.ppermute(normed[3], 'fsdp', x_pairs(3))  5.9 us
    pallas_call x2, Pallas kernels, product_call(): pl.pallas_call(lambda *refs: product_kernel(count, *refs), in_specs=[vm]...  5.48 us
    pallas_call x1, Pallas kernels, norm_call(): pl.pallas_call(norm_kernel, grid_spec=pltpu.PrefetchScalarGridSpec(num_sc...  4.98 us
  transfers between devices with their start and end apart: 22, of which 13 were waited for; matrix products, arithmetic and copies ran while one was open for 4% of the time, Pallas kernels for 18%

profile of v2, /device:TPU:32, one launch (start us, length us, event | category | flops | bytes accessed | tf_op | source)
XLA Modules:
  0.0 107.9 jit_solution(15389732046443344819)
XLA Ops:
  0.0 3.0 %collective-permute-start.4 = (bf16[512,1024]{1,0:T(8,128)(2,1)}, bf16[512,1024]{1,0:T(8,128)(2,1)S(1)}, u32[]{:S(2)}, u32[]{:S(2)}) collective-permute-start(bf16[512,1024]{1,0:T(8,128)(2,1)} %refs_3_.1), channel_id=1, source_target_pairs={{0,136},{1,137},{2,138},{3,139},{4,140},{5,141},{6,142},{7,143},{8... | collective-permute-start | bytes 3145736 | tf_op jit(solution)/shard_map/ppermute | solution.py:273
  3.0 0.6 pad_add_fusion.1.pos_ref
  3.6 5.0 %norm.1 = (bf16[128,2048]{1,0:T(8,128)(2,1)}, bf16[128,2048]{1,0:T(8,128)(2,1)}, bf16[128,2048]{1,0:T(8,128)(2,1)}, bf16[128,2048]{1,0:T(8,128)(2,1)}) custom-call(s32[3]{0:T(128)} %pad_add_fusion.1.pos_ref, bf16[128,8192]{1,0:T(8,128)(2,1)} %bitcast.33, f32[1,8192]{1,0:T(1,128)} %bitcast.37), custom_call_target="tpu_custom_call" | custom-call | flops 4194304 | bytes 4194304 | tf_op jit(solution)/shard_map/norm/pallas_call | solution.py:60
  8.6 1.5 %collective-permute-start.6 = (bf16[128,2048]{1,0:T(8,128)(2,1)}, bf16[128,2048]{1,0:T(8,128)(2,1)}, u32[]{:S(2)}, u32[]{:S(2)}) collective-permute-start(bf16[128,2048]{1,0:T(8,128)(2,1)} %get-tuple-element.25), channel_id=1, source_target_pairs={{0,2},{1,3},{2,4},{3,5},{4,6},{5,7},{6,0},{7,1},{8,10},{9,11},{10,... | collective-permute-start | bytes 1572872 | tf_op jit(solution)/shard_map/ppermute | solution.py:277
  10.1 1.7 %collective-permute-start.7 = (bf16[128,2048]{1,0:T(8,128)(2,1)}, bf16[128,2048]{1,0:T(8,128)(2,1)}, u32[]{:S(2)}, u32[]{:S(2)}) collective-permute-start(bf16[128,2048]{1,0:T(8,128)(2,1)} %get-tuple-element.26), channel_id=1, source_target_pairs={{0,6},{1,7},{2,0},{3,1},{4,2},{5,3},{6,4},{7,5},{8,14},{9,15},{10,... | collective-permute-start | bytes 1572872 | tf_op jit(solution)/shard_map/ppermute | solution.py:278
  11.8 1.8 %collective-permute-start.8 = (bf16[128,2048]{1,0:T(8,128)(2,1)}, bf16[128,2048]{1,0:T(8,128)(2,1)}, u32[]{:S(2)}, u32[]{:S(2)}) collective-permute-start(bf16[128,2048]{1,0:T(8,128)(2,1)} %get-tuple-element.27), channel_id=1, source_target_pairs={{0,4},{1,5},{2,6},{3,7},{4,0},{5,1},{6,2},{7,3},{8,12},{9,13},{10,... | collective-permute-start | bytes 1572872 | tf_op jit(solution)/shard_map/ppermute | solution.py:276
  13.7 0.6 gather_fusion
  14.3 12.1 %collective-permute-done.4.refs_3_.refs_5_ = bf16[512,1024]{1,0:T(8,128)(2,1)S(1)} collective-permute-done((bf16[512,1024]{1,0:T(8,128)(2,1)}, bf16[512,1024]{1,0:T(8,128)(2,1)S(1)}, u32[]{:S(2)}, u32[]{:S(2)}) %collective-permute-start.4) | collective-permute-done | bytes 1048608 | tf_op jit(solution)/shard_map/ppermute | solution.py:273
  26.4 0.1 copy.9
  26.6 0.6 gather_fusion.1
  27.3 1.3 %constant_dynamic-slice_fusion = (bf16[1,128,1024]{2,1,0:T(8,128)(2,1)S(1)}, bf16[128,1024]{1,0:T(8,128)(2,1)S(1)}, bf16[128,1024]{1,0:T(8,128)(2,1)S(1)}, bf16[128,1024]{1,0:T(8,128)(2,1)S(1)}) fusion(bf16[1,128,4096]{2,1,0:T(8,128)(2,1)} %param.7, s32[]{:T(128)S(6)} %select_n.68, s32[]{:T(128)S(6)} %select_n.69, s32[]{:T(128)S(6)} %select_n.71, ...), kind=kLoop, calls=%fused_computation.29 | loop fusion | bytes 2097168 | tf_op jit(solution)/shard_map/dynamic_slice | solution.py:283
  28.6 0.3 fusion
  28.9 0.2 collective-permute-start
  29.1 5.9 %collective-permute-done.7.refs_1_ = bf16[128,2048]{1,0:T(8,128)(2,1)} collective-permute-done((bf16[128,2048]{1,0:T(8,128)(2,1)}, bf16[128,2048]{1,0:T(8,128)(2,1)}, u32[]{:S(2)}, u32[]{:S(2)}) %collective-permute-start.7) | collective-permute-done | bytes 524320 | tf_op jit(solution)/shard_map/ppermute | solution.py:278
  35.0 0.1 collective-permute-start.1
  35.1 1.5 %collective-permute-done.8.refs_2_ = bf16[128,2048]{1,0:T(8,128)(2,1)} collective-permute-done((bf16[128,2048]{1,0:T(8,128)(2,1)}, bf16[128,2048]{1,0:T(8,128)(2,1)}, u32[]{:S(2)}, u32[]{:S(2)}) %collective-permute-start.8) | collective-permute-done | bytes 524320 | tf_op jit(solution)/shard_map/ppermute | solution.py:276
  36.7 3.5 %products.1 = (bf16[128,1024]{1,0:T(8,128)(2,1)S(1)}, bf16[128,1024]{1,0:T(8,128)(2,1)S(1)}, bf16[128,1024]{1,0:T(8,128)(2,1)S(1)}) custom-call(bf16[128,2048]{1,0:T(8,128)(2,1)} %collective-permute-done.6.refs_0_, bf16[128,2048]{1,0:T(8,128)(2,1)} %collective-permute-done.7.refs_1_, bf16[128,2048]{1,0:T(8,128)(2,1)} %collective-permute-done.8.refs_2_, ...), custom_call_target="tpu_custom_call" | custom-call | flops 1610612736 | bytes 4194304 | tf_op jit(solution)/shard_map/products/pallas_call | solution.py:98
  40.2 1.2 %collective-permute-start.10 = (bf16[128,1024]{1,0:T(8,128)(2,1)S(1)}, bf16[128,1024]{1,0:T(8,128)(2,1)S(1)}, u32[]{:S(2)}, u32[]{:S(2)}) collective-permute-start(bf16[128,1024]{1,0:T(8,128)(2,1)S(1)} %get-tuple-element.29), channel_id=1, source_target_pairs={{0,2},{1,3},{2,4},{3,5},{4,6},{5,7},{6,0},{7,1},{8,10},{9,11},{10,... | collective-permute-start | bytes 786440 | tf_op jit(solution)/shard_map/ppermute | solution.py:289
  41.4 2.4 %collective-permute-start.11 = (bf16[128,1024]{1,0:T(8,128)(2,1)S(1)}, bf16[128,1024]{1,0:T(8,128)(2,1)S(1)}, u32[]{:S(2)}, u32[]{:S(2)}) collective-permute-start(bf16[128,1024]{1,0:T(8,128)(2,1)S(1)} %get-tuple-element.30), channel_id=1, source_target_pairs={{0,4},{1,5},{2,6},{3,7},{4,0},{5,1},{6,2},{7,3},{8,12},{9,13},{10,... | collective-permute-start | bytes 786440 | tf_op jit(solution)/shard_map/ppermute | solution.py:289
  43.9 0.3 collective-permute-start.9
  44.3 0.1 pad_maximum_fusion.1
  44.4 2.0 %own_product.1.own_ref = f32[128,1024]{1,0:T(8,128)S(1)} custom-call(bf16[128,2048]{1,0:T(8,128)(2,1)S(1)} %copy-done.2, bf16[512,1024]{1,0:T(8,128)(2,1)S(1)} %copy-done.1, bf16[512,1024]{1,0:T(8,128)(2,1)S(1)} %collective-permute-done.3.refs_2_.refs_4_, bf16[512,1024]{1,0:T(8,128)(2,1)S(1)} %collective-permute-done.4.refs_3_.refs_5_, ...), custom_call_target="tpu_custom_call" | custom-call | flops 536870912 | bytes 4194304 | tf_op jit(solution)/shard_map/own_product/pallas_call | solution.py:98
  46.4 8.7 %collective-permute-done.10.r2_ref = bf16[128,1024]{1,0:T(8,128)(2,1)S(1)} collective-permute-done((bf16[128,1024]{1,0:T(8,128)(2,1)S(1)}, bf16[128,1024]{1,0:T(8,128)(2,1)S(1)}, u32[]{:S(2)}, u32[]{:S(2)}) %collective-permute-start.10) | collective-permute-done | bytes 262176 | tf_op jit(solution)/shard_map/ppermute | solution.py:289
  55.1 0.6 collective-permute-done.9.r1_ref
  55.7 0.4 keys_values.1
  56.0 1.1 %collective-permute-start.12 = (bf16[128,256]{1,0:T(8,128)(2,1)S(1)}, bf16[128,256]{1,0:T(8,128)(2,1)S(1)}, u32[]{:S(2)}, u32[]{:S(2)}) collective-permute-start(bf16[128,256]{1,0:T(8,128)(2,1)S(1)} %get-tuple-element.32), channel_id=1, source_target_pairs={{0,16},{16,0},{32,48},{48,32},{64,80},{80,64},{96,112},{112,96},{1... | collective-permute-start | bytes 196616 | tf_op jit(solution)/shard_map/ppermute | solution.py:294
  57.1 1.9 %collective-permute-start.13 = (bf16[128,256]{1,0:T(8,128)(2,1)S(1)}, bf16[128,256]{1,0:T(8,128)(2,1)S(1)}, u32[]{:S(2)}, u32[]{:S(2)}) collective-permute-start(bf16[128,256]{1,0:T(8,128)(2,1)S(1)} %get-tuple-element.33), channel_id=1, source_target_pairs={{0,128},{16,144},{32,160},{48,176},{64,192},{80,208},{96,224},{112... | collective-permute-start | bytes 196616 | tf_op jit(solution)/shard_map/ppermute | solution.py:294
  59.0 3.6 %collective-permute-done.12 = bf16[128,256]{1,0:T(8,128)(2,1)S(1)} collective-permute-done((bf16[128,256]{1,0:T(8,128)(2,1)S(1)}, bf16[128,256]{1,0:T(8,128)(2,1)S(1)}, u32[]{:S(2)}, u32[]{:S(2)}) %collective-permute-start.12) | collective-permute-done | bytes 65568 | tf_op jit(solution)/shard_map/ppermute | solution.py:294
  62.6 1.3 %collective-permute-start.14 = (bf16[128,256]{1,0:T(8,128)(2,1)S(1)}, bf16[128,256]{1,0:T(8,128)(2,1)S(1)}, u32[]{:S(2)}, u32[]{:S(2)}) collective-permute-start(bf16[128,256]{1,0:T(8,128)(2,1)S(1)} %get-tuple-element.34), channel_id=1, source_target_pairs={{0,144},{16,128},{32,176},{48,160},{64,208},{80,192},{96,240},{112... | collective-permute-start | bytes 196616 | tf_op jit(solution)/shard_map/ppermute | solution.py:294
  63.9 4.2 %collective-permute-done.14 = bf16[128,256]{1,0:T(8,128)(2,1)S(1)} collective-permute-done((bf16[128,256]{1,0:T(8,128)(2,1)S(1)}, bf16[128,256]{1,0:T(8,128)(2,1)S(1)}, u32[]{:S(2)}, u32[]{:S(2)}) %collective-permute-start.14) | collective-permute-done | bytes 65568 | tf_op jit(solution)/shard_map/ppermute | solution.py:294
  68.1 3.1 %collective-permute-start.15 = (bf16[512,256]{1,0:T(8,128)(2,1)S(1)}, bf16[512,256]{1,0:T(8,128)(2,1)S(1)}, u32[]{:S(2)}, u32[]{:S(2)}) collective-permute-start(bf16[512,256]{1,0:T(8,128)(2,1)S(1)} %constant_dynamic-update-slice_fusion.kv_ref), channel_id=1, source_target_pairs={{0,32},{16,48},{32,64},{48,80},{64,96},{80,112},{96,0},{112,16},{1... | collective-permute-start | bytes 786440 | tf_op jit(solution)/shard_map/ppermute | solution.py:296
  71.2 4.3 %collective-permute-start.17 = (bf16[512,256]{1,0:T(8,128)(2,1)S(1)}, bf16[512,256]{1,0:T(8,128)(2,1)S(1)}, u32[]{:S(2)}, u32[]{:S(2)}) collective-permute-start(bf16[512,256]{1,0:T(8,128)(2,1)S(1)} %constant_dynamic-update-slice_fusion.kv_ref), channel_id=1, source_target_pairs={{0,96},{16,112},{32,0},{48,16},{64,32},{80,48},{96,64},{112,80},{1... | collective-permute-start | bytes 786440 | tf_op jit(solution)/shard_map/ppermute | solution.py:297
  75.5 0.1 pad_maximum_fusion.q_ref.refs_1_
  75.7 5.2 %attend_first.1 = (f32[4,8,128,128]{3,2,1,0:T(8,128)S(1)}, f32[4,8,128,256]{3,2,1,0:T(8,128)S(1)}) custom-call(s32[4,16]{1,0:T(4,128)S(1)} %select_select_fusion.flag_ref.refs_0_, bf16[4,128,1024]{2,1,0:T(8,128)(2,1)S(1)} %pad_maximum_fusion.q_ref.refs_1_, bf16[512,256]{1,0:T(8,128)(2,1)S(1)} %constant_dynamic-update-slice_fusion.kv_ref), custom_call_target="tpu_custom_call" | custom-call | flops 1073741824 | bytes 4194304 | tf_op jit(solution)/shard_map/attend_first/pallas_call | solution.py:220
  80.9 4.6 %collective-permute-done.15.up_ref = bf16[512,256]{1,0:T(8,128)(2,1)S(1)} collective-permute-done((bf16[512,256]{1,0:T(8,128)(2,1)S(1)}, bf16[512,256]{1,0:T(8,128)(2,1)S(1)}, u32[]{:S(2)}, u32[]{:S(2)}) %collective-permute-start.15) | collective-permute-done | bytes 262176 | tf_op jit(solution)/shard_map/ppermute | solution.py:296
  85.4 0.1 collective-permute-start.16
  85.5 1.6 %collective-permute-done.17.down_ref = bf16[512,256]{1,0:T(8,128)(2,1)S(1)} collective-permute-done((bf16[512,256]{1,0:T(8,128)(2,1)S(1)}, bf16[512,256]{1,0:T(8,128)(2,1)S(1)}, u32[]{:S(2)}, u32[]{:S(2)}) %collective-permute-start.17) | collective-permute-done | bytes 262176 | tf_op jit(solution)/shard_map/ppermute | solution.py:297
  87.1 2.6 %collective-permute-start.18 = (bf16[256,256]{1,0:T(8,128)(2,1)S(1)}, bf16[256,256]{1,0:T(8,128)(2,1)S(1)}, u32[]{:S(2)}, u32[]{:S(2)}) collective-permute-start(bf16[256,256]{1,0:T(8,128)(2,1)S(1)} %slice.13), channel_id=1, source_target_pairs={{0,96},{16,112},{32,0},{48,16},{64,32},{80,48},{96,64},{112,80},{1... | collective-permute-start | bytes 393224 | tf_op jit(solution)/shard_map/ppermute | solution.py:299
  89.7 2.2 %attend_more.1 = (f32[4,8,128,128]{3,2,1,0:T(8,128)S(1)}, f32[4,8,128,256]{3,2,1,0:T(8,128)S(1)}) custom-call(s32[4,16]{1,0:T(4,128)S(1)} %select_select_fusion.flag_ref.refs_0_, bf16[4,128,1024]{2,1,0:T(8,128)(2,1)S(1)} %pad_maximum_fusion.q_ref.refs_1_, ...), custom_call_target="tpu_custom_call", output_to_operand_aliasing={{0}: (4, {}), {1}: (5, {})} | custom-call | flops 3221225472 | bytes 4194304 | tf_op jit(solution)/shard_map/attend_more/pallas_call | solution.py:220
  91.9 0.7 collective-permute-done.16.refs_2_
  92.6 1.1 %collective-permute-done.18.refs_3_ = bf16[256,256]{1,0:T(8,128)(2,1)S(1)} collective-permute-done((bf16[256,256]{1,0:T(8,128)(2,1)S(1)}, bf16[256,256]{1,0:T(8,128)(2,1)S(1)}, u32[]{:S(2)}, u32[]{:S(2)}) %collective-permute-start.18) | collective-permute-done | bytes 131104 | tf_op jit(solution)/shard_map/ppermute | solution.py:299
  93.7 2.4 %attend_others.1 = (bf16[128,1024]{1,0:T(8,128)(2,1)S(1)}, bf16[128,1024]{1,0:T(8,128)(2,1)S(1)}) custom-call(s32[4,16]{1,0:T(4,128)S(1)} %select_select_fusion.flag_ref.refs_0_, bf16[4,128,1024]{2,1,0:T(8,128)(2,1)S(1)} %pad_maximum_fusion.q_ref.refs_1_, bf16[256,256]{1,0:T(8,128)(2,1)S(1)} %collective-permute-done.16.refs_2_, ...), custom_call_target="tpu_custom_call" | custom-call | flops 1073741824 | bytes 4194304 | tf_op jit(solution)/shard_map/attend_others/pallas_call | solution.py:220
  96.1 0.8 collective-permute-start.20
  97.0 1.0 attend_own.1
  97.9 2.8 %collective-permute-start.19 = (bf16[128,1024]{1,0:T(8,128)(2,1)S(1)}, bf16[128,1024]{1,0:T(8,128)(2,1)S(1)}, u32[]{:S(2)}, u32[]{:S(2)}) collective-permute-start(bf16[128,1024]{1,0:T(8,128)(2,1)S(1)} %get-tuple-element.40), channel_id=1, source_target_pairs={{0,16},{16,0},{32,48},{48,32},{64,80},{80,64},{96,112},{112,96},{1... | collective-permute-start | bytes 786440 | tf_op jit(solution)/shard_map/ppermute | solution.py:329
  100.8 4.6 %collective-permute-done.20.refs_2_ = bf16[128,1024]{1,0:T(8,128)(2,1)S(1)} collective-permute-done((bf16[128,1024]{1,0:T(8,128)(2,1)S(1)}, bf16[128,1024]{1,0:T(8,128)(2,1)S(1)}, u32[]{:S(2)}, u32[]{:S(2)}) %collective-permute-start.20) | collective-permute-done | bytes 262176 | tf_op jit(solution)/shard_map/ppermute | solution.py:329
  105.4 1.5 %collective-permute-done.19.refs_1_ = bf16[128,1024]{1,0:T(8,128)(2,1)S(1)} collective-permute-done((bf16[128,1024]{1,0:T(8,128)(2,1)S(1)}, bf16[128,1024]{1,0:T(8,128)(2,1)S(1)}, u32[]{:S(2)}, u32[]{:S(2)}) %collective-permute-start.19) | collective-permute-done | bytes 262176 | tf_op jit(solution)/shard_map/ppermute | solution.py:329
  106.9 1.0 place.1
  (41 shorter events, 0.6 us)
Async XLA Ops:
  0.0 13.7 %copy-start = (s32[1,16,16]{2,1,0:T(8,128)S(1)}, s32[1,16,16]{2,1,0:T(8,128)}, u32[]{:S(2)}) copy-start(s32[1,16,16]{2,1,0:T(8,128)} %param.11) | copy-start | bytes 3076
  0.0 26.4 %collective-permute-start.4 = (bf16[512,1024]{1,0:T(8,128)(2,1)}, bf16[512,1024]{1,0:T(8,128)(2,1)S(1)}, u32[]{:S(2)}, u32[]{:S(2)}) collective-permute-start(bf16[512,1024]{1,0:T(8,128)(2,1)} %refs_3_.1), channel_id=1, source_target_pairs={{0,136},{1,137},{2,138},{3,139},{4,140},{5,141},{6,142},{7,143},{8... | collective-permute-start | bytes 3145736 | tf_op jit(solution)/shard_map/ppermute | solution.py:273
  3.0 33.6 %collective-permute-start.3 = (bf16[512,1024]{1,0:T(8,128)(2,1)}, bf16[512,1024]{1,0:T(8,128)(2,1)S(1)}, u32[]{:S(2)}, u32[]{:S(2)}) collective-permute-start(bf16[512,1024]{1,0:T(8,128)(2,1)} %refs_3_.1), channel_id=1, source_target_pairs={{0,1},{1,0},{2,3},{3,2},{4,5},{5,4},{6,7},{7,6},{8,9},{9,8},{10,11... | collective-permute-start | bytes 3145736 | tf_op jit(solution)/shard_map/ppermute | solution.py:272
  3.6 33.1 %copy-start.1 = (bf16[512,1024]{1,0:T(8,128)(2,1)S(1)}, bf16[512,1024]{1,0:T(8,128)(2,1)}, u32[]{:S(2)}) copy-start(bf16[512,1024]{1,0:T(8,128)(2,1)} %refs_3_.1) | copy-start | bytes 3145732
  8.6 20.3 %collective-permute-start.6 = (bf16[128,2048]{1,0:T(8,128)(2,1)}, bf16[128,2048]{1,0:T(8,128)(2,1)}, u32[]{:S(2)}, u32[]{:S(2)}) collective-permute-start(bf16[128,2048]{1,0:T(8,128)(2,1)} %get-tuple-element.25), channel_id=1, source_target_pairs={{0,2},{1,3},{2,4},{3,5},{4,6},{5,7},{6,0},{7,1},{8,10},{9,11},{10,... | collective-permute-start | bytes 1572872 | tf_op jit(solution)/shard_map/ppermute | solution.py:277
  10.1 24.9 %collective-permute-start.7 = (bf16[128,2048]{1,0:T(8,128)(2,1)}, bf16[128,2048]{1,0:T(8,128)(2,1)}, u32[]{:S(2)}, u32[]{:S(2)}) collective-permute-start(bf16[128,2048]{1,0:T(8,128)(2,1)} %get-tuple-element.26), channel_id=1, source_target_pairs={{0,6},{1,7},{2,0},{3,1},{4,2},{5,3},{6,4},{7,5},{8,14},{9,15},{10,... | collective-permute-start | bytes 1572872 | tf_op jit(solution)/shard_map/ppermute | solution.py:278
  11.8 24.8 %collective-permute-start.8 = (bf16[128,2048]{1,0:T(8,128)(2,1)}, bf16[128,2048]{1,0:T(8,128)(2,1)}, u32[]{:S(2)}, u32[]{:S(2)}) collective-permute-start(bf16[128,2048]{1,0:T(8,128)(2,1)} %get-tuple-element.27), channel_id=1, source_target_pairs={{0,4},{1,5},{2,6},{3,7},{4,0},{5,1},{6,2},{7,3},{8,12},{9,13},{10,... | collective-permute-start | bytes 1572872 | tf_op jit(solution)/shard_map/ppermute | solution.py:276
  26.4 10.3 %collective-permute-start.5 = (bf16[512,1024]{1,0:T(8,128)(2,1)S(1)}, bf16[512,1024]{1,0:T(8,128)(2,1)}, u32[]{:S(2)}, u32[]{:S(2)}) collective-permute-start(bf16[512,1024]{1,0:T(8,128)(2,1)S(1)} %collective-permute-done.4.refs_3_.refs_5_), channel_id=1, source_target_pairs={{0,1},{1,0},{2,3},{3,2},{4,5},{5,4},{6,7},{7,6},{8,9},{9,8},{10,11... | collective-permute-start | bytes 3145736 | tf_op jit(solution)/shard_map/ppermute | solution.py:279
  28.9 46.7 %collective-permute-start = (bf16[128,1024]{1,0:T(8,128)(2,1)S(1)}, bf16[128,1024]{1,0:T(8,128)(2,1)S(1)}, u32[]{:S(2)}, u32[]{:S(2)}) collective-permute-start(bf16[128,1024]{1,0:T(8,128)(2,1)S(1)} %get-tuple-element.48), channel_id=1, source_target_pairs={{0,16},{16,0},{32,48},{48,32},{64,80},{80,64},{96,112},{112,96},{1... | collective-permute-start | bytes 786440 | tf_op jit(solution)/shard_map/ppermute | solution.py:284
  35.0 9.4 %copy-start.2 = (bf16[128,2048]{1,0:T(8,128)(2,1)S(1)}, bf16[128,2048]{1,0:T(8,128)(2,1)}, u32[]{:S(2)}) copy-start(bf16[128,2048]{1,0:T(8,128)(2,1)} %get-tuple-element.24.refs_0_) | copy-start | bytes 1572868
  35.0 40.6 %collective-permute-start.1 = (bf16[128,1024]{1,0:T(8,128)(2,1)S(1)}, bf16[128,1024]{1,0:T(8,128)(2,1)S(1)}, u32[]{:S(2)}, u32[]{:S(2)}) collective-permute-start(bf16[128,1024]{1,0:T(8,128)(2,1)S(1)} %get-tuple-element.50), channel_id=1, source_target_pairs={{0,128},{16,144},{32,160},{48,176},{64,192},{80,208},{96,224},{112... | collective-permute-start | bytes 786440 | tf_op jit(solution)/shard_map/ppermute | solution.py:284
  40.2 14.8 %collective-permute-start.10 = (bf16[128,1024]{1,0:T(8,128)(2,1)S(1)}, bf16[128,1024]{1,0:T(8,128)(2,1)S(1)}, u32[]{:S(2)}, u32[]{:S(2)}) collective-permute-start(bf16[128,1024]{1,0:T(8,128)(2,1)S(1)} %get-tuple-element.29), channel_id=1, source_target_pairs={{0,2},{1,3},{2,4},{3,5},{4,6},{5,7},{6,0},{7,1},{8,10},{9,11},{10,... | collective-permute-start | bytes 786440 | tf_op jit(solution)/shard_map/ppermute | solution.py:289
  41.4 13.6 %collective-permute-start.11 = (bf16[128,1024]{1,0:T(8,128)(2,1)S(1)}, bf16[128,1024]{1,0:T(8,128)(2,1)S(1)}, u32[]{:S(2)}, u32[]{:S(2)}) collective-permute-start(bf16[128,1024]{1,0:T(8,128)(2,1)S(1)} %get-tuple-element.30), channel_id=1, source_target_pairs={{0,4},{1,5},{2,6},{3,7},{4,0},{5,1},{6,2},{7,3},{8,12},{9,13},{10,... | collective-permute-start | bytes 786440 | tf_op jit(solution)/shard_map/ppermute | solution.py:289
  43.9 11.8 %collective-permute-start.9 = (bf16[128,1024]{1,0:T(8,128)(2,1)S(1)}, bf16[128,1024]{1,0:T(8,128)(2,1)S(1)}, u32[]{:S(2)}, u32[]{:S(2)}) collective-permute-start(bf16[128,1024]{1,0:T(8,128)(2,1)S(1)} %get-tuple-element.28), channel_id=1, source_target_pairs={{0,6},{1,7},{2,0},{3,1},{4,2},{5,3},{6,4},{7,5},{8,14},{9,15},{10,... | collective-permute-start | bytes 786440 | tf_op jit(solution)/shard_map/ppermute | solution.py:289
  44.4 11.3 %copy-start.3 = (f32[1024]{0:T(1024)S(1)}, f32[1024]{0:T(1024)}, u32[]{:S(2)}) copy-start(f32[1024]{0:T(1024)} %param.9) | copy-start | bytes 12292
  55.0 20.5 %collective-permute-start.2 = (bf16[128,1024]{1,0:T(8,128)(2,1)S(1)}, bf16[128,1024]{1,0:T(8,128)(2,1)S(1)}, u32[]{:S(2)}, u32[]{:S(2)}) collective-permute-start(bf16[128,1024]{1,0:T(8,128)(2,1)S(1)} %get-tuple-element.49), channel_id=1, source_target_pairs={{0,144},{16,128},{32,176},{48,160},{64,208},{80,192},{96,240},{112... | collective-permute-start | bytes 786440 | tf_op jit(solution)/shard_map/ppermute | solution.py:284
  56.0 6.6 %collective-permute-start.12 = (bf16[128,256]{1,0:T(8,128)(2,1)S(1)}, bf16[128,256]{1,0:T(8,128)(2,1)S(1)}, u32[]{:S(2)}, u32[]{:S(2)}) collective-permute-start(bf16[128,256]{1,0:T(8,128)(2,1)S(1)} %get-tuple-element.32), channel_id=1, source_target_pairs={{0,16},{16,0},{32,48},{48,32},{64,80},{80,64},{96,112},{112,96},{1... | collective-permute-start | bytes 196616 | tf_op jit(solution)/shard_map/ppermute | solution.py:294
  57.1 6.8 %collective-permute-start.13 = (bf16[128,256]{1,0:T(8,128)(2,1)S(1)}, bf16[128,256]{1,0:T(8,128)(2,1)S(1)}, u32[]{:S(2)}, u32[]{:S(2)}) collective-permute-start(bf16[128,256]{1,0:T(8,128)(2,1)S(1)} %get-tuple-element.33), channel_id=1, source_target_pairs={{0,128},{16,144},{32,160},{48,176},{64,192},{80,208},{96,224},{112... | collective-permute-start | bytes 196616 | tf_op jit(solution)/shard_map/ppermute | solution.py:294
  62.6 5.5 %collective-permute-start.14 = (bf16[128,256]{1,0:T(8,128)(2,1)S(1)}, bf16[128,256]{1,0:T(8,128)(2,1)S(1)}, u32[]{:S(2)}, u32[]{:S(2)}) collective-permute-start(bf16[128,256]{1,0:T(8,128)(2,1)S(1)} %get-tuple-element.34), channel_id=1, source_target_pairs={{0,144},{16,128},{32,176},{48,160},{64,208},{80,192},{96,240},{112... | collective-permute-start | bytes 196616 | tf_op jit(solution)/shard_map/ppermute | solution.py:294
  68.1 17.3 %collective-permute-start.15 = (bf16[512,256]{1,0:T(8,128)(2,1)S(1)}, bf16[512,256]{1,0:T(8,128)(2,1)S(1)}, u32[]{:S(2)}, u32[]{:S(2)}) collective-permute-start(bf16[512,256]{1,0:T(8,128)(2,1)S(1)} %constant_dynamic-update-slice_fusion.kv_ref), channel_id=1, source_target_pairs={{0,32},{16,48},{32,64},{48,80},{64,96},{80,112},{96,0},{112,16},{1... | collective-permute-start | bytes 786440 | tf_op jit(solution)/shard_map/ppermute | solution.py:296
  71.2 15.9 %collective-permute-start.17 = (bf16[512,256]{1,0:T(8,128)(2,1)S(1)}, bf16[512,256]{1,0:T(8,128)(2,1)S(1)}, u32[]{:S(2)}, u32[]{:S(2)}) collective-permute-start(bf16[512,256]{1,0:T(8,128)(2,1)S(1)} %constant_dynamic-update-slice_fusion.kv_ref), channel_id=1, source_target_pairs={{0,96},{16,112},{32,0},{48,16},{64,32},{80,48},{96,64},{112,80},{1... | collective-permute-start | bytes 786440 | tf_op jit(solution)/shard_map/ppermute | solution.py:297
  85.4 7.2 %collective-permute-start.16 = (bf16[256,256]{1,0:T(8,128)(2,1)S(1)}, bf16[256,256]{1,0:T(8,128)(2,1)S(1)}, u32[]{:S(2)}, u32[]{:S(2)}) collective-permute-start(bf16[256,256]{1,0:T(8,128)(2,1)S(1)} %slice.12), channel_id=1, source_target_pairs={{0,32},{16,48},{32,64},{48,80},{64,96},{80,112},{96,0},{112,16},{1... | collective-permute-start | bytes 393224 | tf_op jit(solution)/shard_map/ppermute | solution.py:298
  87.1 6.6 %collective-permute-start.18 = (bf16[256,256]{1,0:T(8,128)(2,1)S(1)}, bf16[256,256]{1,0:T(8,128)(2,1)S(1)}, u32[]{:S(2)}, u32[]{:S(2)}) collective-permute-start(bf16[256,256]{1,0:T(8,128)(2,1)S(1)} %slice.13), channel_id=1, source_target_pairs={{0,96},{16,112},{32,0},{48,16},{64,32},{80,48},{96,64},{112,80},{1... | collective-permute-start | bytes 393224 | tf_op jit(solution)/shard_map/ppermute | solution.py:299
  96.1 9.3 %collective-permute-start.20 = (bf16[128,1024]{1,0:T(8,128)(2,1)S(1)}, bf16[128,1024]{1,0:T(8,128)(2,1)S(1)}, u32[]{:S(2)}, u32[]{:S(2)}) collective-permute-start(bf16[128,1024]{1,0:T(8,128)(2,1)S(1)} %get-tuple-element.41), channel_id=1, source_target_pairs={{0,128},{16,144},{32,160},{48,176},{64,192},{80,208},{96,224},{112... | collective-permute-start | bytes 786440 | tf_op jit(solution)/shard_map/ppermute | solution.py:329
  97.0 8.4 %collective-permute-start.21 = (bf16[128,1024]{1,0:T(8,128)(2,1)S(1)}, bf16[128,1024]{1,0:T(8,128)(2,1)S(1)}, u32[]{:S(2)}, u32[]{:S(2)}) collective-permute-start(bf16[128,1024]{1,0:T(8,128)(2,1)S(1)} %get-tuple-element.42), channel_id=1, source_target_pairs={{0,144},{16,128},{32,176},{48,160},{64,208},{80,192},{96,240},{112... | collective-permute-start | bytes 786440 | tf_op jit(solution)/shard_map/ppermute | solution.py:329
  97.9 9.0 %collective-permute-start.19 = (bf16[128,1024]{1,0:T(8,128)(2,1)S(1)}, bf16[128,1024]{1,0:T(8,128)(2,1)S(1)}, u32[]{:S(2)}, u32[]{:S(2)}) collective-permute-start(bf16[128,1024]{1,0:T(8,128)(2,1)S(1)} %get-tuple-element.40), channel_id=1, source_target_pairs={{0,16},{16,0},{32,48},{48,32},{64,80},{80,64},{96,112},{112,96},{1... | collective-permute-start | bytes 786440 | tf_op jit(solution)/shard_map/ppermute | solution.py:329

commit v3 on v2

--- a/solution.py
+++ b/solution.py
@@ -36,40 +36,58 @@
     return [(c, (c & 8) | ((c + k) & 7)) for c in range(16)]
 
 
-def norm_kernel(pos_ref, x_ref, gain_ref, *outs):
+def norm_kernel(pos_ref, x_hbm, gain_hbm, *refs):
+    outs, (x_ref, gain_ref, sems) = refs[:4], refs[4:]
     xi, yhi, core = pos_ref[0], pos_ref[1], pos_ref[2]
-    total = None
-    for j in range(D // 128):
-        part = x_ref[:, j * 128 : (j + 1) * 128].astype(F32)
-        part = part * part
-        total = part if total is None else total + part
-    inv = lax.rsqrt(jnp.sum(total, axis=-1, keepdims=True) / D + 1e-06)
-    for k in range(4):
-        for a in range(2):
-            for b in range(2):
-                src = (yhi ^ a) * 4096 + ((xi + k) & 3) * 1024 + (core ^ b) * 512
-                cols = pl.ds(pl.multiple_of(src, 512), 512)
-                wide = x_ref[:, cols].astype(F32)
-                dst = (a * 2 + b) * 512
-                outs[k][:, dst : dst + 512] = (wide * inv * gain_ref[:, cols]).astype(BF)
+    step = 32
+    count = x_ref.shape[0] // step
+    copies = [
+        pltpu.make_async_copy(
+            x_hbm.at[pl.ds(i * step, step)], x_ref.at[pl.ds(i * step, step)], sems.at[i]
+        )
+        for i in range(count)
+    ]
+    gain_copy = pltpu.make_async_copy(gain_hbm, gain_ref, sems.at[count])
+    copies[0].start()
+    gain_copy.start()
+    for copy in copies[1:]:
+        copy.start()
+    for n in range(count):
+        copies[n].wait()
+        if n == 0:
+            gain_copy.wait()
+        rows = slice(n * step, (n + 1) * step)
+        total = None
+        for j in range(D // 128):
+            part = x_ref[rows, j * 128 : (j + 1) * 128].astype(F32)
+            part = part * part
+            total = part if total is None else total + part
+        inv = lax.rsqrt(jnp.sum(total, axis=-1, keepdims=True) / D + 1e-06)
+        for k in (2, 1, 3, 0):
+            for a in range(2):
+                for b in range(2):
+                    src = (yhi ^ a) * 4096 + ((xi + k) & 3) * 1024 + (core ^ b) * 512
+                    cols = pl.ds(pl.multiple_of(src, 512), 512)
+                    wide = x_ref[rows, cols].astype(F32)
+                    dst = (a * 2 + b) * 512
+                    outs[k][rows, dst : dst + 512] = (wide * inv * gain_ref[:, cols]).astype(BF)
 
 
 def norm_call(pos, hidden, gain):
     rows = hidden.shape[0]
-    step = 32
+    vm = pl.BlockSpec(memory_space=pltpu.VMEM)
+    hbm = pl.BlockSpec(memory_space=pl.ANY)
     return pl.pallas_call(
         norm_kernel,
-        grid_spec=pltpu.PrefetchScalarGridSpec(
-            num_scalar_prefetch=1,
-            grid=(rows // step,),
-            in_specs=[
-                pl.BlockSpec((step, D), lambda i, p: (i, 0)),
-                pl.BlockSpec((1, D), lambda i, p: (0, 0)),
-            ],
-            out_specs=[pl.BlockSpec((step, D // 4), lambda i, p: (i, 0))] * 4,
-        ),
+        in_specs=[pl.BlockSpec(memory_space=pltpu.SMEM), hbm, hbm],
+        out_specs=[vm] * 4,
         out_shape=[jax.ShapeDtypeStruct((rows, D // 4), BF)] * 4,
-        compiler_params=pltpu.CompilerParams(vmem_limit_bytes=60 * 1024 * 1024),
+        scratch_shapes=[
+            pltpu.VMEM((rows, D), BF),
+            pltpu.VMEM((1, D), F32),
+            pltpu.SemaphoreType.DMA((rows // 32 + 1,)),
+        ],
+        compiler_params=pltpu.CompilerParams(vmem_limit_bytes=50 * 1024 * 1024),
         cost_estimate=pl.CostEstimate(flops=4 << 20, bytes_accessed=4 << 20, transcendentals=0),
         name="norm",
     )(pos, hidden, gain)
@@ -80,14 +98,9 @@
     tokens = rows[0].shape[0]
     for n in range(4):
         cols = slice(n * 256, (n + 1) * 256)
-        total = None
-        at = 0
-        for w_ref in weights:
-            depth = w_ref.shape[0]
-            left = jnp.concatenate([r[:, at : at + depth] for r in rows], axis=0)
-            part = jnp.dot(left, w_ref[:, cols], preferred_element_type=F32)
-            total = part if total is None else total + part
-            at += depth
+        left = jnp.concatenate([r[...] for r in rows], axis=0)
+        right = jnp.concatenate([w[:, cols] for w in weights], axis=0)
+        total = jnp.dot(left, right, preferred_element_type=F32)
         for i in range(count):
             outs[i][:, cols] = total[i * tokens : (i + 1) * tokens].astype(outs[i].dtype)
 
@@ -137,92 +150,127 @@
     )(j, own, r1, r2, r3, bias, cos, sin)
 
 
-def attend_chunks(flag_ref, base, qi, q_ref, kv_refs, top, acc):
-    heads = H // KVH
-    ones = jnp.ones((256, HD), BF)
-
-    def update(ref, low, valid):
-        keys = ref[low : low + 256, :HD]
-        values = jnp.concatenate([ref[low : low + 256, HD:], ones], axis=1)
-        for h in range(heads):
-            q = q_ref[qi, :, h * HD : (h + 1) * HD]
+def visit(pair, q_ref, pieces, reach, top, acc, fresh=False):
+    parts = [ref[pl.ds(row, 256), :] for ref, row in pieces]
+    width = 256 * len(parts)
+    keys = jnp.concatenate([p[:, :HD] for p in parts], axis=0)
+    values = jnp.concatenate([p[:, HD:] for p in parts], axis=0)
+    values = jnp.concatenate([values, jnp.ones((width, HD), BF)], axis=1)
+    for b in range(2):
+        block = pair * 2 + b
+        for h in range(0, H // KVH, 4):
+            q = jnp.concatenate([q_ref[block, :, (h + i) * HD : (h + i + 1) * HD] for i in range(4)], axis=0)
             s = lax.dot_general(q, keys, (((1,), (1,)), ((), ())), preferred_element_type=F32)
-            if valid is not None:
-                s = jnp.where(valid, s, LOW)
-            old = top[h]
-            new = jnp.maximum(old, jnp.max(s, axis=-1, keepdims=True))
-            top[h] = new
-            factor = jnp.exp2((old - new) * SCALE)
-            p = jnp.exp2((s - jnp.concatenate([new, new], axis=1)) * SCALE)
-            if valid is not None:
-                p = jnp.where(valid, p, 0.0)
+            if reach is not None:
+                col = lax.broadcasted_iota(jnp.int32, (BLK, BLK), 1)
+                valid = jnp.concatenate([col <= r for r in reach[b]], axis=1)
+                s = jnp.where(jnp.concatenate([valid] * 4, axis=0), s, LOW)
+            rows = slice(h * BLK, (h + 4) * BLK)
+            peak = jnp.max(s, axis=-1, keepdims=True)
+            if fresh:
+                new = jnp.broadcast_to(peak, (4 * BLK, HD))
+            else:
+                old = top[block, rows]
+                new = jnp.maximum(old, peak)
+            top[block, rows] = new
+            shift = new if reach is None else jnp.maximum(new, LOW / 2)
+            p = jnp.exp2((s - jnp.concatenate([shift] * (width // HD), axis=1)) * SCALE)
             add = jnp.dot(p.astype(BF), values, preferred_element_type=F32)
-            acc[h] = acc[h] * jnp.concatenate([factor, factor], axis=1) + add
-
-    c = base
-    for ref in kv_refs:
-        for low in range(0, ref.shape[0], 256):
-            f0 = flag_ref[qi, c * 2]
-            f1 = flag_ref[qi, c * 2 + 1]
-            c += 1
-            plain = (f0 == 1) & (f1 == 1)
-
-            @pl.when(plain)
-            def _(ref=ref, low=low):
-                update(ref, low, None)
-
-            @pl.when(jnp.logical_not(plain) & ((f0 + f1) > 0))
-            def _(ref=ref, low=low, f0=f0, f1=f1):
-                row = lax.broadcasted_iota(jnp.int32, (BLK, BLK), 0)
-                col = lax.broadcasted_iota(jnp.int32, (BLK, BLK), 1)
-                reach0 = jnp.where(f0 == 2, row, jnp.where(f0 == 1, BLK, -1))
-                reach1 = jnp.where(f1 == 2, row, jnp.where(f1 == 1, BLK, -1))
-                reach = jnp.concatenate([reach0, reach1], axis=1)
-                update(ref, low, jnp.concatenate([col, col], axis=1) <= reach)
+            if fresh:
+                acc[block, rows] = add
+            else:
+                factor = jnp.exp2((old - new) * SCALE)
+                acc[block, rows] = acc[block, rows] * jnp.concatenate([factor, factor], axis=1) + add
+
+
+def reaches(flag_ref, pair, blocks):
+    row = lax.broadcasted_iota(jnp.int32, (BLK, BLK), 0)
+    out = []
+    for b in range(2):
+        flags = [flag_ref[pair * 2 + b, u] for u in blocks]
+        out.append([jnp.where(f == 2, row, jnp.where(f == 1, BLK, -1)) for f in flags])
+    return out
+
+
+def flag_sum(flag_ref, pair, blocks):
+    return sum(flag_ref[pair * 2 + b, u] for b in range(2) for u in blocks)
+
+
+def all_whole(flag_ref, pair, blocks):
+    whole = True
+    for b in range(2):
+        for u in blocks:
+            whole = (flag_ref[pair * 2 + b, u] == 1) & whole
+    return whole
+
+
+def attend_source(flag_ref, source, pair, q_ref, pieces, top, acc):
+    blocks = [source * 4 + i for i in range(4)]
+    whole = all_whole(flag_ref, pair, blocks)
+
+    @pl.when(whole)
+    def _():
+        visit(pair, q_ref, pieces, None, top, acc)
+
+    for i in range(2):
+        half = blocks[2 * i : 2 * i + 2]
+
+        @pl.when(jnp.logical_not(whole) & (flag_sum(flag_ref, pair, half) > 0))
+        def _(i=i, half=half):
+            visit(pair, q_ref, pieces[i : i + 1], reaches(flag_ref, pair, half), top, acc)
 
 
 def attend_first_kernel(flag_ref, q_ref, kv_ref, top, acc):
-    def step(qi, carry):
-        top[qi] = jnp.full(top.shape[1:], LOW, F32)
-        acc[qi] = jnp.zeros(acc.shape[1:], F32)
-        attend_chunks(flag_ref, 0, qi, q_ref, [kv_ref], top.at[qi], acc.at[qi])
+    def step(pair, carry):
+        other = flag_sum(flag_ref, pair, [(1 - pair) * 2, (1 - pair) * 2 + 1])
+        both = other > 0
+
+        @pl.when(both)
+        def _():
+            visit(pair, q_ref, [(kv_ref, 0), (kv_ref, 256)], reaches(flag_ref, pair, range(4)), top, acc, True)
+
+        @pl.when(jnp.logical_not(both))
+        def _():
+            row = pl.multiple_of(pair * 256, 256)
+            mine = [pair * 2, pair * 2 + 1]
+            visit(pair, q_ref, [(kv_ref, row)], reaches(flag_ref, pair, mine), top, acc, True)
+
         return carry
 
-    lax.fori_loop(0, 4, step, 0)
+    lax.fori_loop(0, 2, step, 0)
 
 
 def attend_more_kernel(flag_ref, q_ref, up_ref, down_ref, top_in, acc_in, top, acc):
-    def step(qi, carry):
-        attend_chunks(flag_ref, 2, qi, q_ref, [up_ref, down_ref], top.at[qi], acc.at[qi])
+    def step(pair, carry):
+        for source, ref in ((1, up_ref), (2, down_ref)):
+            attend_source(flag_ref, source, pair, q_ref, [(ref, 0), (ref, 256)], top, acc)
         return carry
 
-    lax.fori_loop(0, 4, step, 0)
-
-
-def attend_last_kernel(blocks, flag_ref, q_ref, far0_ref, far1_ref, top_in, acc_in, *refs):
-    outs, (top, acc) = refs[:-2], refs[-2:]
-    for i, qi in enumerate(blocks):
-        top[...] = top_in[qi]
-        acc[...] = acc_in[qi]
-        attend_chunks(flag_ref, 6, qi, q_ref, [far0_ref, far1_ref], top, acc)
+    lax.fori_loop(0, 2, step, 0)
+
+
+def attend_last_kernel(pair, flag_ref, q_ref, far0_ref, far1_ref, top_in, acc_in, top, acc, *outs):
+    attend_source(flag_ref, 3, pair, q_ref, [(far0_ref, 0), (far1_ref, 0)], top, acc)
+    for b in range(2):
         for h in range(H // KVH):
-            outs[i][:, h * HD : (h + 1) * HD] = (acc[h, :, :HD] / acc[h, :, HD:]).astype(BF)
+            rows = slice(h * BLK, (h + 1) * BLK)
+            mixed = acc[pair * 2 + b, rows]
+            outs[b][:, h * HD : (h + 1) * HD] = (mixed[:, :HD] / mixed[:, HD:]).astype(BF)
 
 
 STATE = [
-    jax.ShapeDtypeStruct((4, H // KVH, BLK, HD), F32),
-    jax.ShapeDtypeStruct((4, H // KVH, BLK, 2 * HD), F32),
+    jax.ShapeDtypeStruct((4, GW, HD), F32),
+    jax.ShapeDtypeStruct((4, GW, 2 * HD), F32),
 ]
 
 
-def attend_call(kernel, flags, arrays, outs, scratch=(), aliases=None, share=1, name="attend"):
+def attend_call(kernel, flags, arrays, outs, aliases=None, share=1, name="attend"):
     vm = pl.BlockSpec(memory_space=pltpu.VMEM)
     return pl.pallas_call(
         kernel,
         in_specs=[pl.BlockSpec(memory_space=pltpu.SMEM)] + [vm] * len(arrays),
         out_specs=[vm] * len(outs),
         out_shape=outs,
-        scratch_shapes=list(scratch),
         input_output_aliases=aliases or {},
         compiler_params=pltpu.CompilerParams(vmem_limit_bytes=24 * 1024 * 1024),
         cost_estimate=pl.CostEstimate(flops=share << 30, bytes_accessed=4 << 20, transcendentals=share << 20),
@@ -314,18 +362,18 @@
         attend_more_kernel, flags, [q4, up, down, top, acc], STATE, aliases={4: 0, 5: 1}, share=3, name="attend_more"
     )
 
-    def finish(blocks, name):
+    def finish(pair, top, acc, name):
         return attend_call(
-            lambda *refs: attend_last_kernel(blocks, *refs),
+            lambda *refs: attend_last_kernel(pair, *refs),
             flags,
             [q4, far0, far1, top, acc],
-            [jax.ShapeDtypeStruct((BLK, GW), BF)] * len(blocks),
-            scratch=[pltpu.VMEM(STATE[0].shape[1:], F32), pltpu.VMEM(STATE[1].shape[1:], F32)],
+            STATE + [jax.ShapeDtypeStruct((BLK, GW), BF)] * 2,
+            aliases={4: 0, 5: 1},
             name=name,
         )
 
-    out3, out2 = finish((3, 2), "attend_others")
-    out1, out0 = finish((1, 0), "attend_own")
+    top, acc, out2, out3 = finish(1, top, acc, "attend_others")
+    top, acc, out0, out1 = finish(0, top, acc, "attend_own")
     parts = [out0] + [lax.ppermute(o, "ctx", member_pairs(k)) for k, o in ((1, out1), (2, out2), (3, out3))]
     return place_call(j1, parts).reshape(1, BLK, H * HD)
 

time: 110 us -> 112 us (1.018)
  starting transfers between devices: 30.4 us -> 33.2 us
  Pallas kernels: 22.6 us -> 19.9 us
  waiting for transfers between devices: 50.6 us -> 52.3 us
  local copies, waits for them, and re-layouts: 2.62 us -> 4.16 us
    ppermute x1, waiting for transfers between devices: 0.68 us -> 5.58 us  [on_device(): far0 = lax.ppermute(up[:256], 'ctx', z_pairs(2))]
    ppermute x1, starting transfers between devices: 4.25 us -> 8.33 us  [on_device(): down = lax.ppermute(group, 'ctx', z_pairs(-2))]
    ppermute x3, starting transfers between devices: 4.27 us -> 0.51 us  [on_device(): lax.ppermute(kvs[k], 'ctx', member_pairs(k))]
    ppermute x3, starting transfers between devices: 0.34 us -> 4.08 us  [on_device(): lax.ppermute(piece, 'ctx', member_pairs(k))]
    ppermute x1, starting transfers between devices: 3.08 us -> 0.01 us  [on_device(): up = lax.ppermute(group, 'ctx', z_pairs(2))]
    ppermute x3, waiting for transfers between devices: 9.28 us -> 6.25 us  [on_device(): lax.ppermute(p, 'fsdp', x_pairs(k))]
    ppermute x1, starting transfers between devices: 2.63 us -> 4.67 us  [on_device(): far1 = lax.ppermute(down[256:], 'ctx', z_pairs(-2))]
    unnamed x11 -> x15, local copies, waits for them, and re-layouts: 0.04 us -> 1.58 us
  transfers between devices with their start and end apart: 22 -> 22, of which waited for: 13 -> 13; matrix products, arithmetic and copies ran while one was open for 4% -> 3% of each run, Pallas kernels for 18% -> 14%
where the time goes in v3:
time: 112 us; the launch traced here: 111 us
  waiting for transfers between devices  52.3 us (47%)
  starting transfers between devices  33.2 us (30%)
  Pallas kernels  19.9 us (18%)
  local copies, waits for them, and re-layouts  4.16 us (4%)
    ppermute x1, waiting for transfers between devices, on_device(): w_y = lax.ppermute(kv_weight, ('ctx', 'fsdp'), DIAG_PAIRS)  12.2 us
    pallas_call x4, Pallas kernels, attend_call(): pl.pallas_call(kernel, in_specs=[pl.BlockSpec(memory_space=pltpu.SMEM)] +...  9.19 us
    ppermute x3, waiting for transfers between devices, on_device(): lax.ppermute(kvs[k], 'ctx', member_pairs(k))  8.99 us
    ppermute x1, starting transfers between devices, on_device(): down = lax.ppermute(group, 'ctx', z_pairs(-2))  8.33 us
    ppermute x3, waiting for transfers between devices, on_device(): lax.ppermute(p, 'fsdp', x_pairs(k))  6.25 us
    ppermute x3, waiting for transfers between devices, on_device(): lax.ppermute(o, 'ctx', member_pairs(k))  6 us
    ppermute x1, waiting for transfers between devices, on_device(): n3 = lax.ppermute(normed[3], 'fsdp', x_pairs(3))  5.81 us
    ppermute x1, waiting for transfers between devices, on_device(): far0 = lax.ppermute(up[:256], 'ctx', z_pairs(2))  5.58 us
  transfers between devices with their start and end apart: 22, of which 13 were waited for; matrix products, arithmetic and copies ran while one was open for 3% of the time, Pallas kernels for 14%

profile of v3, /device:TPU:32, one launch (start us, length us, event | category | flops | bytes accessed | tf_op | source)
XLA Modules:
  0.0 110.8 jit_solution(11901305136616815968)
XLA Ops:
  0.0 3.0 %collective-permute-start.4 = (bf16[512,1024]{1,0:T(8,128)(2,1)}, bf16[512,1024]{1,0:T(8,128)(2,1)S(1)}, u32[]{:S(2)}, u32[]{:S(2)}) collective-permute-start(bf16[512,1024]{1,0:T(8,128)(2,1)} %refs_3_.1), channel_id=1, source_target_pairs={{0,136},{1,137},{2,138},{3,139},{4,140},{5,141},{6,142},{7,143},{8... | collective-permute-start | bytes 3145736 | tf_op jit(solution)/shard_map/ppermute | solution.py:321
  3.1 0.8 copy-done.4
  3.9 3.8 %norm.1 = (bf16[128,2048]{1,0:T(8,128)(2,1)S(1)}, bf16[128,2048]{1,0:T(8,128)(2,1)}, bf16[128,2048]{1,0:T(8,128)(2,1)}, bf16[128,2048]{1,0:T(8,128)(2,1)}) custom-call(s32[3]{0:T(128)S(1)} %pad_add_fusion.1.pos_ref, bf16[128,8192]{1,0:T(8,128)(2,1)} %bitcast.34, f32[1,8192]{1,0:T(1,128)S(1)} %bitcast.32), custom_call_target="tpu_custom_call" | custom-call | flops 4194304 | bytes 4194304 | tf_op jit(solution)/shard_map/norm/pallas_call | solution.py:80
  7.7 0.8 copy-done.2
  8.5 1.5 %collective-permute-start.6 = (bf16[128,2048]{1,0:T(8,128)(2,1)}, bf16[128,2048]{1,0:T(8,128)(2,1)}, u32[]{:S(2)}, u32[]{:S(2)}) collective-permute-start(bf16[128,2048]{1,0:T(8,128)(2,1)} %get-tuple-element.27), channel_id=1, source_target_pairs={{0,2},{1,3},{2,4},{3,5},{4,6},{5,7},{6,0},{7,1},{8,10},{9,11},{10,... | collective-permute-start | bytes 1572872 | tf_op jit(solution)/shard_map/ppermute | solution.py:325
  10.0 1.7 %collective-permute-start.7 = (bf16[128,2048]{1,0:T(8,128)(2,1)}, bf16[128,2048]{1,0:T(8,128)(2,1)}, u32[]{:S(2)}, u32[]{:S(2)}) collective-permute-start(bf16[128,2048]{1,0:T(8,128)(2,1)} %get-tuple-element.28), channel_id=1, source_target_pairs={{0,6},{1,7},{2,0},{3,1},{4,2},{5,3},{6,4},{7,5},{8,14},{9,15},{10,... | collective-permute-start | bytes 1572872 | tf_op jit(solution)/shard_map/ppermute | solution.py:326
  11.7 1.8 %collective-permute-start.8 = (bf16[128,2048]{1,0:T(8,128)(2,1)}, bf16[128,2048]{1,0:T(8,128)(2,1)}, u32[]{:S(2)}, u32[]{:S(2)}) collective-permute-start(bf16[128,2048]{1,0:T(8,128)(2,1)} %get-tuple-element.29), channel_id=1, source_target_pairs={{0,4},{1,5},{2,6},{3,7},{4,0},{5,1},{6,2},{7,3},{8,12},{9,13},{10,... | collective-permute-start | bytes 1572872 | tf_op jit(solution)/shard_map/ppermute | solution.py:324
  13.6 0.6 gather_fusion
  14.2 12.2 %collective-permute-done.4.refs_3_.refs_5_ = bf16[512,1024]{1,0:T(8,128)(2,1)S(1)} collective-permute-done((bf16[512,1024]{1,0:T(8,128)(2,1)}, bf16[512,1024]{1,0:T(8,128)(2,1)S(1)}, u32[]{:S(2)}, u32[]{:S(2)}) %collective-permute-start.4) | collective-permute-done | bytes 1048608 | tf_op jit(solution)/shard_map/ppermute | solution.py:321
  26.4 0.1 copy.13
  26.6 0.6 gather_fusion.1
  27.2 0.1 copy.14
  27.3 1.3 %constant_dynamic-slice_fusion = (bf16[1,128,1024]{2,1,0:T(8,128)(2,1)S(1)}, bf16[128,1024]{1,0:T(8,128)(2,1)S(1)}, bf16[128,1024]{1,0:T(8,128)(2,1)S(1)}, bf16[128,1024]{1,0:T(8,128)(2,1)S(1)}) fusion(bf16[1,128,4096]{2,1,0:T(8,128)(2,1)} %param.7, s32[]{:T(128)S(6)} %select_n.68, s32[]{:T(128)S(6)} %select_n.69, s32[]{:T(128)S(6)} %select_n.71, ...), kind=kLoop, calls=%fused_computation.29 | loop fusion | bytes 2097168 | tf_op jit(solution)/shard_map/dynamic_slice | solution.py:331
  28.6 0.3 fusion
  28.9 0.2 collective-permute-start
  29.1 5.8 %collective-permute-done.7.refs_1_ = bf16[128,2048]{1,0:T(8,128)(2,1)} collective-permute-done((bf16[128,2048]{1,0:T(8,128)(2,1)}, bf16[128,2048]{1,0:T(8,128)(2,1)}, u32[]{:S(2)}, u32[]{:S(2)}) %collective-permute-start.7) | collective-permute-done | bytes 524320 | tf_op jit(solution)/shard_map/ppermute | solution.py:326
  34.9 1.7 %collective-permute-done.8.refs_2_ = bf16[128,2048]{1,0:T(8,128)(2,1)} collective-permute-done((bf16[128,2048]{1,0:T(8,128)(2,1)}, bf16[128,2048]{1,0:T(8,128)(2,1)}, u32[]{:S(2)}, u32[]{:S(2)}) %collective-permute-start.8) | collective-permute-done | bytes 524320 | tf_op jit(solution)/shard_map/ppermute | solution.py:324
  36.6 3.5 %products.1 = (bf16[128,1024]{1,0:T(8,128)(2,1)S(1)}, bf16[128,1024]{1,0:T(8,128)(2,1)S(1)}, bf16[128,1024]{1,0:T(8,128)(2,1)S(1)}) custom-call(bf16[128,2048]{1,0:T(8,128)(2,1)} %collective-permute-done.6.refs_0_, bf16[128,2048]{1,0:T(8,128)(2,1)} %collective-permute-done.7.refs_1_, bf16[128,2048]{1,0:T(8,128)(2,1)} %collective-permute-done.8.refs_2_, ...), custom_call_target="tpu_custom_call" | custom-call | flops 1610612736 | bytes 4194304 | tf_op jit(solution)/shard_map/products/pallas_call | solution.py:111
  40.1 2.1 %collective-permute-start.9 = (bf16[128,1024]{1,0:T(8,128)(2,1)S(1)}, bf16[128,1024]{1,0:T(8,128)(2,1)S(1)}, u32[]{:S(2)}, u32[]{:S(2)}) collective-permute-start(bf16[128,1024]{1,0:T(8,128)(2,1)S(1)} %get-tuple-element.30), channel_id=1, source_target_pairs={{0,6},{1,7},{2,0},{3,1},{4,2},{5,3},{6,4},{7,5},{8,14},{9,15},{10,... | collective-permute-start | bytes 786440 | tf_op jit(solution)/shard_map/ppermute | solution.py:337
  42.3 1.6 %collective-permute-start.11 = (bf16[128,1024]{1,0:T(8,128)(2,1)S(1)}, bf16[128,1024]{1,0:T(8,128)(2,1)S(1)}, u32[]{:S(2)}, u32[]{:S(2)}) collective-permute-start(bf16[128,1024]{1,0:T(8,128)(2,1)S(1)} %get-tuple-element.32), channel_id=1, source_target_pairs={{0,4},{1,5},{2,6},{3,7},{4,0},{5,1},{6,2},{7,3},{8,12},{9,13},{10,... | collective-permute-start | bytes 786440 | tf_op jit(solution)/shard_map/ppermute | solution.py:337
  43.8 0.1 compare_and_fusion.1
  43.9 0.1 pad_maximum_fusion.1
  44.0 1.9 %own_product.1.own_ref = f32[128,1024]{1,0:T(8,128)S(1)} custom-call(bf16[128,2048]{1,0:T(8,128)(2,1)S(1)} %copy-done.3, bf16[512,1024]{1,0:T(8,128)(2,1)S(1)} %copy-done.1, bf16[512,1024]{1,0:T(8,128)(2,1)S(1)} %collective-permute-done.3.refs_2_.refs_4_, bf16[512,1024]{1,0:T(8,128)(2,1)S(1)} %collective-permute-done.4.refs_3_.refs_5_, ...), custom_call_target="tpu_custom_call" | custom-call | flops 536870912 | bytes 4194304 | tf_op jit(solution)/shard_map/own_product/pallas_call | solution.py:111
  46.0 3.4 %collective-permute-done.9.r1_ref = bf16[128,1024]{1,0:T(8,128)(2,1)S(1)} collective-permute-done((bf16[128,1024]{1,0:T(8,128)(2,1)S(1)}, bf16[128,1024]{1,0:T(8,128)(2,1)S(1)}, u32[]{:S(2)}, u32[]{:S(2)}) %collective-permute-start.9) | collective-permute-done | bytes 262176 | tf_op jit(solution)/shard_map/ppermute | solution.py:337
  49.4 3.9 %collective-permute-start.1 = (bf16[128,1024]{1,0:T(8,128)(2,1)S(1)}, bf16[128,1024]{1,0:T(8,128)(2,1)S(1)}, u32[]{:S(2)}, u32[]{:S(2)}) collective-permute-start(bf16[128,1024]{1,0:T(8,128)(2,1)S(1)} %get-tuple-element.54), channel_id=1, source_target_pairs={{0,128},{16,144},{32,160},{48,176},{64,192},{80,208},{96,224},{112... | collective-permute-start | bytes 786440 | tf_op jit(solution)/shard_map/ppermute | solution.py:332
  53.3 2.8 %collective-permute-done.10.r2_ref = bf16[128,1024]{1,0:T(8,128)(2,1)S(1)} collective-permute-done((bf16[128,1024]{1,0:T(8,128)(2,1)S(1)}, bf16[128,1024]{1,0:T(8,128)(2,1)S(1)}, u32[]{:S(2)}, u32[]{:S(2)}) %collective-permute-start.10) | collective-permute-done | bytes 262176 | tf_op jit(solution)/shard_map/ppermute | solution.py:337
  56.1 0.4 keys_values.1
  56.5 0.2 collective-permute-start.12
  56.7 0.3 collective-permute-start.13
  57.0 3.8 %collective-permute-done.12 = bf16[128,256]{1,0:T(8,128)(2,1)S(1)} collective-permute-done((bf16[128,256]{1,0:T(8,128)(2,1)S(1)}, bf16[128,256]{1,0:T(8,128)(2,1)S(1)}, u32[]{:S(2)}, u32[]{:S(2)}) %collective-permute-start.12) | collective-permute-done | bytes 65568 | tf_op jit(solution)/shard_map/ppermute | solution.py:342
  60.8 0.9 collective-permute-done.13
  61.7 4.3 %collective-permute-done.14 = bf16[128,256]{1,0:T(8,128)(2,1)S(1)} collective-permute-done((bf16[128,256]{1,0:T(8,128)(2,1)S(1)}, bf16[128,256]{1,0:T(8,128)(2,1)S(1)}, u32[]{:S(2)}, u32[]{:S(2)}) %collective-permute-start.14) | collective-permute-done | bytes 65568 | tf_op jit(solution)/shard_map/ppermute | solution.py:342
  66.0 8.3 %collective-permute-start.17 = (bf16[512,256]{1,0:T(8,128)(2,1)S(1)}, bf16[512,256]{1,0:T(8,128)(2,1)S(1)}, u32[]{:S(2)}, u32[]{:S(2)}) collective-permute-start(bf16[512,256]{1,0:T(8,128)(2,1)S(1)} %constant_dynamic-update-slice_fusion.kv_ref), channel_id=1, source_target_pairs={{0,96},{16,112},{32,0},{48,16},{64,32},{80,48},{96,64},{112,80},{1... | collective-permute-start | bytes 786440 | tf_op jit(solution)/shard_map/ppermute | solution.py:345
  74.4 0.1 pad_maximum_fusion.q_ref.refs_1_
  74.6 3.3 %attend_first.1 = (f32[4,1024,128]{2,1,0:T(8,128)S(1)}, f32[4,1024,256]{2,1,0:T(8,128)S(1)}) custom-call(s32[4,16]{1,0:T(4,128)S(1)} %select_select_fusion.flag_ref.refs_0_, bf16[4,128,1024]{2,1,0:T(8,128)(2,1)S(1)} %pad_maximum_fusion.q_ref.refs_1_, bf16[512,256]{1,0:T(8,128)(2,1)S(1)} %constant_dynamic-update-slice_fusion.kv_ref), custom_call_target="tpu_custom_call" | custom-call | flops 1073741824 | bytes 4194304 | tf_op jit(solution)/shard_map/attend_first/pallas_call | solution.py:269
  77.9 1.8 %collective-permute-done.17.down_ref = bf16[512,256]{1,0:T(8,128)(2,1)S(1)} collective-permute-done((bf16[512,256]{1,0:T(8,128)(2,1)S(1)}, bf16[512,256]{1,0:T(8,128)(2,1)S(1)}, u32[]{:S(2)}, u32[]{:S(2)}) %collective-permute-start.17) | collective-permute-done | bytes 262176 | tf_op jit(solution)/shard_map/ppermute | solution.py:345
  79.7 4.7 %collective-permute-start.18 = (bf16[256,256]{1,0:T(8,128)(2,1)S(1)}, bf16[256,256]{1,0:T(8,128)(2,1)S(1)}, u32[]{:S(2)}, u32[]{:S(2)}) collective-permute-start(bf16[256,256]{1,0:T(8,128)(2,1)S(1)} %slice.13), channel_id=1, source_target_pairs={{0,96},{16,112},{32,0},{48,16},{64,32},{80,48},{96,64},{112,80},{1... | collective-permute-start | bytes 393224 | tf_op jit(solution)/shard_map/ppermute | solution.py:347
  84.4 4.1 %collective-permute-done.15.up_ref = bf16[512,256]{1,0:T(8,128)(2,1)S(1)} collective-permute-done((bf16[512,256]{1,0:T(8,128)(2,1)S(1)}, bf16[512,256]{1,0:T(8,128)(2,1)S(1)}, u32[]{:S(2)}, u32[]{:S(2)}) %collective-permute-start.15) | collective-permute-done | bytes 262176 | tf_op jit(solution)/shard_map/ppermute | solution.py:344
  88.4 0.3 collective-permute-start.16
  88.8 3.0 %attend_more.1 = (f32[4,1024,128]{2,1,0:T(8,128)S(1)}, f32[4,1024,256]{2,1,0:T(8,128)S(1)}) custom-call(s32[4,16]{1,0:T(4,128)S(1)} %select_select_fusion.flag_ref.refs_0_, bf16[4,128,1024]{2,1,0:T(8,128)(2,1)S(1)} %pad_maximum_fusion.q_ref.refs_1_, ...), custom_call_target="tpu_custom_call", output_to_operand_aliasing={{0}: (4, {}), {1}: (5, {})} | custom-call | flops 3221225472 | bytes 4194304 | tf_op jit(solution)/shard_map/attend_more/pallas_call | solution.py:269
  91.7 5.6 %collective-permute-done.16.refs_2_ = bf16[256,256]{1,0:T(8,128)(2,1)S(1)} collective-permute-done((bf16[256,256]{1,0:T(8,128)(2,1)S(1)}, bf16[256,256]{1,0:T(8,128)(2,1)S(1)}, u32[]{:S(2)}, u32[]{:S(2)}) %collective-permute-start.16) | collective-permute-done | bytes 131104 | tf_op jit(solution)/shard_map/ppermute | solution.py:346
  97.3 1.9 %attend_others.1 = (f32[4,1024,128]{2,1,0:T(8,128)S(1)}, f32[4,1024,256]{2,1,0:T(8,128)S(1)}, bf16[128,1024]{1,0:T(8,128)(2,1)S(1)}, bf16[128,1024]{1,0:T(8,128)(2,1)S(1)}) custom-call(s32[4,16]{1,0:T(4,128)S(1)} %select_select_fusion.flag_ref.refs_0_, ...), custom_call_target="tpu_custom_call", output_to_operand_aliasing={{0}: (4, {}), {1}: (5, {})} | custom-call | flops 1073741824 | bytes 4194304 | tf_op jit(solution)/shard_map/attend_others/pallas_call | solution.py:269
  99.2 1.0 attend_own.1
  100.2 0.4 collective-permute-start.19
  100.6 3.2 %collective-permute-start.21 = (bf16[128,1024]{1,0:T(8,128)(2,1)S(1)}, bf16[128,1024]{1,0:T(8,128)(2,1)S(1)}, u32[]{:S(2)}, u32[]{:S(2)}) collective-permute-start(bf16[128,1024]{1,0:T(8,128)(2,1)S(1)} %get-tuple-element.46), channel_id=1, source_target_pairs={{0,144},{16,128},{32,176},{48,160},{64,208},{80,192},{96,240},{112... | collective-permute-start | bytes 786440 | tf_op jit(solution)/shard_map/ppermute | solution.py:377
  103.8 2.9 %collective-permute-done.19.refs_1_ = bf16[128,1024]{1,0:T(8,128)(2,1)S(1)} collective-permute-done((bf16[128,1024]{1,0:T(8,128)(2,1)S(1)}, bf16[128,1024]{1,0:T(8,128)(2,1)S(1)}, u32[]{:S(2)}, u32[]{:S(2)}) %collective-permute-start.19) | collective-permute-done | bytes 262176 | tf_op jit(solution)/shard_map/ppermute | solution.py:377
  106.7 3.1 %collective-permute-done.20.refs_2_ = bf16[128,1024]{1,0:T(8,128)(2,1)S(1)} collective-permute-done((bf16[128,1024]{1,0:T(8,128)(2,1)S(1)}, bf16[128,1024]{1,0:T(8,128)(2,1)S(1)}, u32[]{:S(2)}, u32[]{:S(2)}) %collective-permute-start.20) | collective-permute-done | bytes 262176 | tf_op jit(solution)/shard_map/ppermute | solution.py:377
  109.8 1.0 place.1
  (45 shorter events, 0.5 us)
Async XLA Ops:
  0.0 13.6 %copy-start = (s32[1,16,16]{2,1,0:T(8,128)S(1)}, s32[1,16,16]{2,1,0:T(8,128)}, u32[]{:S(2)}) copy-start(s32[1,16,16]{2,1,0:T(8,128)} %param.11) | copy-start | bytes 3076
  0.0 26.4 %collective-permute-start.4 = (bf16[512,1024]{1,0:T(8,128)(2,1)}, bf16[512,1024]{1,0:T(8,128)(2,1)S(1)}, u32[]{:S(2)}, u32[]{:S(2)}) collective-permute-start(bf16[512,1024]{1,0:T(8,128)(2,1)} %refs_3_.1), channel_id=1, source_target_pairs={{0,136},{1,137},{2,138},{3,139},{4,140},{5,141},{6,142},{7,143},{8... | collective-permute-start | bytes 3145736 | tf_op jit(solution)/shard_map/ppermute | solution.py:321
  3.0 33.6 %collective-permute-start.3 = (bf16[512,1024]{1,0:T(8,128)(2,1)}, bf16[512,1024]{1,0:T(8,128)(2,1)S(1)}, u32[]{:S(2)}, u32[]{:S(2)}) collective-permute-start(bf16[512,1024]{1,0:T(8,128)(2,1)} %refs_3_.1), channel_id=1, source_target_pairs={{0,1},{1,0},{2,3},{3,2},{4,5},{5,4},{6,7},{7,6},{8,9},{9,8},{10,11... | collective-permute-start | bytes 3145736 | tf_op jit(solution)/shard_map/ppermute | solution.py:320
  3.1 0.8 copy-start.4
  3.9 32.7 %copy-start.1 = (bf16[512,1024]{1,0:T(8,128)(2,1)S(1)}, bf16[512,1024]{1,0:T(8,128)(2,1)}, u32[]{:S(2)}) copy-start(bf16[512,1024]{1,0:T(8,128)(2,1)} %refs_3_.1) | copy-start | bytes 3145732
  7.7 0.8 copy-start.2
  8.5 20.4 %collective-permute-start.6 = (bf16[128,2048]{1,0:T(8,128)(2,1)}, bf16[128,2048]{1,0:T(8,128)(2,1)}, u32[]{:S(2)}, u32[]{:S(2)}) collective-permute-start(bf16[128,2048]{1,0:T(8,128)(2,1)} %get-tuple-element.27), channel_id=1, source_target_pairs={{0,2},{1,3},{2,4},{3,5},{4,6},{5,7},{6,0},{7,1},{8,10},{9,11},{10,... | collective-permute-start | bytes 1572872 | tf_op jit(solution)/shard_map/ppermute | solution.py:325
  10.0 24.9 %collective-permute-start.7 = (bf16[128,2048]{1,0:T(8,128)(2,1)}, bf16[128,2048]{1,0:T(8,128)(2,1)}, u32[]{:S(2)}, u32[]{:S(2)}) collective-permute-start(bf16[128,2048]{1,0:T(8,128)(2,1)} %get-tuple-element.28), channel_id=1, source_target_pairs={{0,6},{1,7},{2,0},{3,1},{4,2},{5,3},{6,4},{7,5},{8,14},{9,15},{10,... | collective-permute-start | bytes 1572872 | tf_op jit(solution)/shard_map/ppermute | solution.py:326
  11.7 24.8 %collective-permute-start.8 = (bf16[128,2048]{1,0:T(8,128)(2,1)}, bf16[128,2048]{1,0:T(8,128)(2,1)}, u32[]{:S(2)}, u32[]{:S(2)}) collective-permute-start(bf16[128,2048]{1,0:T(8,128)(2,1)} %get-tuple-element.29), channel_id=1, source_target_pairs={{0,4},{1,5},{2,6},{3,7},{4,0},{5,1},{6,2},{7,3},{8,12},{9,13},{10,... | collective-permute-start | bytes 1572872 | tf_op jit(solution)/shard_map/ppermute | solution.py:324
  26.4 10.2 %collective-permute-start.5 = (bf16[512,1024]{1,0:T(8,128)(2,1)S(1)}, bf16[512,1024]{1,0:T(8,128)(2,1)}, u32[]{:S(2)}, u32[]{:S(2)}) collective-permute-start(bf16[512,1024]{1,0:T(8,128)(2,1)S(1)} %collective-permute-done.4.refs_3_.refs_5_), channel_id=1, source_target_pairs={{0,1},{1,0},{2,3},{3,2},{4,5},{5,4},{6,7},{7,6},{8,9},{9,8},{10,11... | collective-permute-start | bytes 3145736 | tf_op jit(solution)/shard_map/ppermute | solution.py:327
  28.9 45.5 %collective-permute-start = (bf16[128,1024]{1,0:T(8,128)(2,1)S(1)}, bf16[128,1024]{1,0:T(8,128)(2,1)S(1)}, u32[]{:S(2)}, u32[]{:S(2)}) collective-permute-start(bf16[128,1024]{1,0:T(8,128)(2,1)S(1)} %get-tuple-element.52), channel_id=1, source_target_pairs={{0,16},{16,0},{32,48},{48,32},{64,80},{80,64},{96,112},{112,96},{1... | collective-permute-start | bytes 786440 | tf_op jit(solution)/shard_map/ppermute | solution.py:332
  34.9 9.1 %copy-start.3 = (bf16[128,2048]{1,0:T(8,128)(2,1)S(1)}, bf16[128,2048]{1,0:T(8,128)(2,1)}, u32[]{:S(2)}) copy-start(bf16[128,2048]{1,0:T(8,128)(2,1)} %copy-done.2) | copy-start | bytes 1572868
  34.9 39.5 %collective-permute-start.2 = (bf16[128,1024]{1,0:T(8,128)(2,1)S(1)}, bf16[128,1024]{1,0:T(8,128)(2,1)S(1)}, u32[]{:S(2)}, u32[]{:S(2)}) collective-permute-start(bf16[128,1024]{1,0:T(8,128)(2,1)S(1)} %get-tuple-element.53), channel_id=1, source_target_pairs={{0,144},{16,128},{32,176},{48,160},{64,208},{80,192},{96,240},{112... | collective-permute-start | bytes 786440 | tf_op jit(solution)/shard_map/ppermute | solution.py:332
  40.1 9.3 %collective-permute-start.9 = (bf16[128,1024]{1,0:T(8,128)(2,1)S(1)}, bf16[128,1024]{1,0:T(8,128)(2,1)S(1)}, u32[]{:S(2)}, u32[]{:S(2)}) collective-permute-start(bf16[128,1024]{1,0:T(8,128)(2,1)S(1)} %get-tuple-element.30), channel_id=1, source_target_pairs={{0,6},{1,7},{2,0},{3,1},{4,2},{5,3},{6,4},{7,5},{8,14},{9,15},{10,... | collective-permute-start | bytes 786440 | tf_op jit(solution)/shard_map/ppermute | solution.py:337
  42.3 13.9 %collective-permute-start.10 = (bf16[128,1024]{1,0:T(8,128)(2,1)S(1)}, bf16[128,1024]{1,0:T(8,128)(2,1)S(1)}, u32[]{:S(2)}, u32[]{:S(2)}) collective-permute-start(bf16[128,1024]{1,0:T(8,128)(2,1)S(1)} %get-tuple-element.31), channel_id=1, source_target_pairs={{0,2},{1,3},{2,4},{3,5},{4,6},{5,7},{6,0},{7,1},{8,10},{9,11},{10,... | collective-permute-start | bytes 786440 | tf_op jit(solution)/shard_map/ppermute | solution.py:337
  42.3 13.9 %collective-permute-start.11 = (bf16[128,1024]{1,0:T(8,128)(2,1)S(1)}, bf16[128,1024]{1,0:T(8,128)(2,1)S(1)}, u32[]{:S(2)}, u32[]{:S(2)}) collective-permute-start(bf16[128,1024]{1,0:T(8,128)(2,1)S(1)} %get-tuple-element.32), channel_id=1, source_target_pairs={{0,4},{1,5},{2,6},{3,7},{4,0},{5,1},{6,2},{7,3},{8,12},{9,13},{10,... | collective-permute-start | bytes 786440 | tf_op jit(solution)/shard_map/ppermute | solution.py:337
  44.0 12.1 %copy-start.5 = (f32[1024]{0:T(1024)S(1)}, f32[1024]{0:T(1024)}, u32[]{:S(2)}) copy-start(f32[1024]{0:T(1024)} %param.9) | copy-start | bytes 12292
  49.4 25.0 %collective-permute-start.1 = (bf16[128,1024]{1,0:T(8,128)(2,1)S(1)}, bf16[128,1024]{1,0:T(8,128)(2,1)S(1)}, u32[]{:S(2)}, u32[]{:S(2)}) collective-permute-start(bf16[128,1024]{1,0:T(8,128)(2,1)S(1)} %get-tuple-element.54), channel_id=1, source_target_pairs={{0,128},{16,144},{32,160},{48,176},{64,192},{80,208},{96,224},{112... | collective-permute-start | bytes 786440 | tf_op jit(solution)/shard_map/ppermute | solution.py:332
  56.5 4.4 %collective-permute-start.12 = (bf16[128,256]{1,0:T(8,128)(2,1)S(1)}, bf16[128,256]{1,0:T(8,128)(2,1)S(1)}, u32[]{:S(2)}, u32[]{:S(2)}) collective-permute-start(bf16[128,256]{1,0:T(8,128)(2,1)S(1)} %get-tuple-element.34), channel_id=1, source_target_pairs={{0,16},{16,0},{32,48},{48,32},{64,80},{80,64},{96,112},{112,96},{1... | collective-permute-start | bytes 196616 | tf_op jit(solution)/shard_map/ppermute | solution.py:342
  56.7 5.0 %collective-permute-start.13 = (bf16[128,256]{1,0:T(8,128)(2,1)S(1)}, bf16[128,256]{1,0:T(8,128)(2,1)S(1)}, u32[]{:S(2)}, u32[]{:S(2)}) collective-permute-start(bf16[128,256]{1,0:T(8,128)(2,1)S(1)} %get-tuple-element.35), channel_id=1, source_target_pairs={{0,128},{16,144},{32,160},{48,176},{64,192},{80,208},{96,224},{112... | collective-permute-start | bytes 196616 | tf_op jit(solution)/shard_map/ppermute | solution.py:342
  60.8 5.2 %collective-permute-start.14 = (bf16[128,256]{1,0:T(8,128)(2,1)S(1)}, bf16[128,256]{1,0:T(8,128)(2,1)S(1)}, u32[]{:S(2)}, u32[]{:S(2)}) collective-permute-start(bf16[128,256]{1,0:T(8,128)(2,1)S(1)} %get-tuple-element.36), channel_id=1, source_target_pairs={{0,144},{16,128},{32,176},{48,160},{64,208},{80,192},{96,240},{112... | collective-permute-start | bytes 196616 | tf_op jit(solution)/shard_map/ppermute | solution.py:342
  66.0 13.7 %collective-permute-start.17 = (bf16[512,256]{1,0:T(8,128)(2,1)S(1)}, bf16[512,256]{1,0:T(8,128)(2,1)S(1)}, u32[]{:S(2)}, u32[]{:S(2)}) collective-permute-start(bf16[512,256]{1,0:T(8,128)(2,1)S(1)} %constant_dynamic-update-slice_fusion.kv_ref), channel_id=1, source_target_pairs={{0,96},{16,112},{32,0},{48,16},{64,32},{80,48},{96,64},{112,80},{1... | collective-permute-start | bytes 786440 | tf_op jit(solution)/shard_map/ppermute | solution.py:345
  74.3 14.1 %collective-permute-start.15 = (bf16[512,256]{1,0:T(8,128)(2,1)S(1)}, bf16[512,256]{1,0:T(8,128)(2,1)S(1)}, u32[]{:S(2)}, u32[]{:S(2)}) collective-permute-start(bf16[512,256]{1,0:T(8,128)(2,1)S(1)} %constant_dynamic-update-slice_fusion.kv_ref), channel_id=1, source_target_pairs={{0,32},{16,48},{32,64},{48,80},{64,96},{80,112},{96,0},{112,16},{1... | collective-permute-start | bytes 786440 | tf_op jit(solution)/shard_map/ppermute | solution.py:344
  79.7 12.0 %collective-permute-start.18 = (bf16[256,256]{1,0:T(8,128)(2,1)S(1)}, bf16[256,256]{1,0:T(8,128)(2,1)S(1)}, u32[]{:S(2)}, u32[]{:S(2)}) collective-permute-start(bf16[256,256]{1,0:T(8,128)(2,1)S(1)} %slice.13), channel_id=1, source_target_pairs={{0,96},{16,112},{32,0},{48,16},{64,32},{80,48},{96,64},{112,80},{1... | collective-permute-start | bytes 393224 | tf_op jit(solution)/shard_map/ppermute | solution.py:347
  88.4 8.9 %collective-permute-start.16 = (bf16[256,256]{1,0:T(8,128)(2,1)S(1)}, bf16[256,256]{1,0:T(8,128)(2,1)S(1)}, u32[]{:S(2)}, u32[]{:S(2)}) collective-permute-start(bf16[256,256]{1,0:T(8,128)(2,1)S(1)} %slice.12), channel_id=1, source_target_pairs={{0,32},{16,48},{32,64},{48,80},{64,96},{80,112},{96,0},{112,16},{1... | collective-permute-start | bytes 393224 | tf_op jit(solution)/shard_map/ppermute | solution.py:346
  100.2 6.5 %collective-permute-start.19 = (bf16[128,1024]{1,0:T(8,128)(2,1)S(1)}, bf16[128,1024]{1,0:T(8,128)(2,1)S(1)}, u32[]{:S(2)}, u32[]{:S(2)}) collective-permute-start(bf16[128,1024]{1,0:T(8,128)(2,1)S(1)} %get-tuple-element.44), channel_id=1, source_target_pairs={{0,16},{16,0},{32,48},{48,32},{64,80},{80,64},{96,112},{112,96},{1... | collective-permute-start | bytes 786440 | tf_op jit(solution)/shard_map/ppermute | solution.py:377
  100.6 9.2 %collective-permute-start.20 = (bf16[128,1024]{1,0:T(8,128)(2,1)S(1)}, bf16[128,1024]{1,0:T(8,128)(2,1)S(1)}, u32[]{:S(2)}, u32[]{:S(2)}) collective-permute-start(bf16[128,1024]{1,0:T(8,128)(2,1)S(1)} %get-tuple-element.45), channel_id=1, source_target_pairs={{0,128},{16,144},{32,160},{48,176},{64,192},{80,208},{96,224},{112... | collective-permute-start | bytes 786440 | tf_op jit(solution)/shard_map/ppermute | solution.py:377
  100.6 9.2 %collective-permute-start.21 = (bf16[128,1024]{1,0:T(8,128)(2,1)S(1)}, bf16[128,1024]{1,0:T(8,128)(2,1)S(1)}, u32[]{:S(2)}, u32[]{:S(2)}) collective-permute-start(bf16[128,1024]{1,0:T(8,128)(2,1)S(1)} %get-tuple-element.46), channel_id=1, source_target_pairs={{0,144},{16,128},{32,176},{48,160},{64,208},{80,192},{96,240},{112... | collective-permute-start | bytes 786440 | tf_op jit(solution)/shard_map/ppermute | solution.py:377

commit v4 on v3

--- a/solution.py
+++ b/solution.py
@@ -36,9 +36,13 @@
     return [(c, (c & 8) | ((c + k) & 7)) for c in range(16)]
 
 
-def norm_kernel(pos_ref, x_hbm, gain_hbm, *refs):
-    outs, (x_ref, gain_ref, sems) = refs[:4], refs[4:]
-    xi, yhi, core = pos_ref[0], pos_ref[1], pos_ref[2]
+def part_column(pos_ref, k, i):
+    a, b = i >> 1, i & 1
+    src = (pos_ref[1] ^ a) * 4096 + ((pos_ref[0] + k) & 3) * 1024 + (pos_ref[2] ^ b) * 512
+    return pl.multiple_of(src, 512)
+
+
+def norm_kernel(pos_ref, x_hbm, gain_hbm, out0, out1, out2, out3, x_ref, gain_ref, sems):
     step = 32
     count = x_ref.shape[0] // step
     copies = [
@@ -63,14 +67,11 @@
             part = part * part
             total = part if total is None else total + part
         inv = lax.rsqrt(jnp.sum(total, axis=-1, keepdims=True) / D + 1e-06)
-        for k in (2, 1, 3, 0):
-            for a in range(2):
-                for b in range(2):
-                    src = (yhi ^ a) * 4096 + ((xi + k) & 3) * 1024 + (core ^ b) * 512
-                    cols = pl.ds(pl.multiple_of(src, 512), 512)
-                    wide = x_ref[rows, cols].astype(F32)
-                    dst = (a * 2 + b) * 512
-                    outs[k][rows, dst : dst + 512] = (wide * inv * gain_ref[:, cols]).astype(BF)
+        for k, out in ((2, out2), (1, out1), (3, out3), (0, out0)):
+            for i in range(4):
+                cols = pl.ds(part_column(pos_ref, k, i), 512)
+                wide = x_ref[rows, cols].astype(F32)
+                out[rows, i * 512 : (i + 1) * 512] = (wide * inv * gain_ref[:, cols]).astype(BF)
 
 
 def norm_call(pos, hidden, gain):
@@ -94,15 +95,13 @@
 
 
 def product_kernel(count, *refs):
-    rows, weights, outs = refs[:count], refs[count : -count], refs[-count:]
+    rows, weights, outs = refs[:count], refs[count:-count], refs[-count:]
     tokens = rows[0].shape[0]
-    for n in range(4):
-        cols = slice(n * 256, (n + 1) * 256)
-        left = jnp.concatenate([r[...] for r in rows], axis=0)
-        right = jnp.concatenate([w[:, cols] for w in weights], axis=0)
-        total = jnp.dot(left, right, preferred_element_type=F32)
-        for i in range(count):
-            outs[i][:, cols] = total[i * tokens : (i + 1) * tokens].astype(outs[i].dtype)
+    left = jnp.concatenate([r[...] for r in rows], axis=0)
+    right = jnp.concatenate([w[...] for w in weights], axis=0)
+    total = jnp.dot(left, right, preferred_element_type=F32)
+    for i in range(count):
+        outs[i][...] = total[i * tokens : (i + 1) * tokens].astype(outs[i].dtype)
 
 
 def product_call(rows, weights, dtype, name):
@@ -121,12 +120,12 @@
     )(*rows, *weights)
 
 
-def kv_kernel(j_ref, own_ref, r1_ref, r2_ref, r3_ref, bias_ref, cos_ref, sin_ref, *outs):
+def kv_kernel(j_ref, own_ref, r1_ref, r3_ref, r2_ref, bias_ref, cos_ref, sin_ref, *outs):
     j = j_ref[0]
 
     def part(col):
         cols = pl.ds(pl.multiple_of(col, 128), 128)
-        back = r1_ref[:, cols].astype(F32) + r2_ref[:, cols].astype(F32) + r3_ref[:, cols].astype(F32)
+        back = r1_ref[:, cols].astype(F32) + r3_ref[:, cols].astype(F32) + r2_ref[:, cols].astype(F32)
         return own_ref[:, cols] + back + bias_ref[:, cols]
 
     for k in range(4):
@@ -137,7 +136,7 @@
         outs[k][:, HD:] = part(KVH * HD + head * HD).astype(BF)
 
 
-def kv_call(j, own, r1, r2, r3, bias, cos, sin):
+def kv_call(j, own, r1, r3, r2, bias, cos, sin):
     vm = pl.BlockSpec(memory_space=pltpu.VMEM)
     return pl.pallas_call(
         kv_kernel,
@@ -147,7 +146,7 @@
         compiler_params=pltpu.CompilerParams(vmem_limit_bytes=8 * 1024 * 1024),
         cost_estimate=pl.CostEstimate(flops=1 << 20, bytes_accessed=2 << 20, transcendentals=0),
         name="keys_values",
-    )(j, own, r1, r2, r3, bias, cos, sin)
+    )(j, own, r1, r3, r2, bias, cos, sin)
 
 
 def visit(pair, q_ref, pieces, reach, top, acc, fresh=False):
@@ -306,6 +305,10 @@
     return jnp.concatenate([cosine, cosine], 1), jnp.concatenate([-sine, sine], 1)
 
 
+def after(value, earlier):
+    return lax.optimization_barrier((value, earlier))[0]
+
+
 def on_device(hidden_in, queries, kv_weight, kv_bias, norm_gain, block_mask):
     f = lax.axis_index("fsdp")
     c = lax.axis_index("ctx")
@@ -317,25 +320,27 @@
     q = queries.reshape(BLK, H * HD)
     j1 = jnp.reshape(j, (1,))
 
-    w_core = lax.ppermute(kv_weight, "fsdp", CORE_PAIRS)
+    pos = jnp.stack([xi, yhi, core])
+    gain = norm_gain.reshape(1, D)
     w_y = lax.ppermute(kv_weight, ("ctx", "fsdp"), DIAG_PAIRS)
 
-    normed = norm_call(jnp.stack([xi, yhi, core]), hidden, norm_gain.reshape(1, D))
-    n2 = lax.ppermute(normed[2], "fsdp", x_pairs(2))
-    n1 = lax.ppermute(normed[1], "fsdp", x_pairs(1))
-    n3 = lax.ppermute(normed[3], "fsdp", x_pairs(3))
-    w_yc = lax.ppermute(w_y, "fsdp", CORE_PAIRS)
-
-    q_parts = []
-    for k in range(4):
-        piece = lax.dynamic_slice(q, (0, (j ^ k) * GW), (BLK, GW))
-        q_parts.append(piece if k == 0 else lax.ppermute(piece, "ctx", member_pairs(k)))
+    normed0, normed1, normed2, normed3 = norm_call(pos, hidden, gain)
+    n2 = lax.ppermute(normed2, "fsdp", x_pairs(2))
+    n1 = lax.ppermute(normed1, "fsdp", x_pairs(1))
+    n3 = lax.ppermute(normed3, "fsdp", x_pairs(3))
+    q_parts = [lax.dynamic_slice(q, (0, (j ^ k) * GW), (BLK, GW)) for k in range(4)]
+    q_parts[2] = lax.ppermute(after(q_parts[2], normed0), "ctx", member_pairs(2))
+    q_parts[3] = lax.ppermute(after(q_parts[3], q_parts[2]), "ctx", member_pairs(3))
+    w_core = lax.ppermute(after(kv_weight, q_parts[3]), "fsdp", CORE_PAIRS)
+    w_yc = lax.ppermute(after(w_y, q_parts[3]), "fsdp", CORE_PAIRS)
+    q_parts[1] = lax.ppermute(after(q_parts[1], w_core), "ctx", member_pairs(1))
     q4 = jnp.stack(q_parts)
 
     weights = [kv_weight, w_core, w_y, w_yc]
-    products = product_call([n1, n3, n2], weights, BF, "products")
-    back = [lax.ppermute(p, "fsdp", x_pairs(k)) for p, k in zip(products, (3, 1, 2))]
-    (own,) = product_call([normed[0]], weights, F32, "own_product")
+    p1, p3 = product_call([n1, n3], weights, BF, "products")
+    (p2,) = product_call([n2], weights, BF, "far_product")
+    back = [lax.ppermute(p, "fsdp", x_pairs(k)) for p, k in ((p1, 3), (p3, 1), (p2, 2))]
+    (own,) = product_call([normed0], weights, F32, "own_product")
 
     cos, sin = rotary_tables(c * BLK, BLK)
     kvs = kv_call(j1, own, back[0], back[1], back[2], kv_bias.reshape(1, -1), cos, sin)

time: 112 us -> 105 us (0.938)
  waiting for transfers between devices: 52.3 us -> 41.7 us
  starting transfers between devices: 33.2 us -> 34.9 us
  Pallas kernels: 19.9 us -> 21.4 us
    ppermute x1, waiting for transfers between devices: 12.2 us -> 1.25 us  [on_device(): w_y = lax.ppermute(kv_weight, ('ctx', 'fsdp'), DIAG_PAIRS)]
    ppermute x8, waiting for transfers between devices: 7.51 us -> 16.7 us  [the longest x1 7.25 us: on_device(): lax.ppermute(after(q_parts[3], q_parts[2]), 'ctx', member_pairs(3))]
    ppermute x3, waiting for transfers between devices: 8.99 us -> 2.51 us  [on_device(): lax.ppermute(kvs[k], 'ctx', member_pairs(k))]
    ppermute x8, starting transfers between devices: 9.14 us -> 5.4 us  [the longest x1 1.81 us: on_device(): n2 = lax.ppermute(normed2, 'fsdp', x_pairs(2))]
    ppermute x1, waiting for transfers between devices: 4.06 us -> 0.37 us  [on_device(): up = lax.ppermute(group, 'ctx', z_pairs(2))]
    ppermute x3, starting transfers between devices: 0.51 us -> 3.76 us  [on_device(): lax.ppermute(kvs[k], 'ctx', member_pairs(k))]
    ppermute x1, waiting for transfers between devices: 1.77 us -> 4.29 us  [on_device(): down = lax.ppermute(group, 'ctx', z_pairs(-2))]
    ppermute x3, waiting for transfers between devices: 6.25 us -> 4.22 us  [on_device(): lax.ppermute(p, 'fsdp', x_pairs(k))]
  transfers between devices with their start and end apart: 22 -> 22, of which waited for: 13 -> 14; matrix products, arithmetic and copies ran while one was open for 3% -> 4% of each run, Pallas kernels for 14% -> 17%
where the time goes in v4:
time: 105 us; the launch traced here: 104 us
  waiting for transfers between devices  41.7 us (40%)
  starting transfers between devices  34.9 us (33%)
  Pallas kernels  21.4 us (20%)
  local copies, waits for them, and re-layouts  3.81 us (4%)
  other arithmetic  1.95 us (2%)
    pallas_call x4, Pallas kernels, attend_call(): pl.pallas_call(kernel, in_specs=[pl.BlockSpec(memory_space=pltpu.SMEM)] +...  9.12 us
    ppermute x1, starting transfers between devices, on_device(): down = lax.ppermute(group, 'ctx', z_pairs(-2))  8.43 us
    ppermute x3, waiting for transfers between devices, on_device(): lax.ppermute(o, 'ctx', member_pairs(k))  7.62 us
    ppermute x1, waiting for transfers between devices, on_device(): lax.ppermute(after(q_parts[3], q_parts[2]), 'ctx', member_pairs(3))  7.25 us
    pallas_call x3, Pallas kernels, product_call(): pl.pallas_call(lambda *refs: product_kernel(count, *refs), in_specs=[vm]...  6.94 us
    ppermute x1, waiting for transfers between devices, on_device(): n3 = lax.ppermute(normed3, 'fsdp', x_pairs(3))  6.87 us
    ppermute x3, starting transfers between devices, on_device(): lax.ppermute(p, 'fsdp', x_pairs(k))  5.5 us
    ppermute x1, starting transfers between devices, on_device(): far1 = lax.ppermute(down[256:], 'ctx', z_pairs(-2))  4.72 us
  transfers between devices with their start and end apart: 22, of which 14 were waited for; matrix products, arithmetic and copies ran while one was open for 4% of the time, Pallas kernels for 17%

profile of v4, /device:TPU:32, one launch (start us, length us, event | category | flops | bytes accessed | tf_op | source)
XLA Modules:
  0.0 103.9 jit_solution(241110823395990468)
XLA Ops:
  0.0 3.0 %collective-permute-start.4 = (bf16[512,1024]{1,0:T(8,128)(2,1)}, bf16[512,1024]{1,0:T(8,128)(2,1)S(1)}, u32[]{:S(2)}, u32[]{:S(2)}) collective-permute-start(bf16[512,1024]{1,0:T(8,128)(2,1)} %refs_1_.3), channel_id=1, source_target_pairs={{0,136},{1,137},{2,138},{3,139},{4,140},{5,141},{6,142},{7,143},{8... | collective-permute-start | bytes 3145736 | tf_op jit(solution)/shard_map/ppermute | solution.py:325
  3.1 0.8 copy-done.4
  3.9 3.9 %norm.1 = (bf16[128,2048]{1,0:T(8,128)(2,1)S(1)}, bf16[128,2048]{1,0:T(8,128)(2,1)}, bf16[128,2048]{1,0:T(8,128)(2,1)}, bf16[128,2048]{1,0:T(8,128)(2,1)}) custom-call(s32[3]{0:T(128)S(1)} %pad_add_fusion.1.pos_ref, bf16[128,8192]{1,0:T(8,128)(2,1)} %bitcast.34, f32[1,8192]{1,0:T(1,128)S(1)} %bitcast.32), custom_call_target="tpu_custom_call" | custom-call | flops 4194304 | bytes 4194304 | tf_op jit(solution)/shard_map/norm/pallas_call | solution.py:81
  7.8 0.8 copy-done.2
  8.6 0.8 constant_dynamic-slice_fusion
  9.4 0.1 collective-permute-start
  9.5 1.5 %collective-permute-start.6 = (bf16[128,2048]{1,0:T(8,128)(2,1)}, bf16[128,2048]{1,0:T(8,128)(2,1)}, u32[]{:S(2)}, u32[]{:S(2)}) collective-permute-start(bf16[128,2048]{1,0:T(8,128)(2,1)} %get-tuple-element.36), channel_id=1, source_target_pairs={{0,2},{1,3},{2,4},{3,5},{4,6},{5,7},{6,0},{7,1},{8,10},{9,11},{10,... | collective-permute-start | bytes 1572872 | tf_op jit(solution)/shard_map/ppermute | solution.py:329
  11.0 1.8 %collective-permute-start.7 = (bf16[128,2048]{1,0:T(8,128)(2,1)}, bf16[128,2048]{1,0:T(8,128)(2,1)}, u32[]{:S(2)}, u32[]{:S(2)}) collective-permute-start(bf16[128,2048]{1,0:T(8,128)(2,1)} %get-tuple-element.37), channel_id=1, source_target_pairs={{0,6},{1,7},{2,0},{3,1},{4,2},{5,3},{6,4},{7,5},{8,14},{9,15},{10,... | collective-permute-start | bytes 1572872 | tf_op jit(solution)/shard_map/ppermute | solution.py:330
  12.8 1.8 %collective-permute-start.10 = (bf16[128,2048]{1,0:T(8,128)(2,1)}, bf16[128,2048]{1,0:T(8,128)(2,1)}, u32[]{:S(2)}, u32[]{:S(2)}) collective-permute-start(bf16[128,2048]{1,0:T(8,128)(2,1)} %get-tuple-element.40), channel_id=1, source_target_pairs={{0,4},{1,5},{2,6},{3,7},{4,0},{5,1},{6,2},{7,3},{8,12},{9,13},{10,... | collective-permute-start | bytes 1572872 | tf_op jit(solution)/shard_map/ppermute | solution.py:328
  14.6 2.6 %collective-permute-done = bf16[128,1024]{1,0:T(8,128)(2,1)S(1)} collective-permute-done((bf16[128,1024]{1,0:T(8,128)(2,1)S(1)}, bf16[128,1024]{1,0:T(8,128)(2,1)S(1)}, u32[]{:S(2)}, u32[]{:S(2)}) %collective-permute-start) | collective-permute-done | bytes 262176 | tf_op jit(solution)/shard_map/ppermute | solution.py:332
  17.2 0.6 gather_fusion
  17.9 7.2 %collective-permute-done.1 = bf16[128,1024]{1,0:T(8,128)(2,1)} collective-permute-done((bf16[128,1024]{1,0:T(8,128)(2,1)S(1)}, bf16[128,1024]{1,0:T(8,128)(2,1)}, u32[]{:S(2)}, u32[]{:S(2)}) %collective-permute-start.1) | collective-permute-done | bytes 262176 | tf_op jit(solution)/shard_map/ppermute | solution.py:333
  25.1 1.2 %collective-permute-done.4.refs_3_.refs_4_ = bf16[512,1024]{1,0:T(8,128)(2,1)S(1)} collective-permute-done((bf16[512,1024]{1,0:T(8,128)(2,1)}, bf16[512,1024]{1,0:T(8,128)(2,1)S(1)}, u32[]{:S(2)}, u32[]{:S(2)}) %collective-permute-start.4) | collective-permute-done | bytes 1048608 | tf_op jit(solution)/shard_map/ppermute | solution.py:325
  26.7 0.6 gather_fusion.1
  27.3 0.3 fusion
  27.7 6.9 %collective-permute-done.7.refs_1_ = bf16[128,2048]{1,0:T(8,128)(2,1)} collective-permute-done((bf16[128,2048]{1,0:T(8,128)(2,1)}, bf16[128,2048]{1,0:T(8,128)(2,1)}, u32[]{:S(2)}, u32[]{:S(2)}) %collective-permute-start.7) | collective-permute-done | bytes 524320 | tf_op jit(solution)/shard_map/ppermute | solution.py:330
  34.5 2.8 %products.1 = (bf16[128,1024]{1,0:T(8,128)(2,1)S(1)}, bf16[128,1024]{1,0:T(8,128)(2,1)S(1)}) custom-call(bf16[128,2048]{1,0:T(8,128)(2,1)} %collective-permute-done.6.refs_0_, bf16[128,2048]{1,0:T(8,128)(2,1)} %collective-permute-done.7.refs_1_, bf16[512,1024]{1,0:T(8,128)(2,1)S(1)} %copy-done.1, ...), custom_call_target="tpu_custom_call" | custom-call | flops 1073741824 | bytes 4194304 | tf_op jit(solution)/shard_map/products/pallas_call | solution.py:110
  37.3 3.9 %collective-permute-start.8 = (bf16[128,1024]{1,0:T(8,128)(2,1)S(1)}, bf16[128,1024]{1,0:T(8,128)(2,1)S(1)}, u32[]{:S(2)}, u32[]{:S(2)}) collective-permute-start(bf16[128,1024]{1,0:T(8,128)(2,1)S(1)} %get-tuple-element.38), channel_id=1, source_target_pairs={{0,6},{1,7},{2,0},{3,1},{4,2},{5,3},{6,4},{7,5},{8,14},{9,15},{10,... | collective-permute-start | bytes 786440 | tf_op jit(solution)/shard_map/ppermute | solution.py:342
  41.3 2.2 %far_product.1 = bf16[128,1024]{1,0:T(8,128)(2,1)S(1)} custom-call(bf16[128,2048]{1,0:T(8,128)(2,1)} %collective-permute-done.10.refs_0_, bf16[512,1024]{1,0:T(8,128)(2,1)S(1)} %copy-done.1, bf16[512,1024]{1,0:T(8,128)(2,1)S(1)} %collective-permute-done.2.refs_2_.refs_3_, bf16[512,1024]{1,0:T(8,128)(2,1)S(1)} %collective-permute-done.4.refs_3_.refs_4_, ...), custom_call_target="tpu_custom_call" | custom-call | flops 536870912 | bytes 4194304 | tf_op jit(solution)/shard_map/far_product/pallas_call | solution.py:110
  43.5 1.6 %collective-permute-start.11 = (bf16[128,1024]{1,0:T(8,128)(2,1)S(1)}, bf16[128,1024]{1,0:T(8,128)(2,1)S(1)}, u32[]{:S(2)}, u32[]{:S(2)}) collective-permute-start(bf16[128,1024]{1,0:T(8,128)(2,1)S(1)} %far_product.1), channel_id=1, source_target_pairs={{0,4},{1,5},{2,6},{3,7},{4,0},{5,1},{6,2},{7,3},{8,12},{9,13},{10,... | collective-permute-start | bytes 786440 | tf_op jit(solution)/shard_map/ppermute | solution.py:342
  45.3 0.2 collective-permute-start.3
  45.5 1.9 %own_product.1.own_ref = f32[128,1024]{1,0:T(8,128)S(1)} custom-call(bf16[128,2048]{1,0:T(8,128)(2,1)S(1)} %copy-done.3, bf16[512,1024]{1,0:T(8,128)(2,1)S(1)} %copy-done.1, bf16[512,1024]{1,0:T(8,128)(2,1)S(1)} %collective-permute-done.2.refs_2_.refs_3_, bf16[512,1024]{1,0:T(8,128)(2,1)S(1)} %collective-permute-done.4.refs_3_.refs_4_, ...), custom_call_target="tpu_custom_call" | custom-call | flops 536870912 | bytes 4194304 | tf_op jit(solution)/shard_map/own_product/pallas_call | solution.py:110
  47.4 4.2 %collective-permute-done.9.r3_ref = bf16[128,1024]{1,0:T(8,128)(2,1)S(1)} collective-permute-done((bf16[128,1024]{1,0:T(8,128)(2,1)S(1)}, bf16[128,1024]{1,0:T(8,128)(2,1)S(1)}, u32[]{:S(2)}, u32[]{:S(2)}) %collective-permute-start.9) | collective-permute-done | bytes 262176 | tf_op jit(solution)/shard_map/ppermute | solution.py:342
  51.7 0.4 keys_values.1
  52.0 0.4 collective-permute-start.12
  52.4 0.7 collective-permute-start.13
  53.1 2.6 %collective-permute-start.14 = (bf16[128,256]{1,0:T(8,128)(2,1)S(1)}, bf16[128,256]{1,0:T(8,128)(2,1)S(1)}, u32[]{:S(2)}, u32[]{:S(2)}) collective-permute-start(bf16[128,256]{1,0:T(8,128)(2,1)S(1)} %get-tuple-element.44), channel_id=1, source_target_pairs={{0,144},{16,128},{32,176},{48,160},{64,208},{80,192},{96,240},{112... | collective-permute-start | bytes 196616 | tf_op jit(solution)/shard_map/ppermute | solution.py:347
  55.8 0.8 collective-permute-done.12
  56.6 0.1 collective-permute-done.13
  56.7 1.6 %collective-permute-done.14 = bf16[128,256]{1,0:T(8,128)(2,1)S(1)} collective-permute-done((bf16[128,256]{1,0:T(8,128)(2,1)S(1)}, bf16[128,256]{1,0:T(8,128)(2,1)S(1)}, u32[]{:S(2)}, u32[]{:S(2)}) %collective-permute-start.14) | collective-permute-done | bytes 65568 | tf_op jit(solution)/shard_map/ppermute | solution.py:347
  58.3 8.4 %collective-permute-start.17 = (bf16[512,256]{1,0:T(8,128)(2,1)S(1)}, bf16[512,256]{1,0:T(8,128)(2,1)S(1)}, u32[]{:S(2)}, u32[]{:S(2)}) collective-permute-start(bf16[512,256]{1,0:T(8,128)(2,1)S(1)} %constant_dynamic-update-slice_fusion.kv_ref), channel_id=1, source_target_pairs={{0,96},{16,112},{32,0},{48,16},{64,32},{80,48},{96,64},{112,80},{1... | collective-permute-start | bytes 786440 | tf_op jit(solution)/shard_map/ppermute | solution.py:350
  66.8 1.1 %pad_maximum_fusion.q_ref.refs_1_ = bf16[4,128,1024]{2,1,0:T(8,128)(2,1)S(1)} fusion(bf16[1,128,1024]{2,1,0:T(8,128)(2,1)} %bitcast.19, bf16[1,128,1024]{2,1,0:T(8,128)(2,1)S(1)} %bitcast.35, bf16[1,128,1024]{2,1,0:T(8,128)(2,1)S(1)} %bitcast.36, bf16[1,128,1024]{2,1,0:T(8,128)(2,1)S(1)} %get-tuple-element.59), kind=kLoop, calls=%fused_computation.2 | loop fusion | flops 1572864 | bytes 2097152 | tf_op jit(solution)/shard_map/stack | solution.py:337
  67.9 3.3 %attend_first.1 = (f32[4,1024,128]{2,1,0:T(8,128)S(1)}, f32[4,1024,256]{2,1,0:T(8,128)S(1)}) custom-call(s32[4,16]{1,0:T(4,128)S(1)} %select_select_fusion.flag_ref.refs_0_, bf16[4,128,1024]{2,1,0:T(8,128)(2,1)S(1)} %pad_maximum_fusion.q_ref.refs_1_, bf16[512,256]{1,0:T(8,128)(2,1)S(1)} %constant_dynamic-update-slice_fusion.kv_ref), custom_call_target="tpu_custom_call" | custom-call | flops 1073741824 | bytes 4194304 | tf_op jit(solution)/shard_map/attend_first/pallas_call | solution.py:268
  71.2 4.3 %collective-permute-done.17.down_ref = bf16[512,256]{1,0:T(8,128)(2,1)S(1)} collective-permute-done((bf16[512,256]{1,0:T(8,128)(2,1)S(1)}, bf16[512,256]{1,0:T(8,128)(2,1)S(1)}, u32[]{:S(2)}, u32[]{:S(2)}) %collective-permute-start.17) | collective-permute-done | bytes 262176 | tf_op jit(solution)/shard_map/ppermute | solution.py:350
  75.5 4.7 %collective-permute-start.18 = (bf16[256,256]{1,0:T(8,128)(2,1)S(1)}, bf16[256,256]{1,0:T(8,128)(2,1)S(1)}, u32[]{:S(2)}, u32[]{:S(2)}) collective-permute-start(bf16[256,256]{1,0:T(8,128)(2,1)S(1)} %slice.13), channel_id=1, source_target_pairs={{0,96},{16,112},{32,0},{48,16},{64,32},{80,48},{96,64},{112,80},{1... | collective-permute-start | bytes 393224 | tf_op jit(solution)/shard_map/ppermute | solution.py:352
  80.3 0.4 collective-permute-done.15.up_ref
  80.6 0.3 collective-permute-start.16
  80.9 3.0 %attend_more.1 = (f32[4,1024,128]{2,1,0:T(8,128)S(1)}, f32[4,1024,256]{2,1,0:T(8,128)S(1)}) custom-call(s32[4,16]{1,0:T(4,128)S(1)} %select_select_fusion.flag_ref.refs_0_, bf16[4,128,1024]{2,1,0:T(8,128)(2,1)S(1)} %pad_maximum_fusion.q_ref.refs_1_, ...), custom_call_target="tpu_custom_call", output_to_operand_aliasing={{0}: (4, {}), {1}: (5, {})} | custom-call | flops 3221225472 | bytes 4194304 | tf_op jit(solution)/shard_map/attend_more/pallas_call | solution.py:268
  83.9 0.2 collective-permute-done.18.refs_3_
  84.1 4.5 %collective-permute-done.16.refs_2_ = bf16[256,256]{1,0:T(8,128)(2,1)S(1)} collective-permute-done((bf16[256,256]{1,0:T(8,128)(2,1)S(1)}, bf16[256,256]{1,0:T(8,128)(2,1)S(1)}, u32[]{:S(2)}, u32[]{:S(2)}) %collective-permute-start.16) | collective-permute-done | bytes 131104 | tf_op jit(solution)/shard_map/ppermute | solution.py:351
  88.6 1.9 %attend_others.1 = (f32[4,1024,128]{2,1,0:T(8,128)S(1)}, f32[4,1024,256]{2,1,0:T(8,128)S(1)}, bf16[128,1024]{1,0:T(8,128)(2,1)S(1)}, bf16[128,1024]{1,0:T(8,128)(2,1)S(1)}) custom-call(s32[4,16]{1,0:T(4,128)S(1)} %select_select_fusion.flag_ref.refs_0_, ...), custom_call_target="tpu_custom_call", output_to_operand_aliasing={{0}: (4, {}), {1}: (5, {})} | custom-call | flops 1073741824 | bytes 4194304 | tf_op jit(solution)/shard_map/attend_others/pallas_call | solution.py:268
  90.5 1.0 attend_own.1
  91.5 2.2 %collective-permute-start.19 = (bf16[128,1024]{1,0:T(8,128)(2,1)S(1)}, bf16[128,1024]{1,0:T(8,128)(2,1)S(1)}, u32[]{:S(2)}, u32[]{:S(2)}) collective-permute-start(bf16[128,1024]{1,0:T(8,128)(2,1)S(1)} %get-tuple-element.52), channel_id=1, source_target_pairs={{0,16},{16,0},{32,48},{48,32},{64,80},{80,64},{96,112},{112,96},{1... | collective-permute-start | bytes 786440 | tf_op jit(solution)/shard_map/ppermute | solution.py:382
  93.7 1.4 %collective-permute-start.20 = (bf16[128,1024]{1,0:T(8,128)(2,1)S(1)}, bf16[128,1024]{1,0:T(8,128)(2,1)S(1)}, u32[]{:S(2)}, u32[]{:S(2)}) collective-permute-start(bf16[128,1024]{1,0:T(8,128)(2,1)S(1)} %get-tuple-element.53), channel_id=1, source_target_pairs={{0,128},{16,144},{32,160},{48,176},{64,192},{80,208},{96,224},{112... | collective-permute-start | bytes 786440 | tf_op jit(solution)/shard_map/ppermute | solution.py:382
  95.1 0.1 collective-permute-start.21
  95.3 2.8 %collective-permute-done.19.refs_1_ = bf16[128,1024]{1,0:T(8,128)(2,1)S(1)} collective-permute-done((bf16[128,1024]{1,0:T(8,128)(2,1)S(1)}, bf16[128,1024]{1,0:T(8,128)(2,1)S(1)}, u32[]{:S(2)}, u32[]{:S(2)}) %collective-permute-start.19) | collective-permute-done | bytes 262176 | tf_op jit(solution)/shard_map/ppermute | solution.py:382
  98.1 4.8 %collective-permute-done.20.refs_2_ = bf16[128,1024]{1,0:T(8,128)(2,1)S(1)} collective-permute-done((bf16[128,1024]{1,0:T(8,128)(2,1)S(1)}, bf16[128,1024]{1,0:T(8,128)(2,1)S(1)}, u32[]{:S(2)}, u32[]{:S(2)}) %collective-permute-start.20) | collective-permute-done | bytes 262176 | tf_op jit(solution)/shard_map/ppermute | solution.py:382
  102.9 1.0 %place.1 = bf16[128,4096]{1,0:T(8,128)(2,1)} custom-call(s32[1]{0:T(128)} %bitcast.j_ref, bf16[128,1024]{1,0:T(8,128)(2,1)S(1)} %get-tuple-element.51.refs_0_, bf16[128,1024]{1,0:T(8,128)(2,1)S(1)} %collective-permute-done.19.refs_1_, bf16[128,1024]{1,0:T(8,128)(2,1)S(1)} %collective-permute-done.20.refs_2_, ...), custom_call_target="tpu_custom_call" | custom-call | tf_op jit(solution)/shard_map/place/pallas_call | solution.py:289
  (54 shorter events, 0.9 us)
Async XLA Ops:
  0.0 17.2 %copy-start = (s32[1,16,16]{2,1,0:T(8,128)S(1)}, s32[1,16,16]{2,1,0:T(8,128)}, u32[]{:S(2)}) copy-start(s32[1,16,16]{2,1,0:T(8,128)} %param.11) | copy-start | bytes 3076
  0.0 26.4 %collective-permute-start.4 = (bf16[512,1024]{1,0:T(8,128)(2,1)}, bf16[512,1024]{1,0:T(8,128)(2,1)S(1)}, u32[]{:S(2)}, u32[]{:S(2)}) collective-permute-start(bf16[512,1024]{1,0:T(8,128)(2,1)} %refs_1_.3), channel_id=1, source_target_pairs={{0,136},{1,137},{2,138},{3,139},{4,140},{5,141},{6,142},{7,143},{8... | collective-permute-start | bytes 3145736 | tf_op jit(solution)/shard_map/ppermute | solution.py:325
  3.1 0.8 copy-start.4
  3.9 4.8 %copy-start.6 = (bf16[1,128,4096]{2,1,0:T(8,128)(2,1)S(1)}, bf16[1,128,4096]{2,1,0:T(8,128)(2,1)}, u32[]{:S(2)}) copy-start(bf16[1,128,4096]{2,1,0:T(8,128)(2,1)} %param.7) | copy-start | bytes 3145732
  3.9 21.3 %copy-start.1 = (bf16[512,1024]{1,0:T(8,128)(2,1)S(1)}, bf16[512,1024]{1,0:T(8,128)(2,1)}, u32[]{:S(2)}) copy-start(bf16[512,1024]{1,0:T(8,128)(2,1)} %refs_1_.3) | copy-start | bytes 3145732
  7.8 0.8 copy-start.2
  9.4 7.8 %collective-permute-start = (bf16[128,1024]{1,0:T(8,128)(2,1)S(1)}, bf16[128,1024]{1,0:T(8,128)(2,1)S(1)}, u32[]{:S(2)}, u32[]{:S(2)}) collective-permute-start(bf16[128,1024]{1,0:T(8,128)(2,1)S(1)} %get-tuple-element.31), channel_id=1, source_target_pairs={{0,128},{16,144},{32,160},{48,176},{64,192},{80,208},{96,224},{112... | collective-permute-start | bytes 786440 | tf_op jit(solution)/shard_map/ppermute | solution.py:332
  9.5 18.1 %collective-permute-start.6 = (bf16[128,2048]{1,0:T(8,128)(2,1)}, bf16[128,2048]{1,0:T(8,128)(2,1)}, u32[]{:S(2)}, u32[]{:S(2)}) collective-permute-start(bf16[128,2048]{1,0:T(8,128)(2,1)} %get-tuple-element.36), channel_id=1, source_target_pairs={{0,2},{1,3},{2,4},{3,5},{4,6},{5,7},{6,0},{7,1},{8,10},{9,11},{10,... | collective-permute-start | bytes 1572872 | tf_op jit(solution)/shard_map/ppermute | solution.py:329
  11.0 23.5 %collective-permute-start.7 = (bf16[128,2048]{1,0:T(8,128)(2,1)}, bf16[128,2048]{1,0:T(8,128)(2,1)}, u32[]{:S(2)}, u32[]{:S(2)}) collective-permute-start(bf16[128,2048]{1,0:T(8,128)(2,1)} %get-tuple-element.37), channel_id=1, source_target_pairs={{0,6},{1,7},{2,0},{3,1},{4,2},{5,3},{6,4},{7,5},{8,14},{9,15},{10,... | collective-permute-start | bytes 1572872 | tf_op jit(solution)/shard_map/ppermute | solution.py:330
  12.8 28.5 %collective-permute-start.10 = (bf16[128,2048]{1,0:T(8,128)(2,1)}, bf16[128,2048]{1,0:T(8,128)(2,1)}, u32[]{:S(2)}, u32[]{:S(2)}) collective-permute-start(bf16[128,2048]{1,0:T(8,128)(2,1)} %get-tuple-element.40), channel_id=1, source_target_pairs={{0,4},{1,5},{2,6},{3,7},{4,0},{5,1},{6,2},{7,3},{8,12},{9,13},{10,... | collective-permute-start | bytes 1572872 | tf_op jit(solution)/shard_map/ppermute | solution.py:328
  17.2 0.7 copy-start.8
  17.2 8.0 %collective-permute-start.1 = (bf16[128,1024]{1,0:T(8,128)(2,1)S(1)}, bf16[128,1024]{1,0:T(8,128)(2,1)}, u32[]{:S(2)}, u32[]{:S(2)}) collective-permute-start(bf16[128,1024]{1,0:T(8,128)(2,1)S(1)} %get-tuple-element.32), channel_id=1, source_target_pairs={{0,144},{16,128},{32,176},{48,160},{64,208},{80,192},{96,240},{112... | collective-permute-start | bytes 786440 | tf_op jit(solution)/shard_map/ppermute | solution.py:333
  25.1 9.4 %collective-permute-start.2 = (bf16[512,1024]{1,0:T(8,128)(2,1)S(1)}, bf16[512,1024]{1,0:T(8,128)(2,1)S(1)}, u32[]{:S(2)}, u32[]{:S(2)}) collective-permute-start(bf16[512,1024]{1,0:T(8,128)(2,1)S(1)} %copy-done.1), channel_id=1, source_target_pairs={{0,1},{1,0},{2,3},{3,2},{4,5},{5,4},{6,7},{7,6},{8,9},{9,8},{10,11... | collective-permute-start | bytes 3145736 | tf_op jit(solution)/shard_map/ppermute | solution.py:334
  26.4 8.1 %collective-permute-start.5 = (bf16[512,1024]{1,0:T(8,128)(2,1)S(1)}, bf16[512,1024]{1,0:T(8,128)(2,1)}, u32[]{:S(2)}, u32[]{:S(2)}) collective-permute-start(bf16[512,1024]{1,0:T(8,128)(2,1)S(1)} %collective-permute-done.4.refs_3_.refs_4_), channel_id=1, source_target_pairs={{0,1},{1,0},{2,3},{3,2},{4,5},{5,4},{6,7},{7,6},{8,9},{9,8},{10,11... | collective-permute-start | bytes 3145736 | tf_op jit(solution)/shard_map/ppermute | solution.py:335
  37.3 10.1 %collective-permute-start.8 = (bf16[128,1024]{1,0:T(8,128)(2,1)S(1)}, bf16[128,1024]{1,0:T(8,128)(2,1)S(1)}, u32[]{:S(2)}, u32[]{:S(2)}) collective-permute-start(bf16[128,1024]{1,0:T(8,128)(2,1)S(1)} %get-tuple-element.38), channel_id=1, source_target_pairs={{0,6},{1,7},{2,0},{3,1},{4,2},{5,3},{6,4},{7,5},{8,14},{9,15},{10,... | collective-permute-start | bytes 786440 | tf_op jit(solution)/shard_map/ppermute | solution.py:342
  41.3 4.0 %copy-start.7 = (bf16[128,1024]{1,0:T(8,128)(2,1)S(1)}, bf16[128,1024]{1,0:T(8,128)(2,1)}, u32[]{:S(2)}) copy-start(bf16[128,1024]{1,0:T(8,128)(2,1)} %get-tuple-element.34) | copy-start | bytes 786436
  41.3 4.2 %copy-start.3 = (bf16[128,2048]{1,0:T(8,128)(2,1)S(1)}, bf16[128,2048]{1,0:T(8,128)(2,1)}, u32[]{:S(2)}) copy-start(bf16[128,2048]{1,0:T(8,128)(2,1)} %copy-done.2) | copy-start | bytes 1572868
  41.3 10.4 %collective-permute-start.9 = (bf16[128,1024]{1,0:T(8,128)(2,1)S(1)}, bf16[128,1024]{1,0:T(8,128)(2,1)S(1)}, u32[]{:S(2)}, u32[]{:S(2)}) collective-permute-start(bf16[128,1024]{1,0:T(8,128)(2,1)S(1)} %get-tuple-element.39), channel_id=1, source_target_pairs={{0,2},{1,3},{2,4},{3,5},{4,6},{5,7},{6,0},{7,1},{8,10},{9,11},{10,... | collective-permute-start | bytes 786440 | tf_op jit(solution)/shard_map/ppermute | solution.py:342
  43.5 8.2 %collective-permute-start.11 = (bf16[128,1024]{1,0:T(8,128)(2,1)S(1)}, bf16[128,1024]{1,0:T(8,128)(2,1)S(1)}, u32[]{:S(2)}, u32[]{:S(2)}) collective-permute-start(bf16[128,1024]{1,0:T(8,128)(2,1)S(1)} %far_product.1), channel_id=1, source_target_pairs={{0,4},{1,5},{2,6},{3,7},{4,0},{5,1},{6,2},{7,3},{8,12},{9,13},{10,... | collective-permute-start | bytes 786440 | tf_op jit(solution)/shard_map/ppermute | solution.py:342
  45.2 6.4 %copy-start.5 = (f32[1024]{0:T(1024)S(1)}, f32[1024]{0:T(1024)}, u32[]{:S(2)}) copy-start(f32[1024]{0:T(1024)} %param.9) | copy-start | bytes 12292
  45.3 21.6 %collective-permute-start.3 = (bf16[128,1024]{1,0:T(8,128)(2,1)S(1)}, bf16[128,1024]{1,0:T(8,128)(2,1)S(1)}, u32[]{:S(2)}, u32[]{:S(2)}) collective-permute-start(bf16[128,1024]{1,0:T(8,128)(2,1)S(1)} %copy-done.7), channel_id=1, source_target_pairs={{0,16},{16,0},{32,48},{48,32},{64,80},{80,64},{96,112},{112,96},{1... | collective-permute-start | bytes 786440 | tf_op jit(solution)/shard_map/ppermute | solution.py:336
  47.4 19.4 %copy-start.9 = (bf16[128,1024]{1,0:T(8,128)(2,1)S(1)}, bf16[128,1024]{1,0:T(8,128)(2,1)}, u32[]{:S(2)}) copy-start(bf16[128,1024]{1,0:T(8,128)(2,1)} %copy-done.8) | copy-start | bytes 786436
  52.0 4.5 %collective-permute-start.12 = (bf16[128,256]{1,0:T(8,128)(2,1)S(1)}, bf16[128,256]{1,0:T(8,128)(2,1)S(1)}, u32[]{:S(2)}, u32[]{:S(2)}) collective-permute-start(bf16[128,256]{1,0:T(8,128)(2,1)S(1)} %get-tuple-element.42), channel_id=1, source_target_pairs={{0,16},{16,0},{32,48},{48,32},{64,80},{80,64},{96,112},{112,96},{1... | collective-permute-start | bytes 196616 | tf_op jit(solution)/shard_map/ppermute | solution.py:347
  52.4 4.3 %collective-permute-start.13 = (bf16[128,256]{1,0:T(8,128)(2,1)S(1)}, bf16[128,256]{1,0:T(8,128)(2,1)S(1)}, u32[]{:S(2)}, u32[]{:S(2)}) collective-permute-start(bf16[128,256]{1,0:T(8,128)(2,1)S(1)} %get-tuple-element.43), channel_id=1, source_target_pairs={{0,128},{16,144},{32,160},{48,176},{64,192},{80,208},{96,224},{112... | collective-permute-start | bytes 196616 | tf_op jit(solution)/shard_map/ppermute | solution.py:347
  53.1 5.2 %collective-permute-start.14 = (bf16[128,256]{1,0:T(8,128)(2,1)S(1)}, bf16[128,256]{1,0:T(8,128)(2,1)S(1)}, u32[]{:S(2)}, u32[]{:S(2)}) collective-permute-start(bf16[128,256]{1,0:T(8,128)(2,1)S(1)} %get-tuple-element.44), channel_id=1, source_target_pairs={{0,144},{16,128},{32,176},{48,160},{64,208},{80,192},{96,240},{112... | collective-permute-start | bytes 196616 | tf_op jit(solution)/shard_map/ppermute | solution.py:347
  58.3 17.2 %collective-permute-start.17 = (bf16[512,256]{1,0:T(8,128)(2,1)S(1)}, bf16[512,256]{1,0:T(8,128)(2,1)S(1)}, u32[]{:S(2)}, u32[]{:S(2)}) collective-permute-start(bf16[512,256]{1,0:T(8,128)(2,1)S(1)} %constant_dynamic-update-slice_fusion.kv_ref), channel_id=1, source_target_pairs={{0,96},{16,112},{32,0},{48,16},{64,32},{80,48},{96,64},{112,80},{1... | collective-permute-start | bytes 786440 | tf_op jit(solution)/shard_map/ppermute | solution.py:350
  66.7 13.9 %collective-permute-start.15 = (bf16[512,256]{1,0:T(8,128)(2,1)S(1)}, bf16[512,256]{1,0:T(8,128)(2,1)S(1)}, u32[]{:S(2)}, u32[]{:S(2)}) collective-permute-start(bf16[512,256]{1,0:T(8,128)(2,1)S(1)} %constant_dynamic-update-slice_fusion.kv_ref), channel_id=1, source_target_pairs={{0,32},{16,48},{32,64},{48,80},{64,96},{80,112},{96,0},{112,16},{1... | collective-permute-start | bytes 786440 | tf_op jit(solution)/shard_map/ppermute | solution.py:349
  75.5 8.6 %collective-permute-start.18 = (bf16[256,256]{1,0:T(8,128)(2,1)S(1)}, bf16[256,256]{1,0:T(8,128)(2,1)S(1)}, u32[]{:S(2)}, u32[]{:S(2)}) collective-permute-start(bf16[256,256]{1,0:T(8,128)(2,1)S(1)} %slice.13), channel_id=1, source_target_pairs={{0,96},{16,112},{32,0},{48,16},{64,32},{80,48},{96,64},{112,80},{1... | collective-permute-start | bytes 393224 | tf_op jit(solution)/shard_map/ppermute | solution.py:352
  80.6 8.0 %collective-permute-start.16 = (bf16[256,256]{1,0:T(8,128)(2,1)S(1)}, bf16[256,256]{1,0:T(8,128)(2,1)S(1)}, u32[]{:S(2)}, u32[]{:S(2)}) collective-permute-start(bf16[256,256]{1,0:T(8,128)(2,1)S(1)} %slice.12), channel_id=1, source_target_pairs={{0,32},{16,48},{32,64},{48,80},{64,96},{80,112},{96,0},{112,16},{1... | collective-permute-start | bytes 393224 | tf_op jit(solution)/shard_map/ppermute | solution.py:351
  91.5 6.6 %collective-permute-start.19 = (bf16[128,1024]{1,0:T(8,128)(2,1)S(1)}, bf16[128,1024]{1,0:T(8,128)(2,1)S(1)}, u32[]{:S(2)}, u32[]{:S(2)}) collective-permute-start(bf16[128,1024]{1,0:T(8,128)(2,1)S(1)} %get-tuple-element.52), channel_id=1, source_target_pairs={{0,16},{16,0},{32,48},{48,32},{64,80},{80,64},{96,112},{112,96},{1... | collective-permute-start | bytes 786440 | tf_op jit(solution)/shard_map/ppermute | solution.py:382
  93.7 9.2 %collective-permute-start.20 = (bf16[128,1024]{1,0:T(8,128)(2,1)S(1)}, bf16[128,1024]{1,0:T(8,128)(2,1)S(1)}, u32[]{:S(2)}, u32[]{:S(2)}) collective-permute-start(bf16[128,1024]{1,0:T(8,128)(2,1)S(1)} %get-tuple-element.53), channel_id=1, source_target_pairs={{0,128},{16,144},{32,160},{48,176},{64,192},{80,208},{96,224},{112... | collective-permute-start | bytes 786440 | tf_op jit(solution)/shard_map/ppermute | solution.py:382
  95.1 7.8 %collective-permute-start.21 = (bf16[128,1024]{1,0:T(8,128)(2,1)S(1)}, bf16[128,1024]{1,0:T(8,128)(2,1)S(1)}, u32[]{:S(2)}, u32[]{:S(2)}) collective-permute-start(bf16[128,1024]{1,0:T(8,128)(2,1)S(1)} %get-tuple-element.54), channel_id=1, source_target_pairs={{0,144},{16,128},{32,176},{48,160},{64,208},{80,192},{96,240},{112... | collective-permute-start | bytes 786440 | tf_op jit(solution)/shard_map/ppermute | solution.py:382

commit v5 on v4

--- a/solution.py
+++ b/solution.py
@@ -104,19 +104,19 @@
         outs[i][...] = total[i * tokens : (i + 1) * tokens].astype(outs[i].dtype)
 
 
-def product_call(rows, weights, dtype, name):
+def product_call(rows, weights, dtypes):
     vm = pl.BlockSpec(memory_space=pltpu.VMEM)
     count, tokens = len(rows), rows[0].shape[0]
     return pl.pallas_call(
         lambda *refs: product_kernel(count, *refs),
         in_specs=[vm] * (count + len(weights)),
         out_specs=[vm] * count,
-        out_shape=[jax.ShapeDtypeStruct((tokens, 1024), dtype)] * count,
+        out_shape=[jax.ShapeDtypeStruct((tokens, 1024), dtype) for dtype in dtypes],
         compiler_params=pltpu.CompilerParams(vmem_limit_bytes=24 * 1024 * 1024),
         cost_estimate=pl.CostEstimate(
             flops=count * tokens * 2048 * 2048, bytes_accessed=4 << 20, transcendentals=0
         ),
-        name=name,
+        name="products",
     )(*rows, *weights)
 
 
@@ -337,10 +337,8 @@
     q4 = jnp.stack(q_parts)
 
     weights = [kv_weight, w_core, w_y, w_yc]
-    p1, p3 = product_call([n1, n3], weights, BF, "products")
-    (p2,) = product_call([n2], weights, BF, "far_product")
+    p1, p3, p2, own = product_call([n1, n3, n2, normed0], weights, [BF, BF, BF, F32])
     back = [lax.ppermute(p, "fsdp", x_pairs(k)) for p, k in ((p1, 3), (p3, 1), (p2, 2))]
-    (own,) = product_call([normed0], weights, F32, "own_product")
 
     cos, sin = rotary_tables(c * BLK, BLK)
     kvs = kv_call(j1, own, back[0], back[1], back[2], kv_bias.reshape(1, -1), cos, sin)
@@ -367,18 +365,19 @@
         attend_more_kernel, flags, [q4, up, down, top, acc], STATE, aliases={4: 0, 5: 1}, share=3, name="attend_more"
     )
 
-    def finish(pair, top, acc, name):
+    def finish(pair, top, acc, share, name):
         return attend_call(
             lambda *refs: attend_last_kernel(pair, *refs),
             flags,
             [q4, far0, far1, top, acc],
             STATE + [jax.ShapeDtypeStruct((BLK, GW), BF)] * 2,
             aliases={4: 0, 5: 1},
+            share=share,
             name=name,
         )
 
-    top, acc, out2, out3 = finish(1, top, acc, "attend_others")
-    top, acc, out0, out1 = finish(0, top, acc, "attend_own")
+    top, acc, out2, out3 = finish(1, top, acc, 1, "attend_others")
+    top, acc, out0, out1 = finish(0, top, acc, 16, "attend_own")
     parts = [out0] + [lax.ppermute(o, "ctx", member_pairs(k)) for k, o in ((1, out1), (2, out2), (3, out3))]
     return place_call(j1, parts).reshape(1, BLK, H * HD)
 

time: 105 us -> 113 us (1.076)
  waiting for transfers between devices: 41.7 us -> 48.6 us
  local copies, waits for them, and re-layouts: 3.81 us -> 7.15 us
  other arithmetic: 1.95 us -> 4.41 us
  Pallas kernels: 21.4 us -> 19.3 us
  starting transfers between devices: 34.9 us -> 33.1 us
    ppermute x3, waiting for transfers between devices: 4.22 us -> 10.1 us  [on_device(): lax.ppermute(p, 'fsdp', x_pairs(k))]
    unnamed x23 -> x41, local copies, waits for them, and re-layouts: 1.7 us -> 4.93 us
    pallas_call x3 -> x1, Pallas kernels: 6.94 us -> 4.85 us  [product_call(): pl.pallas_call(lambda *refs: product_kernel(count, *refs), in_specs=[vm]...]
    ppermute x3, starting transfers between devices: 5.5 us -> 3.53 us  [on_device(): lax.ppermute(p, 'fsdp', x_pairs(k))]
    ppermute x1, waiting for transfers between devices: 0.01 us -> 1.69 us  [on_device(): n2 = lax.ppermute(normed2, 'fsdp', x_pairs(2))]
    ppermute x1, waiting for transfers between devices: 6.87 us -> 5.43 us  [on_device(): n3 = lax.ppermute(normed3, 'fsdp', x_pairs(3))]
    ppermute x1, waiting for transfers between devices: 0.37 us -> 1.71 us  [on_device(): up = lax.ppermute(group, 'ctx', z_pairs(2))]
    ppermute x3, waiting for transfers between devices: 7.62 us -> 6.35 us  [on_device(): lax.ppermute(o, 'ctx', member_pairs(k))]
  transfers between devices with their start and end apart: 22 -> 22, of which waited for: 14 -> 15; matrix products, arithmetic and copies ran while one was open for 4% -> 6% of each run, Pallas kernels for 17% -> 9%
where the time goes in v5:
time: 113 us
  waiting for transfers between devices  48.6 us (43%)
  starting transfers between devices  33.1 us (29%)
  Pallas kernels  19.3 us (17%)
  local copies, waits for them, and re-layouts  7.15 us (6%)
  other arithmetic  4.41 us (4%)
    ppermute x3, waiting for transfers between devices, on_device(): lax.ppermute(p, 'fsdp', x_pairs(k))  10.1 us
    pallas_call x4, Pallas kernels, attend_call(): pl.pallas_call(kernel, in_specs=[pl.BlockSpec(memory_space=pltpu.SMEM)] +...  9.15 us
    ppermute x1, starting transfers between devices, on_device(): down = lax.ppermute(group, 'ctx', z_pairs(-2))  8.95 us
    ppermute x1, waiting for transfers between devices, on_device(): lax.ppermute(after(q_parts[3], q_parts[2]), 'ctx', member_pairs(3))  7.26 us
    ppermute x3, waiting for transfers between devices, on_device(): lax.ppermute(o, 'ctx', member_pairs(k))  6.35 us
    ppermute x1, waiting for transfers between devices, on_device(): n3 = lax.ppermute(normed3, 'fsdp', x_pairs(3))  5.43 us
    ppermute x1, waiting for transfers between devices, on_device(): far0 = lax.ppermute(up[:256], 'ctx', z_pairs(2))  5.43 us
    unnamed x41, local copies, waits for them, and re-layouts  4.93 us
  transfers between devices with their start and end apart: 22, of which 15 were waited for; matrix products, arithmetic and copies ran while one was open for 6% of the time, Pallas kernels for 9%

profile of v5, /device:TPU:32, one launch (start us, length us, event | category | flops | bytes accessed | tf_op | source)
XLA Modules:
  0.0 112.7 jit_solution(14849938684224031048)
XLA Ops:
  0.0 3.0 %collective-permute-start.7 = (bf16[512,1024]{1,0:T(8,128)(2,1)}, bf16[512,1024]{1,0:T(8,128)(2,1)S(1)}, u32[]{:S(2)}, u32[]{:S(2)}) collective-permute-start(bf16[512,1024]{1,0:T(8,128)(2,1)} %refs_4_.1), channel_id=1, source_target_pairs={{0,136},{1,137},{2,138},{3,139},{4,140},{5,141},{6,142},{7,143},{8... | collective-permute-start | bytes 3145736 | tf_op jit(solution)/shard_map/ppermute | solution.py:325
  3.1 0.8 copy-done.1
  3.9 3.9 %norm.1 = (bf16[128,2048]{1,0:T(8,128)(2,1)S(1)}, bf16[128,2048]{1,0:T(8,128)(2,1)}, bf16[128,2048]{1,0:T(8,128)(2,1)}, bf16[128,2048]{1,0:T(8,128)(2,1)}) custom-call(s32[3]{0:T(128)S(1)} %pad_add_fusion.1.pos_ref, bf16[128,8192]{1,0:T(8,128)(2,1)} %bitcast.34, f32[1,8192]{1,0:T(1,128)S(1)} %bitcast.32), custom_call_target="tpu_custom_call" | custom-call | flops 4194304 | bytes 4194304 | tf_op jit(solution)/shard_map/norm/pallas_call | solution.py:81
  7.8 0.8 copy-done.6
  8.6 0.8 constant_dynamic-slice_fusion
  9.5 1.5 %collective-permute-start.4 = (bf16[128,2048]{1,0:T(8,128)(2,1)}, bf16[128,2048]{1,0:T(8,128)(2,1)}, u32[]{:S(2)}, u32[]{:S(2)}) collective-permute-start(bf16[128,2048]{1,0:T(8,128)(2,1)} %get-tuple-element.37), channel_id=1, source_target_pairs={{0,2},{1,3},{2,4},{3,5},{4,6},{5,7},{6,0},{7,1},{8,10},{9,11},{10,... | collective-permute-start | bytes 1572872 | tf_op jit(solution)/shard_map/ppermute | solution.py:329
  11.0 1.7 %collective-permute-start.5 = (bf16[128,2048]{1,0:T(8,128)(2,1)}, bf16[128,2048]{1,0:T(8,128)(2,1)}, u32[]{:S(2)}, u32[]{:S(2)}) collective-permute-start(bf16[128,2048]{1,0:T(8,128)(2,1)} %get-tuple-element.38), channel_id=1, source_target_pairs={{0,6},{1,7},{2,0},{3,1},{4,2},{5,3},{6,4},{7,5},{8,14},{9,15},{10,... | collective-permute-start | bytes 1572872 | tf_op jit(solution)/shard_map/ppermute | solution.py:330
  12.7 1.8 %collective-permute-start.6 = (bf16[128,2048]{1,0:T(8,128)(2,1)}, bf16[128,2048]{1,0:T(8,128)(2,1)}, u32[]{:S(2)}, u32[]{:S(2)}) collective-permute-start(bf16[128,2048]{1,0:T(8,128)(2,1)} %get-tuple-element.39), channel_id=1, source_target_pairs={{0,4},{1,5},{2,6},{3,7},{4,0},{5,1},{6,2},{7,3},{8,12},{9,13},{10,... | collective-permute-start | bytes 1572872 | tf_op jit(solution)/shard_map/ppermute | solution.py:328
  14.6 2.6 %collective-permute-done = bf16[128,1024]{1,0:T(8,128)(2,1)S(1)} collective-permute-done((bf16[128,1024]{1,0:T(8,128)(2,1)S(1)}, bf16[128,1024]{1,0:T(8,128)(2,1)S(1)}, u32[]{:S(2)}, u32[]{:S(2)}) %collective-permute-start) | collective-permute-done | bytes 262176 | tf_op jit(solution)/shard_map/ppermute | solution.py:332
  17.1 0.6 multiply_exponential_fusion
  17.8 7.3 %collective-permute-done.1 = bf16[128,1024]{1,0:T(8,128)(2,1)} collective-permute-done((bf16[128,1024]{1,0:T(8,128)(2,1)S(1)}, bf16[128,1024]{1,0:T(8,128)(2,1)}, u32[]{:S(2)}, u32[]{:S(2)}) %collective-permute-start.1) | collective-permute-done | bytes 262176 | tf_op jit(solution)/shard_map/ppermute | solution.py:333
  25.1 1.3 %collective-permute-done.7.refs_6_ = bf16[512,1024]{1,0:T(8,128)(2,1)S(1)} collective-permute-done((bf16[512,1024]{1,0:T(8,128)(2,1)}, bf16[512,1024]{1,0:T(8,128)(2,1)S(1)}, u32[]{:S(2)}, u32[]{:S(2)}) %collective-permute-start.7) | collective-permute-done | bytes 1048608 | tf_op jit(solution)/shard_map/ppermute | solution.py:325
  26.4 0.6 gather_fusion
  27.1 0.6 pad_clamp_fusion
  27.8 1.6 %fusion = (f32[128,64]{1,0:T(8,128)S(1)}, f32[128,64]{1,0:T(8,128)S(1)}, f32[128,64]{1,0:T(8,128)}) fusion(f32[64]{0:T(128)} %multiply_exponential_fusion, f32[128]{0:T(128)S(1)} %add_convert_fusion), kind=kLoop, calls=%fused_computation.10 | loop fusion | flops 16384 | bytes 99072 | tf_op jit(solution)/shard_map/neg | solution.py:305
  29.4 5.4 %collective-permute-done.5.refs_1_ = bf16[128,2048]{1,0:T(8,128)(2,1)} collective-permute-done((bf16[128,2048]{1,0:T(8,128)(2,1)}, bf16[128,2048]{1,0:T(8,128)(2,1)}, u32[]{:S(2)}, u32[]{:S(2)}) %collective-permute-start.5) | collective-permute-done | bytes 524320 | tf_op jit(solution)/shard_map/ppermute | solution.py:330
  34.8 1.7 %collective-permute-done.6.refs_2_ = bf16[128,2048]{1,0:T(8,128)(2,1)} collective-permute-done((bf16[128,2048]{1,0:T(8,128)(2,1)}, bf16[128,2048]{1,0:T(8,128)(2,1)}, u32[]{:S(2)}, u32[]{:S(2)}) %collective-permute-start.6) | collective-permute-done | bytes 524320 | tf_op jit(solution)/shard_map/ppermute | solution.py:328
  36.5 1.0 copy-done.4
  37.5 1.2 %copy-done.5 = bf16[512,1024]{1,0:T(8,128)(2,1)S(1)} copy-done((bf16[512,1024]{1,0:T(8,128)(2,1)S(1)}, bf16[512,1024]{1,0:T(8,128)(2,1)}, u32[]{:S(2)}) %copy-start.5) | copy-done | bytes 1048600
  38.7 1.0 copy-done.7
  39.8 4.9 %products.1 = (bf16[128,1024]{1,0:T(8,128)(2,1)}, bf16[128,1024]{1,0:T(8,128)(2,1)}, bf16[128,1024]{1,0:T(8,128)(2,1)}, f32[128,1024]{1,0:T(8,128)S(1)}) custom-call(bf16[128,2048]{1,0:T(8,128)(2,1)} %collective-permute-done.4.refs_0_, bf16[128,2048]{1,0:T(8,128)(2,1)} %collective-permute-done.5.refs_1_, bf16[128,2048]{1,0:T(8,128)(2,1)} %collective-permute-done.6.refs_2_, ...), custom_call_target="tpu_custom_call" | custom-call | flops 2147483648 | bytes 4194304 | tf_op jit(solution)/shard_map/products/pallas_call | solution.py:110
  44.6 2.0 %collective-permute-start.9 = (bf16[128,1024]{1,0:T(8,128)(2,1)}, bf16[128,1024]{1,0:T(8,128)(2,1)S(1)}, u32[]{:S(2)}, u32[]{:S(2)}) collective-permute-start(bf16[128,1024]{1,0:T(8,128)(2,1)} %get-tuple-element.42), channel_id=1, source_target_pairs={{0,6},{1,7},{2,0},{3,1},{4,2},{5,3},{6,4},{7,5},{8,14},{9,15},{10,... | collective-permute-start | bytes 786440 | tf_op jit(solution)/shard_map/ppermute | solution.py:341
  46.7 1.5 %collective-permute-start.11 = (bf16[128,1024]{1,0:T(8,128)(2,1)}, bf16[128,1024]{1,0:T(8,128)(2,1)S(1)}, u32[]{:S(2)}, u32[]{:S(2)}) collective-permute-start(bf16[128,1024]{1,0:T(8,128)(2,1)} %get-tuple-element.44), channel_id=1, source_target_pairs={{0,4},{1,5},{2,6},{3,7},{4,0},{5,1},{6,2},{7,3},{8,12},{9,13},{10,... | collective-permute-start | bytes 786440 | tf_op jit(solution)/shard_map/ppermute | solution.py:341
  48.3 0.7 gather_fusion.1
  49.4 4.7 %collective-permute-done.9.r1_ref = bf16[128,1024]{1,0:T(8,128)(2,1)S(1)} collective-permute-done((bf16[128,1024]{1,0:T(8,128)(2,1)}, bf16[128,1024]{1,0:T(8,128)(2,1)S(1)}, u32[]{:S(2)}, u32[]{:S(2)}) %collective-permute-start.9) | collective-permute-done | bytes 262176 | tf_op jit(solution)/shard_map/ppermute | solution.py:341
  54.1 5.5 %collective-permute-done.10.r3_ref = bf16[128,1024]{1,0:T(8,128)(2,1)S(1)} collective-permute-done((bf16[128,1024]{1,0:T(8,128)(2,1)}, bf16[128,1024]{1,0:T(8,128)(2,1)S(1)}, u32[]{:S(2)}, u32[]{:S(2)}) %collective-permute-start.10) | collective-permute-done | bytes 262176 | tf_op jit(solution)/shard_map/ppermute | solution.py:341
  59.6 0.4 keys_values.1
  60.1 1.8 %collective-permute-start.13 = (bf16[128,256]{1,0:T(8,128)(2,1)S(1)}, bf16[128,256]{1,0:T(8,128)(2,1)S(1)}, u32[]{:S(2)}, u32[]{:S(2)}) collective-permute-start(bf16[128,256]{1,0:T(8,128)(2,1)S(1)} %get-tuple-element.47), channel_id=1, source_target_pairs={{0,128},{16,144},{32,160},{48,176},{64,192},{80,208},{96,224},{112... | collective-permute-start | bytes 196616 | tf_op jit(solution)/shard_map/ppermute | solution.py:345
  61.9 1.6 %collective-permute-start.14 = (bf16[128,256]{1,0:T(8,128)(2,1)S(1)}, bf16[128,256]{1,0:T(8,128)(2,1)S(1)}, u32[]{:S(2)}, u32[]{:S(2)}) collective-permute-start(bf16[128,256]{1,0:T(8,128)(2,1)S(1)} %get-tuple-element.48), channel_id=1, source_target_pairs={{0,144},{16,128},{32,176},{48,160},{64,208},{80,192},{96,240},{112... | collective-permute-start | bytes 196616 | tf_op jit(solution)/shard_map/ppermute | solution.py:345
  63.5 0.8 collective-permute-done.12
  64.6 2.5 %collective-permute-done.14 = bf16[128,256]{1,0:T(8,128)(2,1)S(1)} collective-permute-done((bf16[128,256]{1,0:T(8,128)(2,1)S(1)}, bf16[128,256]{1,0:T(8,128)(2,1)S(1)}, u32[]{:S(2)}, u32[]{:S(2)}) %collective-permute-start.14) | collective-permute-done | bytes 65568 | tf_op jit(solution)/shard_map/ppermute | solution.py:345
  67.1 9.0 %collective-permute-start.17 = (bf16[512,256]{1,0:T(8,128)(2,1)S(1)}, bf16[512,256]{1,0:T(8,128)(2,1)S(1)}, u32[]{:S(2)}, u32[]{:S(2)}) collective-permute-start(bf16[512,256]{1,0:T(8,128)(2,1)S(1)} %constant_dynamic-update-slice_fusion.kv_ref), channel_id=1, source_target_pairs={{0,96},{16,112},{32,0},{48,16},{64,32},{80,48},{96,64},{112,80},{1... | collective-permute-start | bytes 786440 | tf_op jit(solution)/shard_map/ppermute | solution.py:348
  76.1 1.1 pad_maximum_fusion.q_ref.refs_1_
  77.2 3.3 %attend_first.1 = (f32[4,1024,128]{2,1,0:T(8,128)S(1)}, f32[4,1024,256]{2,1,0:T(8,128)S(1)}) custom-call(s32[4,16]{1,0:T(4,128)S(1)} %select_select_fusion.flag_ref.refs_0_, bf16[4,128,1024]{2,1,0:T(8,128)(2,1)S(1)} %pad_maximum_fusion.q_ref.refs_1_, bf16[512,256]{1,0:T(8,128)(2,1)S(1)} %constant_dynamic-update-slice_fusion.kv_ref), custom_call_target="tpu_custom_call" | custom-call | flops 1073741824 | bytes 4194304 | tf_op jit(solution)/shard_map/attend_first/pallas_call | solution.py:268
  80.5 3.2 %collective-permute-done.17.down_ref = bf16[512,256]{1,0:T(8,128)(2,1)S(1)} collective-permute-done((bf16[512,256]{1,0:T(8,128)(2,1)S(1)}, bf16[512,256]{1,0:T(8,128)(2,1)S(1)}, u32[]{:S(2)}, u32[]{:S(2)}) %collective-permute-start.17) | collective-permute-done | bytes 262176 | tf_op jit(solution)/shard_map/ppermute | solution.py:348
  83.7 4.7 %collective-permute-start.18 = (bf16[256,256]{1,0:T(8,128)(2,1)S(1)}, bf16[256,256]{1,0:T(8,128)(2,1)S(1)}, u32[]{:S(2)}, u32[]{:S(2)}) collective-permute-start(bf16[256,256]{1,0:T(8,128)(2,1)S(1)} %slice.13), channel_id=1, source_target_pairs={{0,96},{16,112},{32,0},{48,16},{64,32},{80,48},{96,64},{112,80},{1... | collective-permute-start | bytes 393224 | tf_op jit(solution)/shard_map/ppermute | solution.py:350
  88.4 1.7 %collective-permute-done.15.up_ref = bf16[512,256]{1,0:T(8,128)(2,1)S(1)} collective-permute-done((bf16[512,256]{1,0:T(8,128)(2,1)S(1)}, bf16[512,256]{1,0:T(8,128)(2,1)S(1)}, u32[]{:S(2)}, u32[]{:S(2)}) %collective-permute-start.15) | collective-permute-done | bytes 262176 | tf_op jit(solution)/shard_map/ppermute | solution.py:347
  90.1 0.3 collective-permute-start.16
  90.4 3.0 %attend_more.1 = (f32[4,1024,128]{2,1,0:T(8,128)S(1)}, f32[4,1024,256]{2,1,0:T(8,128)S(1)}) custom-call(s32[4,16]{1,0:T(4,128)S(1)} %select_select_fusion.flag_ref.refs_0_, bf16[4,128,1024]{2,1,0:T(8,128)(2,1)S(1)} %pad_maximum_fusion.q_ref.refs_1_, ...), custom_call_target="tpu_custom_call", output_to_operand_aliasing={{0}: (4, {}), {1}: (5, {})} | custom-call | flops 3221225472 | bytes 4194304 | tf_op jit(solution)/shard_map/attend_more/pallas_call | solution.py:268
  93.4 5.4 %collective-permute-done.16.refs_2_ = bf16[256,256]{1,0:T(8,128)(2,1)S(1)} collective-permute-done((bf16[256,256]{1,0:T(8,128)(2,1)S(1)}, bf16[256,256]{1,0:T(8,128)(2,1)S(1)}, u32[]{:S(2)}, u32[]{:S(2)}) %collective-permute-start.16) | collective-permute-done | bytes 131104 | tf_op jit(solution)/shard_map/ppermute | solution.py:349
  98.9 1.9 %attend_others.1 = (f32[4,1024,128]{2,1,0:T(8,128)S(1)}, f32[4,1024,256]{2,1,0:T(8,128)S(1)}, bf16[128,1024]{1,0:T(8,128)(2,1)S(1)}, bf16[128,1024]{1,0:T(8,128)(2,1)S(1)}) custom-call(s32[4,16]{1,0:T(4,128)S(1)} %select_select_fusion.flag_ref.refs_0_, ...), custom_call_target="tpu_custom_call", output_to_operand_aliasing={{0}: (4, {}), {1}: (5, {})} | custom-call | flops 1073741824 | bytes 4194304 | tf_op jit(solution)/shard_map/attend_others/pallas_call | solution.py:268
  100.7 1.0 attend_own.1
  101.7 0.7 collective-permute-start.19
  102.5 1.0 collective-permute-start.20
  103.4 1.9 %collective-permute-start.21 = (bf16[128,1024]{1,0:T(8,128)(2,1)S(1)}, bf16[128,1024]{1,0:T(8,128)(2,1)S(1)}, u32[]{:S(2)}, u32[]{:S(2)}) collective-permute-start(bf16[128,1024]{1,0:T(8,128)(2,1)S(1)} %get-tuple-element.58), channel_id=1, source_target_pairs={{0,144},{16,128},{32,176},{48,160},{64,208},{80,192},{96,240},{112... | collective-permute-start | bytes 786440 | tf_op jit(solution)/shard_map/ppermute | solution.py:381
  105.3 2.9 %collective-permute-done.19.refs_1_ = bf16[128,1024]{1,0:T(8,128)(2,1)S(1)} collective-permute-done((bf16[128,1024]{1,0:T(8,128)(2,1)S(1)}, bf16[128,1024]{1,0:T(8,128)(2,1)S(1)}, u32[]{:S(2)}, u32[]{:S(2)}) %collective-permute-start.19) | collective-permute-done | bytes 262176 | tf_op jit(solution)/shard_map/ppermute | solution.py:381
  108.2 3.5 %collective-permute-done.20.refs_2_ = bf16[128,1024]{1,0:T(8,128)(2,1)S(1)} collective-permute-done((bf16[128,1024]{1,0:T(8,128)(2,1)S(1)}, bf16[128,1024]{1,0:T(8,128)(2,1)S(1)}, u32[]{:S(2)}, u32[]{:S(2)}) %collective-permute-start.20) | collective-permute-done | bytes 262176 | tf_op jit(solution)/shard_map/ppermute | solution.py:381
  111.7 1.0 place.1
  (70 shorter events, 1.8 us)
Async XLA Ops:
  0.0 26.4 %copy-start = (s32[1,16,16]{2,1,0:T(8,128)S(1)}, s32[1,16,16]{2,1,0:T(8,128)}, u32[]{:S(2)}) copy-start(s32[1,16,16]{2,1,0:T(8,128)} %param.11) | copy-start | bytes 3076
  0.0 26.4 %collective-permute-start.7 = (bf16[512,1024]{1,0:T(8,128)(2,1)}, bf16[512,1024]{1,0:T(8,128)(2,1)S(1)}, u32[]{:S(2)}, u32[]{:S(2)}) collective-permute-start(bf16[512,1024]{1,0:T(8,128)(2,1)} %refs_4_.1), channel_id=1, source_target_pairs={{0,136},{1,137},{2,138},{3,139},{4,140},{5,141},{6,142},{7,143},{8... | collective-permute-start | bytes 3145736 | tf_op jit(solution)/shard_map/ppermute | solution.py:325
  3.1 0.8 copy-start.1
  3.9 4.7 %copy-start.8 = (bf16[1,128,4096]{2,1,0:T(8,128)(2,1)S(1)}, bf16[1,128,4096]{2,1,0:T(8,128)(2,1)}, u32[]{:S(2)}) copy-start(bf16[1,128,4096]{2,1,0:T(8,128)(2,1)} %param.7) | copy-start | bytes 3145732
  3.9 21.2 %copy-start.3 = (bf16[512,1024]{1,0:T(8,128)(2,1)S(1)}, bf16[512,1024]{1,0:T(8,128)(2,1)}, u32[]{:S(2)}) copy-start(bf16[512,1024]{1,0:T(8,128)(2,1)} %refs_4_.1) | copy-start | bytes 3145732
  7.8 0.8 copy-start.6
  9.4 7.8 %collective-permute-start = (bf16[128,1024]{1,0:T(8,128)(2,1)S(1)}, bf16[128,1024]{1,0:T(8,128)(2,1)S(1)}, u32[]{:S(2)}, u32[]{:S(2)}) collective-permute-start(bf16[128,1024]{1,0:T(8,128)(2,1)S(1)} %get-tuple-element.33), channel_id=1, source_target_pairs={{0,128},{16,144},{32,160},{48,176},{64,192},{80,208},{96,224},{112... | collective-permute-start | bytes 786440 | tf_op jit(solution)/shard_map/ppermute | solution.py:332
  9.5 19.9 %collective-permute-start.4 = (bf16[128,2048]{1,0:T(8,128)(2,1)}, bf16[128,2048]{1,0:T(8,128)(2,1)}, u32[]{:S(2)}, u32[]{:S(2)}) collective-permute-start(bf16[128,2048]{1,0:T(8,128)(2,1)} %get-tuple-element.37), channel_id=1, source_target_pairs={{0,2},{1,3},{2,4},{3,5},{4,6},{5,7},{6,0},{7,1},{8,10},{9,11},{10,... | collective-permute-start | bytes 1572872 | tf_op jit(solution)/shard_map/ppermute | solution.py:329
  11.0 23.8 %collective-permute-start.5 = (bf16[128,2048]{1,0:T(8,128)(2,1)}, bf16[128,2048]{1,0:T(8,128)(2,1)}, u32[]{:S(2)}, u32[]{:S(2)}) collective-permute-start(bf16[128,2048]{1,0:T(8,128)(2,1)} %get-tuple-element.38), channel_id=1, source_target_pairs={{0,6},{1,7},{2,0},{3,1},{4,2},{5,3},{6,4},{7,5},{8,14},{9,15},{10,... | collective-permute-start | bytes 1572872 | tf_op jit(solution)/shard_map/ppermute | solution.py:330
  12.7 23.8 %collective-permute-start.6 = (bf16[128,2048]{1,0:T(8,128)(2,1)}, bf16[128,2048]{1,0:T(8,128)(2,1)}, u32[]{:S(2)}, u32[]{:S(2)}) collective-permute-start(bf16[128,2048]{1,0:T(8,128)(2,1)} %get-tuple-element.39), channel_id=1, source_target_pairs={{0,4},{1,5},{2,6},{3,7},{4,0},{5,1},{6,2},{7,3},{8,12},{9,13},{10,... | collective-permute-start | bytes 1572872 | tf_op jit(solution)/shard_map/ppermute | solution.py:328
  17.1 0.7 copy-start.11
  17.1 8.0 %collective-permute-start.1 = (bf16[128,1024]{1,0:T(8,128)(2,1)S(1)}, bf16[128,1024]{1,0:T(8,128)(2,1)}, u32[]{:S(2)}, u32[]{:S(2)}) collective-permute-start(bf16[128,1024]{1,0:T(8,128)(2,1)S(1)} %get-tuple-element.34), channel_id=1, source_target_pairs={{0,144},{16,128},{32,176},{48,160},{64,208},{80,192},{96,240},{112... | collective-permute-start | bytes 786440 | tf_op jit(solution)/shard_map/ppermute | solution.py:333
  25.1 11.4 %collective-permute-start.2 = (bf16[512,1024]{1,0:T(8,128)(2,1)S(1)}, bf16[512,1024]{1,0:T(8,128)(2,1)S(1)}, u32[]{:S(2)}, u32[]{:S(2)}) collective-permute-start(bf16[512,1024]{1,0:T(8,128)(2,1)S(1)} %copy-done.3), channel_id=1, source_target_pairs={{0,1},{1,0},{2,3},{3,2},{4,5},{5,4},{6,7},{7,6},{8,9},{9,8},{10,11... | collective-permute-start | bytes 3145736 | tf_op jit(solution)/shard_map/ppermute | solution.py:334
  26.4 11.1 %collective-permute-start.8 = (bf16[512,1024]{1,0:T(8,128)(2,1)S(1)}, bf16[512,1024]{1,0:T(8,128)(2,1)}, u32[]{:S(2)}, u32[]{:S(2)}) collective-permute-start(bf16[512,1024]{1,0:T(8,128)(2,1)S(1)} %collective-permute-done.7.refs_6_), channel_id=1, source_target_pairs={{0,1},{1,0},{2,3},{3,2},{4,5},{5,4},{6,7},{7,6},{8,9},{9,8},{10,11... | collective-permute-start | bytes 3145736 | tf_op jit(solution)/shard_map/ppermute | solution.py:335
  27.0 9.5 %copy-start.13 = (s32[4]{0:T(128)}, s32[4]{0:T(128)S(1)}, u32[]{:S(2)}) copy-start(s32[4]{0:T(128)S(1)} %get-tuple-element.62) | copy-start | bytes 52
  27.0 9.5 %copy-start.15 = (s32[4]{0:T(128)}, s32[4]{0:T(128)S(1)}, u32[]{:S(2)}) copy-start(s32[4]{0:T(128)S(1)} %get-tuple-element.70) | copy-start | bytes 52
  27.0 9.5 %copy-start.17 = (s32[4]{0:T(128)}, s32[4]{0:T(128)S(1)}, u32[]{:S(2)}) copy-start(s32[4]{0:T(128)S(1)} %get-tuple-element.71) | copy-start | bytes 52
  29.4 30.2 %copy-start.2 = (f32[1024]{0:T(1024)S(1)}, f32[1024]{0:T(1024)}, u32[]{:S(2)}) copy-start(f32[1024]{0:T(1024)} %param.9) | copy-start | bytes 12292
  36.5 1.0 copy-start.4
  37.5 1.2 %copy-start.5 = (bf16[512,1024]{1,0:T(8,128)(2,1)S(1)}, bf16[512,1024]{1,0:T(8,128)(2,1)}, u32[]{:S(2)}) copy-start(bf16[512,1024]{1,0:T(8,128)(2,1)} %copy-done.4) | copy-start | bytes 3145732
  38.7 1.0 copy-start.7
  39.8 9.3 %copy-start.14 = (s32[4]{0:T(128)S(1)}, s32[4]{0:T(128)}, u32[]{:S(2)}) copy-start(s32[4]{0:T(128)} %copy-done.13) | copy-start | bytes 52
  39.8 9.3 %copy-start.16 = (s32[4]{0:T(128)S(1)}, s32[4]{0:T(128)}, u32[]{:S(2)}) copy-start(s32[4]{0:T(128)} %copy-done.15) | copy-start | bytes 52
  39.8 9.3 %copy-start.18 = (s32[4]{0:T(128)S(1)}, s32[4]{0:T(128)}, u32[]{:S(2)}) copy-start(s32[4]{0:T(128)} %copy-done.17) | copy-start | bytes 52
  39.8 9.3 %copy-start.10 = (f32[128,64]{1,0:T(8,128)S(1)}, f32[128,64]{1,0:T(8,128)}, u32[]{:S(2)}) copy-start(f32[128,64]{1,0:T(8,128)} %get-tuple-element.69) | copy-start | bytes 98308
  44.6 31.5 %copy-start.9 = (bf16[1,128,1024]{2,1,0:T(8,128)(2,1)S(1)}, bf16[1,128,1024]{2,1,0:T(8,128)(2,1)}, u32[]{:S(2)}) copy-start(bf16[1,128,1024]{2,1,0:T(8,128)(2,1)} %get-tuple-element.63) | copy-start | bytes 786436
  44.6 31.5 %copy-start.12 = (bf16[128,1024]{1,0:T(8,128)(2,1)S(1)}, bf16[128,1024]{1,0:T(8,128)(2,1)}, u32[]{:S(2)}) copy-start(bf16[128,1024]{1,0:T(8,128)(2,1)} %copy-done.11) | copy-start | bytes 786436
  44.6 9.5 %collective-permute-start.9 = (bf16[128,1024]{1,0:T(8,128)(2,1)}, bf16[128,1024]{1,0:T(8,128)(2,1)S(1)}, u32[]{:S(2)}, u32[]{:S(2)}) collective-permute-start(bf16[128,1024]{1,0:T(8,128)(2,1)} %get-tuple-element.42), channel_id=1, source_target_pairs={{0,6},{1,7},{2,0},{3,1},{4,2},{5,3},{6,4},{7,5},{8,14},{9,15},{10,... | collective-permute-start | bytes 786440 | tf_op jit(solution)/shard_map/ppermute | solution.py:341
  46.6 12.9 %collective-permute-start.10 = (bf16[128,1024]{1,0:T(8,128)(2,1)}, bf16[128,1024]{1,0:T(8,128)(2,1)S(1)}, u32[]{:S(2)}, u32[]{:S(2)}) collective-permute-start(bf16[128,1024]{1,0:T(8,128)(2,1)} %get-tuple-element.43), channel_id=1, source_target_pairs={{0,2},{1,3},{2,4},{3,5},{4,6},{5,7},{6,0},{7,1},{8,10},{9,11},{10,... | collective-permute-start | bytes 786440 | tf_op jit(solution)/shard_map/ppermute | solution.py:341
  46.7 12.9 %collective-permute-start.11 = (bf16[128,1024]{1,0:T(8,128)(2,1)}, bf16[128,1024]{1,0:T(8,128)(2,1)S(1)}, u32[]{:S(2)}, u32[]{:S(2)}) collective-permute-start(bf16[128,1024]{1,0:T(8,128)(2,1)} %get-tuple-element.44), channel_id=1, source_target_pairs={{0,4},{1,5},{2,6},{3,7},{4,0},{5,1},{6,2},{7,3},{8,12},{9,13},{10,... | collective-permute-start | bytes 786440 | tf_op jit(solution)/shard_map/ppermute | solution.py:341
  49.2 26.9 %collective-permute-start.3 = (bf16[128,1024]{1,0:T(8,128)(2,1)S(1)}, bf16[128,1024]{1,0:T(8,128)(2,1)S(1)}, u32[]{:S(2)}, u32[]{:S(2)}) collective-permute-start(bf16[128,1024]{1,0:T(8,128)(2,1)S(1)} %get-tuple-element.36), channel_id=1, source_target_pairs={{0,16},{16,0},{32,48},{48,32},{64,80},{80,64},{96,112},{112,96},{1... | collective-permute-start | bytes 786440 | tf_op jit(solution)/shard_map/ppermute | solution.py:336
  59.9 4.4 %collective-permute-start.12 = (bf16[128,256]{1,0:T(8,128)(2,1)S(1)}, bf16[128,256]{1,0:T(8,128)(2,1)S(1)}, u32[]{:S(2)}, u32[]{:S(2)}) collective-permute-start(bf16[128,256]{1,0:T(8,128)(2,1)S(1)} %get-tuple-element.46), channel_id=1, source_target_pairs={{0,16},{16,0},{32,48},{48,32},{64,80},{80,64},{96,112},{112,96},{1... | collective-permute-start | bytes 196616 | tf_op jit(solution)/shard_map/ppermute | solution.py:345
  60.1 4.4 %collective-permute-start.13 = (bf16[128,256]{1,0:T(8,128)(2,1)S(1)}, bf16[128,256]{1,0:T(8,128)(2,1)S(1)}, u32[]{:S(2)}, u32[]{:S(2)}) collective-permute-start(bf16[128,256]{1,0:T(8,128)(2,1)S(1)} %get-tuple-element.47), channel_id=1, source_target_pairs={{0,128},{16,144},{32,160},{48,176},{64,192},{80,208},{96,224},{112... | collective-permute-start | bytes 196616 | tf_op jit(solution)/shard_map/ppermute | solution.py:345
  61.9 5.2 %collective-permute-start.14 = (bf16[128,256]{1,0:T(8,128)(2,1)S(1)}, bf16[128,256]{1,0:T(8,128)(2,1)S(1)}, u32[]{:S(2)}, u32[]{:S(2)}) collective-permute-start(bf16[128,256]{1,0:T(8,128)(2,1)S(1)} %get-tuple-element.48), channel_id=1, source_target_pairs={{0,144},{16,128},{32,176},{48,160},{64,208},{80,192},{96,240},{112... | collective-permute-start | bytes 196616 | tf_op jit(solution)/shard_map/ppermute | solution.py:345
  67.1 16.6 %collective-permute-start.17 = (bf16[512,256]{1,0:T(8,128)(2,1)S(1)}, bf16[512,256]{1,0:T(8,128)(2,1)S(1)}, u32[]{:S(2)}, u32[]{:S(2)}) collective-permute-start(bf16[512,256]{1,0:T(8,128)(2,1)S(1)} %constant_dynamic-update-slice_fusion.kv_ref), channel_id=1, source_target_pairs={{0,96},{16,112},{32,0},{48,16},{64,32},{80,48},{96,64},{112,80},{1... | collective-permute-start | bytes 786440 | tf_op jit(solution)/shard_map/ppermute | solution.py:348
  76.0 14.1 %collective-permute-start.15 = (bf16[512,256]{1,0:T(8,128)(2,1)S(1)}, bf16[512,256]{1,0:T(8,128)(2,1)S(1)}, u32[]{:S(2)}, u32[]{:S(2)}) collective-permute-start(bf16[512,256]{1,0:T(8,128)(2,1)S(1)} %constant_dynamic-update-slice_fusion.kv_ref), channel_id=1, source_target_pairs={{0,32},{16,48},{32,64},{48,80},{64,96},{80,112},{96,0},{112,16},{1... | collective-permute-start | bytes 786440 | tf_op jit(solution)/shard_map/ppermute | solution.py:347
  83.7 9.7 %collective-permute-start.18 = (bf16[256,256]{1,0:T(8,128)(2,1)S(1)}, bf16[256,256]{1,0:T(8,128)(2,1)S(1)}, u32[]{:S(2)}, u32[]{:S(2)}) collective-permute-start(bf16[256,256]{1,0:T(8,128)(2,1)S(1)} %slice.13), channel_id=1, source_target_pairs={{0,96},{16,112},{32,0},{48,16},{64,32},{80,48},{96,64},{112,80},{1... | collective-permute-start | bytes 393224 | tf_op jit(solution)/shard_map/ppermute | solution.py:350
  90.1 8.7 %collective-permute-start.16 = (bf16[256,256]{1,0:T(8,128)(2,1)S(1)}, bf16[256,256]{1,0:T(8,128)(2,1)S(1)}, u32[]{:S(2)}, u32[]{:S(2)}) collective-permute-start(bf16[256,256]{1,0:T(8,128)(2,1)S(1)} %slice.12), channel_id=1, source_target_pairs={{0,32},{16,48},{32,64},{48,80},{64,96},{80,112},{96,0},{112,16},{1... | collective-permute-start | bytes 393224 | tf_op jit(solution)/shard_map/ppermute | solution.py:349
  101.7 6.5 %collective-permute-start.19 = (bf16[128,1024]{1,0:T(8,128)(2,1)S(1)}, bf16[128,1024]{1,0:T(8,128)(2,1)S(1)}, u32[]{:S(2)}, u32[]{:S(2)}) collective-permute-start(bf16[128,1024]{1,0:T(8,128)(2,1)S(1)} %get-tuple-element.56), channel_id=1, source_target_pairs={{0,16},{16,0},{32,48},{48,32},{64,80},{80,64},{96,112},{112,96},{1... | collective-permute-start | bytes 786440 | tf_op jit(solution)/shard_map/ppermute | solution.py:381
  102.5 9.2 %collective-permute-start.20 = (bf16[128,1024]{1,0:T(8,128)(2,1)S(1)}, bf16[128,1024]{1,0:T(8,128)(2,1)S(1)}, u32[]{:S(2)}, u32[]{:S(2)}) collective-permute-start(bf16[128,1024]{1,0:T(8,128)(2,1)S(1)} %get-tuple-element.57), channel_id=1, source_target_pairs={{0,128},{16,144},{32,160},{48,176},{64,192},{80,208},{96,224},{112... | collective-permute-start | bytes 786440 | tf_op jit(solution)/shard_map/ppermute | solution.py:381
  103.4 8.2 %collective-permute-start.21 = (bf16[128,1024]{1,0:T(8,128)(2,1)S(1)}, bf16[128,1024]{1,0:T(8,128)(2,1)S(1)}, u32[]{:S(2)}, u32[]{:S(2)}) collective-permute-start(bf16[128,1024]{1,0:T(8,128)(2,1)S(1)} %get-tuple-element.58), channel_id=1, source_target_pairs={{0,144},{16,128},{32,176},{48,160},{64,208},{80,192},{96,240},{112... | collective-permute-start | bytes 786440 | tf_op jit(solution)/shard_map/ppermute | solution.py:381

commit v6 on v4

--- a/solution.py
+++ b/solution.py
@@ -42,7 +42,7 @@
     return pl.multiple_of(src, 512)
 
 
-def norm_kernel(pos_ref, x_hbm, gain_hbm, out0, out1, out2, out3, x_ref, gain_ref, sems):
+def norm_kernel(pos_ref, x_hbm, gain_hbm, q_hbm, out0, out1, out2, out3, q0, q1, q2, q3, x_ref, gain_ref, sems):
     step = 32
     count = x_ref.shape[0] // step
     copies = [
@@ -56,6 +56,11 @@
     gain_copy.start()
     for copy in copies[1:]:
         copy.start()
+    q_copies = []
+    for k, out in ((2, q2), (3, q3), (1, q1), (0, q0)):
+        cols = pl.ds(pl.multiple_of((pos_ref[3] ^ k) * GW, GW), GW)
+        q_copies.append(pltpu.make_async_copy(q_hbm.at[:, cols], out, sems.at[count + 1 + k]))
+        q_copies[-1].start()
     for n in range(count):
         copies[n].wait()
         if n == 0:
@@ -72,26 +77,28 @@
                 cols = pl.ds(part_column(pos_ref, k, i), 512)
                 wide = x_ref[rows, cols].astype(F32)
                 out[rows, i * 512 : (i + 1) * 512] = (wide * inv * gain_ref[:, cols]).astype(BF)
-
-
-def norm_call(pos, hidden, gain):
+    for copy in q_copies:
+        copy.wait()
+
+
+def norm_call(pos, hidden, gain, q):
     rows = hidden.shape[0]
     vm = pl.BlockSpec(memory_space=pltpu.VMEM)
     hbm = pl.BlockSpec(memory_space=pl.ANY)
     return pl.pallas_call(
         norm_kernel,
-        in_specs=[pl.BlockSpec(memory_space=pltpu.SMEM), hbm, hbm],
-        out_specs=[vm] * 4,
-        out_shape=[jax.ShapeDtypeStruct((rows, D // 4), BF)] * 4,
+        in_specs=[pl.BlockSpec(memory_space=pltpu.SMEM), hbm, hbm, hbm],
+        out_specs=[vm] * 8,
+        out_shape=[jax.ShapeDtypeStruct((rows, D // 4), BF)] * 4 + [jax.ShapeDtypeStruct((rows, GW), BF)] * 4,
         scratch_shapes=[
             pltpu.VMEM((rows, D), BF),
             pltpu.VMEM((1, D), F32),
-            pltpu.SemaphoreType.DMA((rows // 32 + 1,)),
+            pltpu.SemaphoreType.DMA((rows // 32 + 5,)),
         ],
         compiler_params=pltpu.CompilerParams(vmem_limit_bytes=50 * 1024 * 1024),
         cost_estimate=pl.CostEstimate(flops=4 << 20, bytes_accessed=4 << 20, transcendentals=0),
         name="norm",
-    )(pos, hidden, gain)
+    )(pos, hidden, gain, q)
 
 
 def product_kernel(count, *refs):
@@ -277,23 +284,30 @@
     )(flags, *arrays)
 
 
-def place_kernel(j_ref, *refs):
-    out_ref = refs[-1]
-    for k in range(4):
+def place_kernel(members, j_ref, *refs):
+    parts, out_ref, sems = refs[: len(members)], refs[-2], refs[-1]
+    copies = []
+    for i, k in enumerate(members):
         cols = pl.ds(pl.multiple_of((j_ref[0] ^ k) * GW, GW), GW)
-        out_ref[:, cols] = refs[k][...]
-
-
-def place_call(j, parts):
+        copies.append(pltpu.make_async_copy(parts[i], out_ref.at[:, cols], sems.at[i]))
+        copies[-1].start()
+    for copy in copies:
+        copy.wait()
+
+
+def place_call(j, parts, members, out=None):
     vm = pl.BlockSpec(memory_space=pltpu.VMEM)
+    hbm = pl.BlockSpec(memory_space=pl.ANY)
     return pl.pallas_call(
-        place_kernel,
-        in_specs=[pl.BlockSpec(memory_space=pltpu.SMEM)] + [vm] * 4,
-        out_specs=vm,
+        lambda *refs: place_kernel(members, *refs),
+        in_specs=[pl.BlockSpec(memory_space=pltpu.SMEM)] + [vm] * len(parts) + ([] if out is None else [hbm]),
+        out_specs=hbm,
         out_shape=jax.ShapeDtypeStruct((BLK, H * HD), BF),
+        scratch_shapes=[pltpu.SemaphoreType.DMA((len(members),))],
+        input_output_aliases={} if out is None else {1 + len(parts): 0},
         compiler_params=pltpu.CompilerParams(vmem_limit_bytes=8 * 1024 * 1024),
         name="place",
-    )(j, *parts)
+    )(j, *parts, *([] if out is None else [out]))
 
 
 def rotary_tables(start, count):
@@ -320,16 +334,15 @@
     q = queries.reshape(BLK, H * HD)
     j1 = jnp.reshape(j, (1,))
 
-    pos = jnp.stack([xi, yhi, core])
+    pos = jnp.stack([xi, yhi, core, j])
     gain = norm_gain.reshape(1, D)
     w_y = lax.ppermute(kv_weight, ("ctx", "fsdp"), DIAG_PAIRS)
 
-    normed0, normed1, normed2, normed3 = norm_call(pos, hidden, gain)
+    normed0, normed1, normed2, normed3, *q_parts = norm_call(pos, hidden, gain, q)
     n2 = lax.ppermute(normed2, "fsdp", x_pairs(2))
     n1 = lax.ppermute(normed1, "fsdp", x_pairs(1))
     n3 = lax.ppermute(normed3, "fsdp", x_pairs(3))
-    q_parts = [lax.dynamic_slice(q, (0, (j ^ k) * GW), (BLK, GW)) for k in range(4)]
-    q_parts[2] = lax.ppermute(after(q_parts[2], normed0), "ctx", member_pairs(2))
+    q_parts[2] = lax.ppermute(q_parts[2], "ctx", member_pairs(2))
     q_parts[3] = lax.ppermute(after(q_parts[3], q_parts[2]), "ctx", member_pairs(3))
     w_core = lax.ppermute(after(kv_weight, q_parts[3]), "fsdp", CORE_PAIRS)
     w_yc = lax.ppermute(after(w_y, q_parts[3]), "fsdp", CORE_PAIRS)
@@ -379,8 +392,10 @@
 
     top, acc, out2, out3 = finish(1, top, acc, "attend_others")
     top, acc, out0, out1 = finish(0, top, acc, "attend_own")
-    parts = [out0] + [lax.ppermute(o, "ctx", member_pairs(k)) for k, o in ((1, out1), (2, out2), (3, out3))]
-    return place_call(j1, parts).reshape(1, BLK, H * HD)
+    got = [lax.ppermute(o, "ctx", member_pairs(k)) for k, o in ((3, out3), (2, out2), (1, out1))]
+    placed = place_call(j1, [out0, got[2]], (0, 1))
+    placed = place_call(j1, [got[1]], (2,), placed)
+    return place_call(j1, [got[0]], (3,), placed).reshape(1, BLK, H * HD)
 
 
 def solution(mesh):

time: 105 us -> 105 us (level)
  Pallas kernels: 21.4 us -> 22.6 us
    pallas_call x1 -> x3, Pallas kernels: 1.04 us -> 2.23 us  [place_call(): pl.pallas_call(lambda *refs: place_kernel(members, *refs), in_specs=[pl.B...]
  transfers between devices with their start and end apart: 22 -> 22, of which waited for: 14 -> 14; matrix products, arithmetic and copies ran while one was open for 4% -> 3% of each run, Pallas kernels for 17% -> 18%
where the time goes in v6:
time: 105 us; the launch traced here: 104 us
  waiting for transfers between devices  40.9 us (39%)
  starting transfers between devices  34.9 us (33%)
  Pallas kernels  22.6 us (22%)
  local copies, waits for them, and re-layouts  3.7 us (4%)
  other arithmetic  1.95 us (2%)
    pallas_call x4, Pallas kernels, attend_call(): pl.pallas_call(kernel, in_specs=[pl.BlockSpec(memory_space=pltpu.SMEM)] +...  9.13 us
    ppermute x1, starting transfers between devices, on_device(): down = lax.ppermute(group, 'ctx', z_pairs(-2))  8.39 us
    ppermute x1, waiting for transfers between devices, on_device(): lax.ppermute(after(q_parts[3], q_parts[2]), 'ctx', member_pairs(3))  7.25 us
    pallas_call x3, Pallas kernels, product_call(): pl.pallas_call(lambda *refs: product_kernel(count, *refs), in_specs=[vm]...  6.95 us
    ppermute x3, waiting for transfers between devices, on_device(): lax.ppermute(o, 'ctx', member_pairs(k))  6.81 us
    ppermute x1, waiting for transfers between devices, on_device(): n3 = lax.ppermute(normed3, 'fsdp', x_pairs(3))  6.74 us
    ppermute x3, starting transfers between devices, on_device(): lax.ppermute(p, 'fsdp', x_pairs(k))  5.5 us
    ppermute x1, starting transfers between devices, on_device(): far1 = lax.ppermute(down[256:], 'ctx', z_pairs(-2))  4.72 us
  transfers between devices with their start and end apart: 22, of which 14 were waited for; matrix products, arithmetic and copies ran while one was open for 3% of the time, Pallas kernels for 18%

profile of v6, /device:TPU:32, one launch (start us, length us, event | category | flops | bytes accessed | tf_op | source)
XLA Modules:
  0.0 104.4 jit_solution(11234559339499596907)
XLA Ops:
  0.0 3.0 %collective-permute-start.4 = (bf16[512,1024]{1,0:T(8,128)(2,1)}, bf16[512,1024]{1,0:T(8,128)(2,1)S(1)}, u32[]{:S(2)}, u32[]{:S(2)}) collective-permute-start(bf16[512,1024]{1,0:T(8,128)(2,1)} %refs_1_.3), channel_id=1, source_target_pairs={{0,136},{1,137},{2,138},{3,139},{4,140},{5,141},{6,142},{7,143},{8... | collective-permute-start | bytes 3145736 | tf_op jit(solution)/shard_map/ppermute | solution.py:339
  3.1 0.8 copy-done.4
  3.9 3.9 %norm.1 = (bf16[128,2048]{1,0:T(8,128)(2,1)S(1)}, bf16[128,2048]{1,0:T(8,128)(2,1)}, bf16[128,2048]{1,0:T(8,128)(2,1)}, bf16[128,2048]{1,0:T(8,128)(2,1)}, bf16[...) custom-call(s32[4]{0:T(128)S(1)} %pad_add_fusion.1.pos_ref, ...), custom_call_target="tpu_custom_call" | custom-call | flops 4194304 | bytes 4194304 | tf_op jit(solution)/shard_map/norm/pallas_call | solution.py:88
  7.8 0.8 copy-done.2
  8.6 0.7 copy-done.6
  9.3 0.1 collective-permute-start
  9.4 1.5 %collective-permute-start.6 = (bf16[128,2048]{1,0:T(8,128)(2,1)}, bf16[128,2048]{1,0:T(8,128)(2,1)}, u32[]{:S(2)}, u32[]{:S(2)}) collective-permute-start(bf16[128,2048]{1,0:T(8,128)(2,1)} %get-tuple-element.42), channel_id=1, source_target_pairs={{0,2},{1,3},{2,4},{3,5},{4,6},{5,7},{6,0},{7,1},{8,10},{9,11},{10,... | collective-permute-start | bytes 1572872 | tf_op jit(solution)/shard_map/ppermute | solution.py:343
  10.9 1.8 %collective-permute-start.7 = (bf16[128,2048]{1,0:T(8,128)(2,1)}, bf16[128,2048]{1,0:T(8,128)(2,1)}, u32[]{:S(2)}, u32[]{:S(2)}) collective-permute-start(bf16[128,2048]{1,0:T(8,128)(2,1)} %get-tuple-element.43), channel_id=1, source_target_pairs={{0,6},{1,7},{2,0},{3,1},{4,2},{5,3},{6,4},{7,5},{8,14},{9,15},{10,... | collective-permute-start | bytes 1572872 | tf_op jit(solution)/shard_map/ppermute | solution.py:344
  12.7 1.8 %collective-permute-start.10 = (bf16[128,2048]{1,0:T(8,128)(2,1)}, bf16[128,2048]{1,0:T(8,128)(2,1)}, u32[]{:S(2)}, u32[]{:S(2)}) collective-permute-start(bf16[128,2048]{1,0:T(8,128)(2,1)} %get-tuple-element.46), channel_id=1, source_target_pairs={{0,4},{1,5},{2,6},{3,7},{4,0},{5,1},{6,2},{7,3},{8,12},{9,13},{10,... | collective-permute-start | bytes 1572872 | tf_op jit(solution)/shard_map/ppermute | solution.py:342
  14.5 2.6 %collective-permute-done = bf16[128,1024]{1,0:T(8,128)(2,1)S(1)} collective-permute-done((bf16[128,1024]{1,0:T(8,128)(2,1)S(1)}, bf16[128,1024]{1,0:T(8,128)(2,1)S(1)}, u32[]{:S(2)}, u32[]{:S(2)}) %collective-permute-start) | collective-permute-done | bytes 262176 | tf_op jit(solution)/shard_map/ppermute | solution.py:345
  17.1 0.6 gather_fusion
  17.8 7.3 %collective-permute-done.1 = bf16[128,1024]{1,0:T(8,128)(2,1)} collective-permute-done((bf16[128,1024]{1,0:T(8,128)(2,1)S(1)}, bf16[128,1024]{1,0:T(8,128)(2,1)}, u32[]{:S(2)}, u32[]{:S(2)}) %collective-permute-start.1) | collective-permute-done | bytes 262176 | tf_op jit(solution)/shard_map/ppermute | solution.py:346
  25.0 1.4 %collective-permute-done.4.refs_3_.refs_4_ = bf16[512,1024]{1,0:T(8,128)(2,1)S(1)} collective-permute-done((bf16[512,1024]{1,0:T(8,128)(2,1)}, bf16[512,1024]{1,0:T(8,128)(2,1)S(1)}, u32[]{:S(2)}, u32[]{:S(2)}) %collective-permute-start.4) | collective-permute-done | bytes 1048608 | tf_op jit(solution)/shard_map/ppermute | solution.py:339
  26.7 0.6 gather_fusion.1
  27.4 0.3 fusion
  27.7 6.7 %collective-permute-done.7.refs_1_ = bf16[128,2048]{1,0:T(8,128)(2,1)} collective-permute-done((bf16[128,2048]{1,0:T(8,128)(2,1)}, bf16[128,2048]{1,0:T(8,128)(2,1)}, u32[]{:S(2)}, u32[]{:S(2)}) %collective-permute-start.7) | collective-permute-done | bytes 524320 | tf_op jit(solution)/shard_map/ppermute | solution.py:344
  34.4 2.8 %products.1 = (bf16[128,1024]{1,0:T(8,128)(2,1)S(1)}, bf16[128,1024]{1,0:T(8,128)(2,1)S(1)}) custom-call(bf16[128,2048]{1,0:T(8,128)(2,1)} %collective-permute-done.6.refs_0_, bf16[128,2048]{1,0:T(8,128)(2,1)} %collective-permute-done.7.refs_1_, bf16[512,1024]{1,0:T(8,128)(2,1)S(1)} %copy-done.1, ...), custom_call_target="tpu_custom_call" | custom-call | flops 1073741824 | bytes 4194304 | tf_op jit(solution)/shard_map/products/pallas_call | solution.py:117
  37.2 3.9 %collective-permute-start.8 = (bf16[128,1024]{1,0:T(8,128)(2,1)S(1)}, bf16[128,1024]{1,0:T(8,128)(2,1)S(1)}, u32[]{:S(2)}, u32[]{:S(2)}) collective-permute-start(bf16[128,1024]{1,0:T(8,128)(2,1)S(1)} %get-tuple-element.44), channel_id=1, source_target_pairs={{0,6},{1,7},{2,0},{3,1},{4,2},{5,3},{6,4},{7,5},{8,14},{9,15},{10,... | collective-permute-start | bytes 786440 | tf_op jit(solution)/shard_map/ppermute | solution.py:355
  41.2 2.2 %far_product.1 = bf16[128,1024]{1,0:T(8,128)(2,1)S(1)} custom-call(bf16[128,2048]{1,0:T(8,128)(2,1)} %collective-permute-done.10.refs_0_, bf16[512,1024]{1,0:T(8,128)(2,1)S(1)} %copy-done.1, bf16[512,1024]{1,0:T(8,128)(2,1)S(1)} %collective-permute-done.2.refs_2_.refs_3_, bf16[512,1024]{1,0:T(8,128)(2,1)S(1)} %collective-permute-done.4.refs_3_.refs_4_, ...), custom_call_target="tpu_custom_call" | custom-call | flops 536870912 | bytes 4194304 | tf_op jit(solution)/shard_map/far_product/pallas_call | solution.py:117
  43.4 1.6 %collective-permute-start.11 = (bf16[128,1024]{1,0:T(8,128)(2,1)S(1)}, bf16[128,1024]{1,0:T(8,128)(2,1)S(1)}, u32[]{:S(2)}, u32[]{:S(2)}) collective-permute-start(bf16[128,1024]{1,0:T(8,128)(2,1)S(1)} %far_product.1), channel_id=1, source_target_pairs={{0,4},{1,5},{2,6},{3,7},{4,0},{5,1},{6,2},{7,3},{8,12},{9,13},{10,... | collective-permute-start | bytes 786440 | tf_op jit(solution)/shard_map/ppermute | solution.py:355
  45.2 0.2 collective-permute-start.3
  45.4 2.0 %own_product.1.own_ref = f32[128,1024]{1,0:T(8,128)S(1)} custom-call(bf16[128,2048]{1,0:T(8,128)(2,1)S(1)} %copy-done.3, bf16[512,1024]{1,0:T(8,128)(2,1)S(1)} %copy-done.1, bf16[512,1024]{1,0:T(8,128)(2,1)S(1)} %collective-permute-done.2.refs_2_.refs_3_, bf16[512,1024]{1,0:T(8,128)(2,1)S(1)} %collective-permute-done.4.refs_3_.refs_4_, ...), custom_call_target="tpu_custom_call" | custom-call | flops 536870912 | bytes 4194304 | tf_op jit(solution)/shard_map/own_product/pallas_call | solution.py:117
  47.3 4.2 %collective-permute-done.9.r3_ref = bf16[128,1024]{1,0:T(8,128)(2,1)S(1)} collective-permute-done((bf16[128,1024]{1,0:T(8,128)(2,1)S(1)}, bf16[128,1024]{1,0:T(8,128)(2,1)S(1)}, u32[]{:S(2)}, u32[]{:S(2)}) %collective-permute-start.9) | collective-permute-done | bytes 262176 | tf_op jit(solution)/shard_map/ppermute | solution.py:355
  51.6 0.4 keys_values.1
  51.9 0.4 collective-permute-start.12
  52.3 0.7 collective-permute-start.13
  53.0 2.6 %collective-permute-start.14 = (bf16[128,256]{1,0:T(8,128)(2,1)S(1)}, bf16[128,256]{1,0:T(8,128)(2,1)S(1)}, u32[]{:S(2)}, u32[]{:S(2)}) collective-permute-start(bf16[128,256]{1,0:T(8,128)(2,1)S(1)} %get-tuple-element.50), channel_id=1, source_target_pairs={{0,144},{16,128},{32,176},{48,160},{64,208},{80,192},{96,240},{112... | collective-permute-start | bytes 196616 | tf_op jit(solution)/shard_map/ppermute | solution.py:360
  55.7 0.8 collective-permute-done.12
  56.6 1.6 %collective-permute-done.14 = bf16[128,256]{1,0:T(8,128)(2,1)S(1)} collective-permute-done((bf16[128,256]{1,0:T(8,128)(2,1)S(1)}, bf16[128,256]{1,0:T(8,128)(2,1)S(1)}, u32[]{:S(2)}, u32[]{:S(2)}) %collective-permute-start.14) | collective-permute-done | bytes 65568 | tf_op jit(solution)/shard_map/ppermute | solution.py:360
  58.2 8.4 %collective-permute-start.17 = (bf16[512,256]{1,0:T(8,128)(2,1)S(1)}, bf16[512,256]{1,0:T(8,128)(2,1)S(1)}, u32[]{:S(2)}, u32[]{:S(2)}) collective-permute-start(bf16[512,256]{1,0:T(8,128)(2,1)S(1)} %constant_dynamic-update-slice_fusion.kv_ref), channel_id=1, source_target_pairs={{0,96},{16,112},{32,0},{48,16},{64,32},{80,48},{96,64},{112,80},{1... | collective-permute-start | bytes 786440 | tf_op jit(solution)/shard_map/ppermute | solution.py:363
  66.7 1.1 %pad_maximum_fusion.q_ref.refs_1_ = bf16[4,128,1024]{2,1,0:T(8,128)(2,1)S(1)} fusion(bf16[1,128,1024]{2,1,0:T(8,128)(2,1)} %bitcast.18, bf16[1,128,1024]{2,1,0:T(8,128)(2,1)S(1)} %bitcast.33, bf16[1,128,1024]{2,1,0:T(8,128)(2,1)S(1)} %bitcast.34, bf16[1,128,1024]{2,1,0:T(8,128)(2,1)S(1)} %bitcast.28), kind=kLoop, calls=%fused_computation.2 | loop fusion | flops 1572864 | bytes 2097152 | tf_op jit(solution)/shard_map/stack | solution.py:350
  67.8 3.3 %attend_first.1 = (f32[4,1024,128]{2,1,0:T(8,128)S(1)}, f32[4,1024,256]{2,1,0:T(8,128)S(1)}) custom-call(s32[4,16]{1,0:T(4,128)S(1)} %select_select_fusion.flag_ref.refs_0_, bf16[4,128,1024]{2,1,0:T(8,128)(2,1)S(1)} %pad_maximum_fusion.q_ref.refs_1_, bf16[512,256]{1,0:T(8,128)(2,1)S(1)} %constant_dynamic-update-slice_fusion.kv_ref), custom_call_target="tpu_custom_call" | custom-call | flops 1073741824 | bytes 4194304 | tf_op jit(solution)/shard_map/attend_first/pallas_call | solution.py:275
  71.1 4.3 %collective-permute-done.17.down_ref = bf16[512,256]{1,0:T(8,128)(2,1)S(1)} collective-permute-done((bf16[512,256]{1,0:T(8,128)(2,1)S(1)}, bf16[512,256]{1,0:T(8,128)(2,1)S(1)}, u32[]{:S(2)}, u32[]{:S(2)}) %collective-permute-start.17) | collective-permute-done | bytes 262176 | tf_op jit(solution)/shard_map/ppermute | solution.py:363
  75.4 4.7 %collective-permute-start.18 = (bf16[256,256]{1,0:T(8,128)(2,1)S(1)}, bf16[256,256]{1,0:T(8,128)(2,1)S(1)}, u32[]{:S(2)}, u32[]{:S(2)}) collective-permute-start(bf16[256,256]{1,0:T(8,128)(2,1)S(1)} %slice.13), channel_id=1, source_target_pairs={{0,96},{16,112},{32,0},{48,16},{64,32},{80,48},{96,64},{112,80},{1... | collective-permute-start | bytes 393224 | tf_op jit(solution)/shard_map/ppermute | solution.py:365
  80.2 0.3 collective-permute-done.15.up_ref
  80.5 0.3 collective-permute-start.16
  80.8 3.0 %attend_more.1 = (f32[4,1024,128]{2,1,0:T(8,128)S(1)}, f32[4,1024,256]{2,1,0:T(8,128)S(1)}) custom-call(s32[4,16]{1,0:T(4,128)S(1)} %select_select_fusion.flag_ref.refs_0_, bf16[4,128,1024]{2,1,0:T(8,128)(2,1)S(1)} %pad_maximum_fusion.q_ref.refs_1_, ...), custom_call_target="tpu_custom_call", output_to_operand_aliasing={{0}: (4, {}), {1}: (5, {})} | custom-call | flops 3221225472 | bytes 4194304 | tf_op jit(solution)/shard_map/attend_more/pallas_call | solution.py:275
  83.8 0.2 collective-permute-done.18.refs_3_
  84.0 4.5 %collective-permute-done.16.refs_2_ = bf16[256,256]{1,0:T(8,128)(2,1)S(1)} collective-permute-done((bf16[256,256]{1,0:T(8,128)(2,1)S(1)}, bf16[256,256]{1,0:T(8,128)(2,1)S(1)}, u32[]{:S(2)}, u32[]{:S(2)}) %collective-permute-start.16) | collective-permute-done | bytes 131104 | tf_op jit(solution)/shard_map/ppermute | solution.py:364
  88.5 1.9 %attend_others.1 = (f32[4,1024,128]{2,1,0:T(8,128)S(1)}, f32[4,1024,256]{2,1,0:T(8,128)S(1)}, bf16[128,1024]{1,0:T(8,128)(2,1)S(1)}, bf16[128,1024]{1,0:T(8,128)(2,1)S(1)}) custom-call(s32[4,16]{1,0:T(4,128)S(1)} %select_select_fusion.flag_ref.refs_0_, ...), custom_call_target="tpu_custom_call", output_to_operand_aliasing={{0}: (4, {}), {1}: (5, {})} | custom-call | flops 1073741824 | bytes 4194304 | tf_op jit(solution)/shard_map/attend_others/pallas_call | solution.py:275
  90.3 1.0 attend_own.1
  91.4 2.2 %collective-permute-start.21 = (bf16[128,1024]{1,0:T(8,128)(2,1)S(1)}, bf16[128,1024]{1,0:T(8,128)(2,1)S(1)}, u32[]{:S(2)}, u32[]{:S(2)}) collective-permute-start(bf16[128,1024]{1,0:T(8,128)(2,1)S(1)} %get-tuple-element.60), channel_id=1, source_target_pairs={{0,16},{16,0},{32,48},{48,32},{64,80},{80,64},{96,112},{112,96},{1... | collective-permute-start | bytes 786440 | tf_op jit(solution)/shard_map/ppermute | solution.py:395
  93.6 1.4 %collective-permute-start.20 = (bf16[128,1024]{1,0:T(8,128)(2,1)S(1)}, bf16[128,1024]{1,0:T(8,128)(2,1)S(1)}, u32[]{:S(2)}, u32[]{:S(2)}) collective-permute-start(bf16[128,1024]{1,0:T(8,128)(2,1)S(1)} %get-tuple-element.56), channel_id=1, source_target_pairs={{0,128},{16,144},{32,160},{48,176},{64,192},{80,208},{96,224},{112... | collective-permute-start | bytes 786440 | tf_op jit(solution)/shard_map/ppermute | solution.py:395
  95.1 2.8 %collective-permute-done.21.refs_2_ = bf16[128,1024]{1,0:T(8,128)(2,1)S(1)} collective-permute-done((bf16[128,1024]{1,0:T(8,128)(2,1)S(1)}, bf16[128,1024]{1,0:T(8,128)(2,1)S(1)}, u32[]{:S(2)}, u32[]{:S(2)}) %collective-permute-start.21) | collective-permute-done | bytes 262176 | tf_op jit(solution)/shard_map/ppermute | solution.py:395
  97.9 0.8 place.3.refs_2_
  98.7 4.0 %collective-permute-done.20.refs_1_ = bf16[128,1024]{1,0:T(8,128)(2,1)S(1)} collective-permute-done((bf16[128,1024]{1,0:T(8,128)(2,1)S(1)}, bf16[128,1024]{1,0:T(8,128)(2,1)S(1)}, u32[]{:S(2)}, u32[]{:S(2)}) %collective-permute-start.20) | collective-permute-done | bytes 262176 | tf_op jit(solution)/shard_map/ppermute | solution.py:395
  102.8 0.7 place.4.refs_2_
  103.5 0.7 place.5
  (55 shorter events, 1.1 us)
Async XLA Ops:
  0.0 17.1 %copy-start = (s32[1,16,16]{2,1,0:T(8,128)S(1)}, s32[1,16,16]{2,1,0:T(8,128)}, u32[]{:S(2)}) copy-start(s32[1,16,16]{2,1,0:T(8,128)} %param.11) | copy-start | bytes 3076
  0.0 25.0 %copy-start.1 = (bf16[512,1024]{1,0:T(8,128)(2,1)S(1)}, bf16[512,1024]{1,0:T(8,128)(2,1)}, u32[]{:S(2)}) copy-start(bf16[512,1024]{1,0:T(8,128)(2,1)} %refs_1_.3) | copy-start | bytes 3145732
  0.0 26.4 %collective-permute-start.4 = (bf16[512,1024]{1,0:T(8,128)(2,1)}, bf16[512,1024]{1,0:T(8,128)(2,1)S(1)}, u32[]{:S(2)}, u32[]{:S(2)}) collective-permute-start(bf16[512,1024]{1,0:T(8,128)(2,1)} %refs_1_.3), channel_id=1, source_target_pairs={{0,136},{1,137},{2,138},{3,139},{4,140},{5,141},{6,142},{7,143},{8... | collective-permute-start | bytes 3145736 | tf_op jit(solution)/shard_map/ppermute | solution.py:339
  3.1 0.8 copy-start.4
  7.8 0.8 copy-start.2
  8.6 0.7 copy-start.6
  9.3 7.8 %collective-permute-start = (bf16[128,1024]{1,0:T(8,128)(2,1)S(1)}, bf16[128,1024]{1,0:T(8,128)(2,1)S(1)}, u32[]{:S(2)}, u32[]{:S(2)}) collective-permute-start(bf16[128,1024]{1,0:T(8,128)(2,1)S(1)} %get-tuple-element.36), channel_id=1, source_target_pairs={{0,128},{16,144},{32,160},{48,176},{64,192},{80,208},{96,224},{112... | collective-permute-start | bytes 786440 | tf_op jit(solution)/shard_map/ppermute | solution.py:345
  9.4 18.2 %collective-permute-start.6 = (bf16[128,2048]{1,0:T(8,128)(2,1)}, bf16[128,2048]{1,0:T(8,128)(2,1)}, u32[]{:S(2)}, u32[]{:S(2)}) collective-permute-start(bf16[128,2048]{1,0:T(8,128)(2,1)} %get-tuple-element.42), channel_id=1, source_target_pairs={{0,2},{1,3},{2,4},{3,5},{4,6},{5,7},{6,0},{7,1},{8,10},{9,11},{10,... | collective-permute-start | bytes 1572872 | tf_op jit(solution)/shard_map/ppermute | solution.py:343
  10.9 23.5 %collective-permute-start.7 = (bf16[128,2048]{1,0:T(8,128)(2,1)}, bf16[128,2048]{1,0:T(8,128)(2,1)}, u32[]{:S(2)}, u32[]{:S(2)}) collective-permute-start(bf16[128,2048]{1,0:T(8,128)(2,1)} %get-tuple-element.43), channel_id=1, source_target_pairs={{0,6},{1,7},{2,0},{3,1},{4,2},{5,3},{6,4},{7,5},{8,14},{9,15},{10,... | collective-permute-start | bytes 1572872 | tf_op jit(solution)/shard_map/ppermute | solution.py:344
  12.7 28.5 %collective-permute-start.10 = (bf16[128,2048]{1,0:T(8,128)(2,1)}, bf16[128,2048]{1,0:T(8,128)(2,1)}, u32[]{:S(2)}, u32[]{:S(2)}) collective-permute-start(bf16[128,2048]{1,0:T(8,128)(2,1)} %get-tuple-element.46), channel_id=1, source_target_pairs={{0,4},{1,5},{2,6},{3,7},{4,0},{5,1},{6,2},{7,3},{8,12},{9,13},{10,... | collective-permute-start | bytes 1572872 | tf_op jit(solution)/shard_map/ppermute | solution.py:342
  17.1 0.7 copy-start.8
  17.1 8.0 %collective-permute-start.1 = (bf16[128,1024]{1,0:T(8,128)(2,1)S(1)}, bf16[128,1024]{1,0:T(8,128)(2,1)}, u32[]{:S(2)}, u32[]{:S(2)}) collective-permute-start(bf16[128,1024]{1,0:T(8,128)(2,1)S(1)} %get-tuple-element.37), channel_id=1, source_target_pairs={{0,144},{16,128},{32,176},{48,160},{64,208},{80,192},{96,240},{112... | collective-permute-start | bytes 786440 | tf_op jit(solution)/shard_map/ppermute | solution.py:346
  25.0 9.4 %collective-permute-start.2 = (bf16[512,1024]{1,0:T(8,128)(2,1)S(1)}, bf16[512,1024]{1,0:T(8,128)(2,1)S(1)}, u32[]{:S(2)}, u32[]{:S(2)}) collective-permute-start(bf16[512,1024]{1,0:T(8,128)(2,1)S(1)} %copy-done.1), channel_id=1, source_target_pairs={{0,1},{1,0},{2,3},{3,2},{4,5},{5,4},{6,7},{7,6},{8,9},{9,8},{10,11... | collective-permute-start | bytes 3145736 | tf_op jit(solution)/shard_map/ppermute | solution.py:347
  26.4 8.0 %collective-permute-start.5 = (bf16[512,1024]{1,0:T(8,128)(2,1)S(1)}, bf16[512,1024]{1,0:T(8,128)(2,1)}, u32[]{:S(2)}, u32[]{:S(2)}) collective-permute-start(bf16[512,1024]{1,0:T(8,128)(2,1)S(1)} %collective-permute-done.4.refs_3_.refs_4_), channel_id=1, source_target_pairs={{0,1},{1,0},{2,3},{3,2},{4,5},{5,4},{6,7},{7,6},{8,9},{9,8},{10,11... | collective-permute-start | bytes 3145736 | tf_op jit(solution)/shard_map/ppermute | solution.py:348
  37.2 10.1 %collective-permute-start.8 = (bf16[128,1024]{1,0:T(8,128)(2,1)S(1)}, bf16[128,1024]{1,0:T(8,128)(2,1)S(1)}, u32[]{:S(2)}, u32[]{:S(2)}) collective-permute-start(bf16[128,1024]{1,0:T(8,128)(2,1)S(1)} %get-tuple-element.44), channel_id=1, source_target_pairs={{0,6},{1,7},{2,0},{3,1},{4,2},{5,3},{6,4},{7,5},{8,14},{9,15},{10,... | collective-permute-start | bytes 786440 | tf_op jit(solution)/shard_map/ppermute | solution.py:355
  41.2 4.0 %copy-start.7 = (bf16[128,1024]{1,0:T(8,128)(2,1)S(1)}, bf16[128,1024]{1,0:T(8,128)(2,1)}, u32[]{:S(2)}) copy-start(bf16[128,1024]{1,0:T(8,128)(2,1)} %copy-done.6) | copy-start | bytes 786436
  41.2 4.2 %copy-start.3 = (bf16[128,2048]{1,0:T(8,128)(2,1)S(1)}, bf16[128,2048]{1,0:T(8,128)(2,1)}, u32[]{:S(2)}) copy-start(bf16[128,2048]{1,0:T(8,128)(2,1)} %copy-done.2) | copy-start | bytes 1572868
  41.2 10.4 %collective-permute-start.9 = (bf16[128,1024]{1,0:T(8,128)(2,1)S(1)}, bf16[128,1024]{1,0:T(8,128)(2,1)S(1)}, u32[]{:S(2)}, u32[]{:S(2)}) collective-permute-start(bf16[128,1024]{1,0:T(8,128)(2,1)S(1)} %get-tuple-element.45), channel_id=1, source_target_pairs={{0,2},{1,3},{2,4},{3,5},{4,6},{5,7},{6,0},{7,1},{8,10},{9,11},{10,... | collective-permute-start | bytes 786440 | tf_op jit(solution)/shard_map/ppermute | solution.py:355
  43.4 8.2 %collective-permute-start.11 = (bf16[128,1024]{1,0:T(8,128)(2,1)S(1)}, bf16[128,1024]{1,0:T(8,128)(2,1)S(1)}, u32[]{:S(2)}, u32[]{:S(2)}) collective-permute-start(bf16[128,1024]{1,0:T(8,128)(2,1)S(1)} %far_product.1), channel_id=1, source_target_pairs={{0,4},{1,5},{2,6},{3,7},{4,0},{5,1},{6,2},{7,3},{8,12},{9,13},{10,... | collective-permute-start | bytes 786440 | tf_op jit(solution)/shard_map/ppermute | solution.py:355
  45.2 21.5 %collective-permute-start.3 = (bf16[128,1024]{1,0:T(8,128)(2,1)S(1)}, bf16[128,1024]{1,0:T(8,128)(2,1)S(1)}, u32[]{:S(2)}, u32[]{:S(2)}) collective-permute-start(bf16[128,1024]{1,0:T(8,128)(2,1)S(1)} %copy-done.7), channel_id=1, source_target_pairs={{0,16},{16,0},{32,48},{48,32},{64,80},{80,64},{96,112},{112,96},{1... | collective-permute-start | bytes 786440 | tf_op jit(solution)/shard_map/ppermute | solution.py:349
  45.3 6.2 %copy-start.5 = (f32[1024]{0:T(1024)S(1)}, f32[1024]{0:T(1024)}, u32[]{:S(2)}) copy-start(f32[1024]{0:T(1024)} %param.9) | copy-start | bytes 12292
  47.3 19.4 %copy-start.9 = (bf16[128,1024]{1,0:T(8,128)(2,1)S(1)}, bf16[128,1024]{1,0:T(8,128)(2,1)}, u32[]{:S(2)}) copy-start(bf16[128,1024]{1,0:T(8,128)(2,1)} %copy-done.8) | copy-start | bytes 786436
  51.9 4.5 %collective-permute-start.12 = (bf16[128,256]{1,0:T(8,128)(2,1)S(1)}, bf16[128,256]{1,0:T(8,128)(2,1)S(1)}, u32[]{:S(2)}, u32[]{:S(2)}) collective-permute-start(bf16[128,256]{1,0:T(8,128)(2,1)S(1)} %get-tuple-element.48), channel_id=1, source_target_pairs={{0,16},{16,0},{32,48},{48,32},{64,80},{80,64},{96,112},{112,96},{1... | collective-permute-start | bytes 196616 | tf_op jit(solution)/shard_map/ppermute | solution.py:360
  52.3 4.3 %collective-permute-start.13 = (bf16[128,256]{1,0:T(8,128)(2,1)S(1)}, bf16[128,256]{1,0:T(8,128)(2,1)S(1)}, u32[]{:S(2)}, u32[]{:S(2)}) collective-permute-start(bf16[128,256]{1,0:T(8,128)(2,1)S(1)} %get-tuple-element.49), channel_id=1, source_target_pairs={{0,128},{16,144},{32,160},{48,176},{64,192},{80,208},{96,224},{112... | collective-permute-start | bytes 196616 | tf_op jit(solution)/shard_map/ppermute | solution.py:360
  53.0 5.2 %collective-permute-start.14 = (bf16[128,256]{1,0:T(8,128)(2,1)S(1)}, bf16[128,256]{1,0:T(8,128)(2,1)S(1)}, u32[]{:S(2)}, u32[]{:S(2)}) collective-permute-start(bf16[128,256]{1,0:T(8,128)(2,1)S(1)} %get-tuple-element.50), channel_id=1, source_target_pairs={{0,144},{16,128},{32,176},{48,160},{64,208},{80,192},{96,240},{112... | collective-permute-start | bytes 196616 | tf_op jit(solution)/shard_map/ppermute | solution.py:360
  58.2 17.2 %collective-permute-start.17 = (bf16[512,256]{1,0:T(8,128)(2,1)S(1)}, bf16[512,256]{1,0:T(8,128)(2,1)S(1)}, u32[]{:S(2)}, u32[]{:S(2)}) collective-permute-start(bf16[512,256]{1,0:T(8,128)(2,1)S(1)} %constant_dynamic-update-slice_fusion.kv_ref), channel_id=1, source_target_pairs={{0,96},{16,112},{32,0},{48,16},{64,32},{80,48},{96,64},{112,80},{1... | collective-permute-start | bytes 786440 | tf_op jit(solution)/shard_map/ppermute | solution.py:363
  66.6 13.9 %collective-permute-start.15 = (bf16[512,256]{1,0:T(8,128)(2,1)S(1)}, bf16[512,256]{1,0:T(8,128)(2,1)S(1)}, u32[]{:S(2)}, u32[]{:S(2)}) collective-permute-start(bf16[512,256]{1,0:T(8,128)(2,1)S(1)} %constant_dynamic-update-slice_fusion.kv_ref), channel_id=1, source_target_pairs={{0,32},{16,48},{32,64},{48,80},{64,96},{80,112},{96,0},{112,16},{1... | collective-permute-start | bytes 786440 | tf_op jit(solution)/shard_map/ppermute | solution.py:362
  75.4 8.6 %collective-permute-start.18 = (bf16[256,256]{1,0:T(8,128)(2,1)S(1)}, bf16[256,256]{1,0:T(8,128)(2,1)S(1)}, u32[]{:S(2)}, u32[]{:S(2)}) collective-permute-start(bf16[256,256]{1,0:T(8,128)(2,1)S(1)} %slice.13), channel_id=1, source_target_pairs={{0,96},{16,112},{32,0},{48,16},{64,32},{80,48},{96,64},{112,80},{1... | collective-permute-start | bytes 393224 | tf_op jit(solution)/shard_map/ppermute | solution.py:365
  80.5 8.0 %collective-permute-start.16 = (bf16[256,256]{1,0:T(8,128)(2,1)S(1)}, bf16[256,256]{1,0:T(8,128)(2,1)S(1)}, u32[]{:S(2)}, u32[]{:S(2)}) collective-permute-start(bf16[256,256]{1,0:T(8,128)(2,1)S(1)} %slice.12), channel_id=1, source_target_pairs={{0,32},{16,48},{32,64},{48,80},{64,96},{80,112},{96,0},{112,16},{1... | collective-permute-start | bytes 393224 | tf_op jit(solution)/shard_map/ppermute | solution.py:364
  91.4 6.6 %collective-permute-start.21 = (bf16[128,1024]{1,0:T(8,128)(2,1)S(1)}, bf16[128,1024]{1,0:T(8,128)(2,1)S(1)}, u32[]{:S(2)}, u32[]{:S(2)}) collective-permute-start(bf16[128,1024]{1,0:T(8,128)(2,1)S(1)} %get-tuple-element.60), channel_id=1, source_target_pairs={{0,16},{16,0},{32,48},{48,32},{64,80},{80,64},{96,112},{112,96},{1... | collective-permute-start | bytes 786440 | tf_op jit(solution)/shard_map/ppermute | solution.py:395
  93.6 9.2 %collective-permute-start.20 = (bf16[128,1024]{1,0:T(8,128)(2,1)S(1)}, bf16[128,1024]{1,0:T(8,128)(2,1)S(1)}, u32[]{:S(2)}, u32[]{:S(2)}) collective-permute-start(bf16[128,1024]{1,0:T(8,128)(2,1)S(1)} %get-tuple-element.56), channel_id=1, source_target_pairs={{0,128},{16,144},{32,160},{48,176},{64,192},{80,208},{96,224},{112... | collective-permute-start | bytes 786440 | tf_op jit(solution)/shard_map/ppermute | solution.py:395
  95.0 8.5 %collective-permute-start.19 = (bf16[128,1024]{1,0:T(8,128)(2,1)S(1)}, bf16[128,1024]{1,0:T(8,128)(2,1)S(1)}, u32[]{:S(2)}, u32[]{:S(2)}) collective-permute-start(bf16[128,1024]{1,0:T(8,128)(2,1)S(1)} %get-tuple-element.55), channel_id=1, source_target_pairs={{0,144},{16,128},{32,176},{48,160},{64,208},{80,192},{96,240},{112... | collective-permute-start | bytes 786440 | tf_op jit(solution)/shard_map/ppermute | solution.py:395

commit v7 on v6

--- a/solution.py
+++ b/solution.py
@@ -339,14 +339,15 @@
     w_y = lax.ppermute(kv_weight, ("ctx", "fsdp"), DIAG_PAIRS)
 
     normed0, normed1, normed2, normed3, *q_parts = norm_call(pos, hidden, gain, q)
-    n2 = lax.ppermute(normed2, "fsdp", x_pairs(2))
     n1 = lax.ppermute(normed1, "fsdp", x_pairs(1))
     n3 = lax.ppermute(normed3, "fsdp", x_pairs(3))
-    q_parts[2] = lax.ppermute(q_parts[2], "ctx", member_pairs(2))
+    w_core = lax.ppermute(kv_weight, "fsdp", CORE_PAIRS)
+    n2 = lax.ppermute(normed2, "fsdp", x_pairs(2))
+
+    q_parts[2] = lax.ppermute(after(q_parts[2], w_core), "ctx", member_pairs(2))
     q_parts[3] = lax.ppermute(after(q_parts[3], q_parts[2]), "ctx", member_pairs(3))
-    w_core = lax.ppermute(after(kv_weight, q_parts[3]), "fsdp", CORE_PAIRS)
     w_yc = lax.ppermute(after(w_y, q_parts[3]), "fsdp", CORE_PAIRS)
-    q_parts[1] = lax.ppermute(after(q_parts[1], w_core), "ctx", member_pairs(1))
+    q_parts[1] = lax.ppermute(after(q_parts[1], q_parts[3]), "ctx", member_pairs(1))
     q4 = jnp.stack(q_parts)
 
     weights = [kv_weight, w_core, w_y, w_yc]

time: 105 us -> 106 us (level)
  starting transfers between devices: 34.9 us -> 36.1 us
    ppermute x1, waiting for transfers between devices: 7.25 us -> 0.51 us  [on_device(): lax.ppermute(after(q_parts[3], q_parts[2]), 'ctx', member_pairs(3))]
    ppermute x1, waiting for transfers between devices: 1.39 us -> 7.63 us  [on_device(): w_y = lax.ppermute(kv_weight, ('ctx', 'fsdp'), DIAG_PAIRS)]
    ppermute x1, waiting for transfers between devices: 4.34 us -> 1.91 us  [on_device(): down = lax.ppermute(group, 'ctx', z_pairs(-2))]
    ppermute x1, waiting for transfers between devices: 0.32 us -> 2.02 us  [on_device(): up = lax.ppermute(group, 'ctx', z_pairs(2))]
    unnamed x23 -> x21, local copies, waits for them, and re-layouts: 2.38 us -> 2.98 us
  transfers between devices with their start and end apart: 22 -> 22, of which waited for: 14 -> 13; matrix products, arithmetic and copies ran while one was open for 3% -> 3% of each run, Pallas kernels for 18% -> 18%
where the time goes in v7:
time: 106 us
  waiting for transfers between devices  40.6 us (38%)
  starting transfers between devices  36.1 us (34%)
  Pallas kernels  22.7 us (21%)
  local copies, waits for them, and re-layouts  4.3 us (4%)
  other arithmetic  2.03 us (2%)
    pallas_call x4, Pallas kernels, attend_call(): pl.pallas_call(kernel, in_specs=[pl.BlockSpec(memory_space=pltpu.SMEM)] +...  9.16 us
    ppermute x1, starting transfers between devices, on_device(): down = lax.ppermute(group, 'ctx', z_pairs(-2))  9.13 us
    ppermute x1, waiting for transfers between devices, on_device(): w_y = lax.ppermute(kv_weight, ('ctx', 'fsdp'), DIAG_PAIRS)  7.63 us
    pallas_call x3, Pallas kernels, product_call(): pl.pallas_call(lambda *refs: product_kernel(count, *refs), in_specs=[vm]...  6.96 us
    ppermute x1, waiting for transfers between devices, on_device(): n3 = lax.ppermute(normed3, 'fsdp', x_pairs(3))  6.57 us
    ppermute x3, waiting for transfers between devices, on_device(): lax.ppermute(o, 'ctx', member_pairs(k))  6.54 us
    ppermute x3, starting transfers between devices, on_device(): lax.ppermute(p, 'fsdp', x_pairs(k))  5.56 us
    ppermute x1, waiting for transfers between devices, on_device(): far0 = lax.ppermute(up[:256], 'ctx', z_pairs(2))  4.93 us
  transfers between devices with their start and end apart: 22, of which 13 were waited for; matrix products, arithmetic and copies ran while one was open for 3% of the time, Pallas kernels for 18%

profile of v7, /device:TPU:32, one launch (start us, length us, event | category | flops | bytes accessed | tf_op | source)
XLA Modules:
  0.0 106.1 jit_solution(2438208366879987062)
XLA Ops:
  0.0 3.1 %collective-permute-start.4 = (bf16[512,1024]{1,0:T(8,128)(2,1)}, bf16[512,1024]{1,0:T(8,128)(2,1)S(1)}, u32[]{:S(2)}, u32[]{:S(2)}) collective-permute-start(bf16[512,1024]{1,0:T(8,128)(2,1)} %refs_1_.3), channel_id=1, source_target_pairs={{0,136},{1,137},{2,138},{3,139},{4,140},{5,141},{6,142},{7,143},{8... | collective-permute-start | bytes 3145736 | tf_op jit(solution)/shard_map/ppermute | solution.py:339
  3.2 0.8 copy-done.4
  4.0 4.0 %norm.1 = (bf16[128,2048]{1,0:T(8,128)(2,1)S(1)}, bf16[128,2048]{1,0:T(8,128)(2,1)}, bf16[128,2048]{1,0:T(8,128)(2,1)}, bf16[128,2048]{1,0:T(8,128)(2,1)}, bf16[...) custom-call(s32[4]{0:T(128)S(1)} %pad_add_fusion.1.pos_ref, ...), custom_call_target="tpu_custom_call" | custom-call | flops 4194304 | bytes 4194304 | tf_op jit(solution)/shard_map/norm/pallas_call | solution.py:88
  7.9 0.8 copy-done.2
  8.7 0.7 copy-done.6
  9.4 0.7 copy-done.8
  10.3 1.5 %collective-permute-start.6 = (bf16[128,2048]{1,0:T(8,128)(2,1)}, bf16[128,2048]{1,0:T(8,128)(2,1)}, u32[]{:S(2)}, u32[]{:S(2)}) collective-permute-start(bf16[128,2048]{1,0:T(8,128)(2,1)} %get-tuple-element.42), channel_id=1, source_target_pairs={{0,2},{1,3},{2,4},{3,5},{4,6},{5,7},{6,0},{7,1},{8,10},{9,11},{10,... | collective-permute-start | bytes 1572872 | tf_op jit(solution)/shard_map/ppermute | solution.py:342
  11.8 1.7 %collective-permute-start.7 = (bf16[128,2048]{1,0:T(8,128)(2,1)}, bf16[128,2048]{1,0:T(8,128)(2,1)}, u32[]{:S(2)}, u32[]{:S(2)}) collective-permute-start(bf16[128,2048]{1,0:T(8,128)(2,1)} %get-tuple-element.43), channel_id=1, source_target_pairs={{0,6},{1,7},{2,0},{3,1},{4,2},{5,3},{6,4},{7,5},{8,14},{9,15},{10,... | collective-permute-start | bytes 1572872 | tf_op jit(solution)/shard_map/ppermute | solution.py:343
  13.5 1.8 %collective-permute-start.10 = (bf16[128,2048]{1,0:T(8,128)(2,1)}, bf16[128,2048]{1,0:T(8,128)(2,1)}, u32[]{:S(2)}, u32[]{:S(2)}) collective-permute-start(bf16[128,2048]{1,0:T(8,128)(2,1)} %get-tuple-element.46), channel_id=1, source_target_pairs={{0,4},{1,5},{2,6},{3,7},{4,0},{5,1},{6,2},{7,3},{8,12},{9,13},{10,... | collective-permute-start | bytes 1572872 | tf_op jit(solution)/shard_map/ppermute | solution.py:345
  15.3 3.5 %collective-permute-done.1 = bf16[128,1024]{1,0:T(8,128)(2,1)} collective-permute-done((bf16[128,1024]{1,0:T(8,128)(2,1)}, bf16[128,1024]{1,0:T(8,128)(2,1)}, u32[]{:S(2)}, u32[]{:S(2)}) %collective-permute-start.1) | collective-permute-done | bytes 262176 | tf_op jit(solution)/shard_map/ppermute | solution.py:347
  18.9 0.6 gather_fusion
  19.4 7.6 %collective-permute-done.4.refs_3_.refs_4_ = bf16[512,1024]{1,0:T(8,128)(2,1)S(1)} collective-permute-done((bf16[512,1024]{1,0:T(8,128)(2,1)}, bf16[512,1024]{1,0:T(8,128)(2,1)S(1)}, u32[]{:S(2)}, u32[]{:S(2)}) %collective-permute-start.4) | collective-permute-done | bytes 1048608 | tf_op jit(solution)/shard_map/ppermute | solution.py:339
  27.1 0.5 collective-permute-done.2
  27.8 0.6 gather_fusion.1
  28.5 0.3 fusion
  28.8 6.6 %collective-permute-done.7.refs_1_ = bf16[128,2048]{1,0:T(8,128)(2,1)} collective-permute-done((bf16[128,2048]{1,0:T(8,128)(2,1)}, bf16[128,2048]{1,0:T(8,128)(2,1)}, u32[]{:S(2)}, u32[]{:S(2)}) %collective-permute-start.7) | collective-permute-done | bytes 524320 | tf_op jit(solution)/shard_map/ppermute | solution.py:343
  35.4 2.8 %products.1 = (bf16[128,1024]{1,0:T(8,128)(2,1)S(1)}, bf16[128,1024]{1,0:T(8,128)(2,1)S(1)}) custom-call(bf16[128,2048]{1,0:T(8,128)(2,1)} %collective-permute-done.6.refs_0_, bf16[128,2048]{1,0:T(8,128)(2,1)} %collective-permute-done.7.refs_1_, bf16[512,1024]{1,0:T(8,128)(2,1)S(1)} %copy-done.1, bf16[512,1024]{1,0:T(8,128)(2,1)S(1)} %collective-permute-done.refs_2_.refs_3_, ...), custom_call_target="tpu_custom_call" | custom-call | flops 1073741824 | bytes 4194304 | tf_op jit(solution)/shard_map/products/pallas_call | solution.py:117
  38.2 4.0 %collective-permute-start.8 = (bf16[128,1024]{1,0:T(8,128)(2,1)S(1)}, bf16[128,1024]{1,0:T(8,128)(2,1)S(1)}, u32[]{:S(2)}, u32[]{:S(2)}) collective-permute-start(bf16[128,1024]{1,0:T(8,128)(2,1)S(1)} %get-tuple-element.44), channel_id=1, source_target_pairs={{0,6},{1,7},{2,0},{3,1},{4,2},{5,3},{6,4},{7,5},{8,14},{9,15},{10,... | collective-permute-start | bytes 786440 | tf_op jit(solution)/shard_map/ppermute | solution.py:356
  42.2 2.2 %far_product.1 = bf16[128,1024]{1,0:T(8,128)(2,1)S(1)} custom-call(bf16[128,2048]{1,0:T(8,128)(2,1)} %collective-permute-done.10.refs_0_, bf16[512,1024]{1,0:T(8,128)(2,1)S(1)} %copy-done.1, bf16[512,1024]{1,0:T(8,128)(2,1)S(1)} %collective-permute-done.refs_2_.refs_3_, bf16[512,1024]{1,0:T(8,128)(2,1)S(1)} %collective-permute-done.4.refs_3_.refs_4_, ...), custom_call_target="tpu_custom_call" | custom-call | flops 536870912 | bytes 4194304 | tf_op jit(solution)/shard_map/far_product/pallas_call | solution.py:117
  44.4 1.6 %collective-permute-start.11 = (bf16[128,1024]{1,0:T(8,128)(2,1)S(1)}, bf16[128,1024]{1,0:T(8,128)(2,1)S(1)}, u32[]{:S(2)}, u32[]{:S(2)}) collective-permute-start(bf16[128,1024]{1,0:T(8,128)(2,1)S(1)} %far_product.1), channel_id=1, source_target_pairs={{0,4},{1,5},{2,6},{3,7},{4,0},{5,1},{6,2},{7,3},{8,12},{9,13},{10,... | collective-permute-start | bytes 786440 | tf_op jit(solution)/shard_map/ppermute | solution.py:356
  46.2 0.8 collective-permute-start.3
  46.9 2.0 %own_product.1.own_ref = f32[128,1024]{1,0:T(8,128)S(1)} custom-call(bf16[128,2048]{1,0:T(8,128)(2,1)S(1)} %copy-done.3, bf16[512,1024]{1,0:T(8,128)(2,1)S(1)} %copy-done.1, bf16[512,1024]{1,0:T(8,128)(2,1)S(1)} %collective-permute-done.refs_2_.refs_3_, bf16[512,1024]{1,0:T(8,128)(2,1)S(1)} %collective-permute-done.4.refs_3_.refs_4_, ...), custom_call_target="tpu_custom_call" | custom-call | flops 536870912 | bytes 4194304 | tf_op jit(solution)/shard_map/own_product/pallas_call | solution.py:117
  48.9 3.7 %collective-permute-done.9.r3_ref = bf16[128,1024]{1,0:T(8,128)(2,1)S(1)} collective-permute-done((bf16[128,1024]{1,0:T(8,128)(2,1)S(1)}, bf16[128,1024]{1,0:T(8,128)(2,1)S(1)}, u32[]{:S(2)}, u32[]{:S(2)}) %collective-permute-start.9) | collective-permute-done | bytes 262176 | tf_op jit(solution)/shard_map/ppermute | solution.py:356
  52.6 0.4 keys_values.1
  53.0 0.9 collective-permute-start.12
  53.9 1.0 collective-permute-start.13
  54.9 1.8 %collective-permute-start.14 = (bf16[128,256]{1,0:T(8,128)(2,1)S(1)}, bf16[128,256]{1,0:T(8,128)(2,1)S(1)}, u32[]{:S(2)}, u32[]{:S(2)}) collective-permute-start(bf16[128,256]{1,0:T(8,128)(2,1)S(1)} %get-tuple-element.50), channel_id=1, source_target_pairs={{0,144},{16,128},{32,176},{48,160},{64,208},{80,192},{96,240},{112... | collective-permute-start | bytes 196616 | tf_op jit(solution)/shard_map/ppermute | solution.py:361
  56.7 0.8 collective-permute-done.12
  57.5 0.6 collective-permute-done.13
  58.1 1.9 %collective-permute-done.14 = bf16[128,256]{1,0:T(8,128)(2,1)S(1)} collective-permute-done((bf16[128,256]{1,0:T(8,128)(2,1)S(1)}, bf16[128,256]{1,0:T(8,128)(2,1)S(1)}, u32[]{:S(2)}, u32[]{:S(2)}) %collective-permute-start.14) | collective-permute-done | bytes 65568 | tf_op jit(solution)/shard_map/ppermute | solution.py:361
  60.1 9.1 %collective-permute-start.17 = (bf16[512,256]{1,0:T(8,128)(2,1)S(1)}, bf16[512,256]{1,0:T(8,128)(2,1)S(1)}, u32[]{:S(2)}, u32[]{:S(2)}) collective-permute-start(bf16[512,256]{1,0:T(8,128)(2,1)S(1)} %constant_dynamic-update-slice_fusion.kv_ref), channel_id=1, source_target_pairs={{0,96},{16,112},{32,0},{48,16},{64,32},{80,48},{96,64},{112,80},{1... | collective-permute-start | bytes 786440 | tf_op jit(solution)/shard_map/ppermute | solution.py:364
  69.3 1.2 %pad_maximum_fusion.q_ref.refs_1_ = bf16[4,128,1024]{2,1,0:T(8,128)(2,1)S(1)} fusion(bf16[1,128,1024]{2,1,0:T(8,128)(2,1)} %bitcast.18, bf16[1,128,1024]{2,1,0:T(8,128)(2,1)} %bitcast.17, bf16[1,128,1024]{2,1,0:T(8,128)(2,1)S(1)} %bitcast.33, bf16[1,128,1024]{2,1,0:T(8,128)(2,1)S(1)} %bitcast.28), kind=kLoop, calls=%fused_computation.2 | loop fusion | flops 1572864 | bytes 2097152 | tf_op jit(solution)/shard_map/stack | solution.py:351
  70.4 3.3 %attend_first.1 = (f32[4,1024,128]{2,1,0:T(8,128)S(1)}, f32[4,1024,256]{2,1,0:T(8,128)S(1)}) custom-call(s32[4,16]{1,0:T(4,128)S(1)} %select_select_fusion.flag_ref.refs_0_, bf16[4,128,1024]{2,1,0:T(8,128)(2,1)S(1)} %pad_maximum_fusion.q_ref.refs_1_, bf16[512,256]{1,0:T(8,128)(2,1)S(1)} %constant_dynamic-update-slice_fusion.kv_ref), custom_call_target="tpu_custom_call" | custom-call | flops 1073741824 | bytes 4194304 | tf_op jit(solution)/shard_map/attend_first/pallas_call | solution.py:275
  73.8 1.9 %collective-permute-done.17.down_ref = bf16[512,256]{1,0:T(8,128)(2,1)S(1)} collective-permute-done((bf16[512,256]{1,0:T(8,128)(2,1)S(1)}, bf16[512,256]{1,0:T(8,128)(2,1)S(1)}, u32[]{:S(2)}, u32[]{:S(2)}) %collective-permute-start.17) | collective-permute-done | bytes 262176 | tf_op jit(solution)/shard_map/ppermute | solution.py:364
  75.7 4.7 %collective-permute-start.18 = (bf16[256,256]{1,0:T(8,128)(2,1)S(1)}, bf16[256,256]{1,0:T(8,128)(2,1)S(1)}, u32[]{:S(2)}, u32[]{:S(2)}) collective-permute-start(bf16[256,256]{1,0:T(8,128)(2,1)S(1)} %slice.13), channel_id=1, source_target_pairs={{0,96},{16,112},{32,0},{48,16},{64,32},{80,48},{96,64},{112,80},{1... | collective-permute-start | bytes 393224 | tf_op jit(solution)/shard_map/ppermute | solution.py:366
  80.4 2.0 %collective-permute-done.15.up_ref = bf16[512,256]{1,0:T(8,128)(2,1)S(1)} collective-permute-done((bf16[512,256]{1,0:T(8,128)(2,1)S(1)}, bf16[512,256]{1,0:T(8,128)(2,1)S(1)}, u32[]{:S(2)}, u32[]{:S(2)}) %collective-permute-start.15) | collective-permute-done | bytes 262176 | tf_op jit(solution)/shard_map/ppermute | solution.py:363
  82.7 3.0 %attend_more.1 = (f32[4,1024,128]{2,1,0:T(8,128)S(1)}, f32[4,1024,256]{2,1,0:T(8,128)S(1)}) custom-call(s32[4,16]{1,0:T(4,128)S(1)} %select_select_fusion.flag_ref.refs_0_, bf16[4,128,1024]{2,1,0:T(8,128)(2,1)S(1)} %pad_maximum_fusion.q_ref.refs_1_, ...), custom_call_target="tpu_custom_call", output_to_operand_aliasing={{0}: (4, {}), {1}: (5, {})} | custom-call | flops 3221225472 | bytes 4194304 | tf_op jit(solution)/shard_map/attend_more/pallas_call | solution.py:275
  85.7 4.9 %collective-permute-done.16.refs_2_ = bf16[256,256]{1,0:T(8,128)(2,1)S(1)} collective-permute-done((bf16[256,256]{1,0:T(8,128)(2,1)S(1)}, bf16[256,256]{1,0:T(8,128)(2,1)S(1)}, u32[]{:S(2)}, u32[]{:S(2)}) %collective-permute-start.16) | collective-permute-done | bytes 131104 | tf_op jit(solution)/shard_map/ppermute | solution.py:365
  90.7 1.9 %attend_others.1 = (f32[4,1024,128]{2,1,0:T(8,128)S(1)}, f32[4,1024,256]{2,1,0:T(8,128)S(1)}, bf16[128,1024]{1,0:T(8,128)(2,1)S(1)}, bf16[128,1024]{1,0:T(8,128)(2,1)S(1)}) custom-call(s32[4,16]{1,0:T(4,128)S(1)} %select_select_fusion.flag_ref.refs_0_, ...), custom_call_target="tpu_custom_call", output_to_operand_aliasing={{0}: (4, {}), {1}: (5, {})} | custom-call | flops 1073741824 | bytes 4194304 | tf_op jit(solution)/shard_map/attend_others/pallas_call | solution.py:275
  92.6 1.0 attend_own.1
  93.6 1.7 %collective-permute-start.21 = (bf16[128,1024]{1,0:T(8,128)(2,1)S(1)}, bf16[128,1024]{1,0:T(8,128)(2,1)S(1)}, u32[]{:S(2)}, u32[]{:S(2)}) collective-permute-start(bf16[128,1024]{1,0:T(8,128)(2,1)S(1)} %get-tuple-element.60), channel_id=1, source_target_pairs={{0,16},{16,0},{32,48},{48,32},{64,80},{80,64},{96,112},{112,96},{1... | collective-permute-start | bytes 786440 | tf_op jit(solution)/shard_map/ppermute | solution.py:396
  95.3 0.6 collective-permute-start.20
  95.9 1.2 %collective-permute-start.19 = (bf16[128,1024]{1,0:T(8,128)(2,1)S(1)}, bf16[128,1024]{1,0:T(8,128)(2,1)S(1)}, u32[]{:S(2)}, u32[]{:S(2)}) collective-permute-start(bf16[128,1024]{1,0:T(8,128)(2,1)S(1)} %get-tuple-element.55), channel_id=1, source_target_pairs={{0,144},{16,128},{32,176},{48,160},{64,208},{80,192},{96,240},{112... | collective-permute-start | bytes 786440 | tf_op jit(solution)/shard_map/ppermute | solution.py:396
  97.1 2.9 %collective-permute-done.21.refs_2_ = bf16[128,1024]{1,0:T(8,128)(2,1)S(1)} collective-permute-done((bf16[128,1024]{1,0:T(8,128)(2,1)S(1)}, bf16[128,1024]{1,0:T(8,128)(2,1)S(1)}, u32[]{:S(2)}, u32[]{:S(2)}) %collective-permute-start.21) | collective-permute-done | bytes 262176 | tf_op jit(solution)/shard_map/ppermute | solution.py:396
  100.0 0.8 place.3.refs_2_
  100.8 3.7 %collective-permute-done.20.refs_1_ = bf16[128,1024]{1,0:T(8,128)(2,1)S(1)} collective-permute-done((bf16[128,1024]{1,0:T(8,128)(2,1)S(1)}, bf16[128,1024]{1,0:T(8,128)(2,1)S(1)}, u32[]{:S(2)}, u32[]{:S(2)}) %collective-permute-start.20) | collective-permute-done | bytes 262176 | tf_op jit(solution)/shard_map/ppermute | solution.py:396
  104.5 0.7 place.4.refs_2_
  105.2 0.7 place.5
  (53 shorter events, 1.3 us)
Async XLA Ops:
  0.0 18.8 %copy-start = (s32[1,16,16]{2,1,0:T(8,128)S(1)}, s32[1,16,16]{2,1,0:T(8,128)}, u32[]{:S(2)}) copy-start(s32[1,16,16]{2,1,0:T(8,128)} %param.11) | copy-start | bytes 3076
  0.0 35.4 %copy-start.1 = (bf16[512,1024]{1,0:T(8,128)(2,1)S(1)}, bf16[512,1024]{1,0:T(8,128)(2,1)}, u32[]{:S(2)}) copy-start(bf16[512,1024]{1,0:T(8,128)(2,1)} %refs_1_.3) | copy-start | bytes 3145732
  0.0 10.1 %collective-permute-start = (bf16[512,1024]{1,0:T(8,128)(2,1)}, bf16[512,1024]{1,0:T(8,128)(2,1)S(1)}, u32[]{:S(2)}, u32[]{:S(2)}) collective-permute-start(bf16[512,1024]{1,0:T(8,128)(2,1)} %refs_1_.3), channel_id=1, source_target_pairs={{0,1},{1,0},{2,3},{3,2},{4,5},{5,4},{6,7},{7,6},{8,9},{9,8},{10,11... | collective-permute-start | bytes 3145736 | tf_op jit(solution)/shard_map/ppermute | solution.py:344
  0.0 27.0 %collective-permute-start.4 = (bf16[512,1024]{1,0:T(8,128)(2,1)}, bf16[512,1024]{1,0:T(8,128)(2,1)S(1)}, u32[]{:S(2)}, u32[]{:S(2)}) collective-permute-start(bf16[512,1024]{1,0:T(8,128)(2,1)} %refs_1_.3), channel_id=1, source_target_pairs={{0,136},{1,137},{2,138},{3,139},{4,140},{5,141},{6,142},{7,143},{8... | collective-permute-start | bytes 3145736 | tf_op jit(solution)/shard_map/ppermute | solution.py:339
  3.2 0.8 copy-start.4
  7.9 0.8 copy-start.2
  8.7 0.7 copy-start.6
  9.4 0.7 copy-start.8
  10.1 8.7 %collective-permute-start.1 = (bf16[128,1024]{1,0:T(8,128)(2,1)}, bf16[128,1024]{1,0:T(8,128)(2,1)}, u32[]{:S(2)}, u32[]{:S(2)}) collective-permute-start(bf16[128,1024]{1,0:T(8,128)(2,1)} %get-tuple-element.37), channel_id=1, source_target_pairs={{0,128},{16,144},{32,160},{48,176},{64,192},{80,208},{96,224},{112... | collective-permute-start | bytes 786440 | tf_op jit(solution)/shard_map/ppermute | solution.py:347
  10.3 18.6 %collective-permute-start.6 = (bf16[128,2048]{1,0:T(8,128)(2,1)}, bf16[128,2048]{1,0:T(8,128)(2,1)}, u32[]{:S(2)}, u32[]{:S(2)}) collective-permute-start(bf16[128,2048]{1,0:T(8,128)(2,1)} %get-tuple-element.42), channel_id=1, source_target_pairs={{0,2},{1,3},{2,4},{3,5},{4,6},{5,7},{6,0},{7,1},{8,10},{9,11},{10,... | collective-permute-start | bytes 1572872 | tf_op jit(solution)/shard_map/ppermute | solution.py:342
  11.8 23.6 %collective-permute-start.7 = (bf16[128,2048]{1,0:T(8,128)(2,1)}, bf16[128,2048]{1,0:T(8,128)(2,1)}, u32[]{:S(2)}, u32[]{:S(2)}) collective-permute-start(bf16[128,2048]{1,0:T(8,128)(2,1)} %get-tuple-element.43), channel_id=1, source_target_pairs={{0,6},{1,7},{2,0},{3,1},{4,2},{5,3},{6,4},{7,5},{8,14},{9,15},{10,... | collective-permute-start | bytes 1572872 | tf_op jit(solution)/shard_map/ppermute | solution.py:343
  13.5 28.7 %collective-permute-start.10 = (bf16[128,2048]{1,0:T(8,128)(2,1)}, bf16[128,2048]{1,0:T(8,128)(2,1)}, u32[]{:S(2)}, u32[]{:S(2)}) collective-permute-start(bf16[128,2048]{1,0:T(8,128)(2,1)} %get-tuple-element.46), channel_id=1, source_target_pairs={{0,4},{1,5},{2,6},{3,7},{4,0},{5,1},{6,2},{7,3},{8,12},{9,13},{10,... | collective-permute-start | bytes 1572872 | tf_op jit(solution)/shard_map/ppermute | solution.py:345
  18.8 8.8 %collective-permute-start.2 = (bf16[128,1024]{1,0:T(8,128)(2,1)}, bf16[128,1024]{1,0:T(8,128)(2,1)}, u32[]{:S(2)}, u32[]{:S(2)}) collective-permute-start(bf16[128,1024]{1,0:T(8,128)(2,1)} %copy-done.8), channel_id=1, source_target_pairs={{0,144},{16,128},{32,176},{48,160},{64,208},{80,192},{96,240},{112... | collective-permute-start | bytes 786440 | tf_op jit(solution)/shard_map/ppermute | solution.py:348
  27.6 7.8 %collective-permute-start.5 = (bf16[512,1024]{1,0:T(8,128)(2,1)S(1)}, bf16[512,1024]{1,0:T(8,128)(2,1)}, u32[]{:S(2)}, u32[]{:S(2)}) collective-permute-start(bf16[512,1024]{1,0:T(8,128)(2,1)S(1)} %collective-permute-done.4.refs_3_.refs_4_), channel_id=1, source_target_pairs={{0,1},{1,0},{2,3},{3,2},{4,5},{5,4},{6,7},{7,6},{8,9},{9,8},{10,11... | collective-permute-start | bytes 3145736 | tf_op jit(solution)/shard_map/ppermute | solution.py:349
  38.2 10.7 %collective-permute-start.8 = (bf16[128,1024]{1,0:T(8,128)(2,1)S(1)}, bf16[128,1024]{1,0:T(8,128)(2,1)S(1)}, u32[]{:S(2)}, u32[]{:S(2)}) collective-permute-start(bf16[128,1024]{1,0:T(8,128)(2,1)S(1)} %get-tuple-element.44), channel_id=1, source_target_pairs={{0,6},{1,7},{2,0},{3,1},{4,2},{5,3},{6,4},{7,5},{8,14},{9,15},{10,... | collective-permute-start | bytes 786440 | tf_op jit(solution)/shard_map/ppermute | solution.py:356
  42.2 4.0 %copy-start.7 = (bf16[128,1024]{1,0:T(8,128)(2,1)S(1)}, bf16[128,1024]{1,0:T(8,128)(2,1)}, u32[]{:S(2)}) copy-start(bf16[128,1024]{1,0:T(8,128)(2,1)} %copy-done.6) | copy-start | bytes 786436
  42.2 4.7 %copy-start.3 = (bf16[128,2048]{1,0:T(8,128)(2,1)S(1)}, bf16[128,2048]{1,0:T(8,128)(2,1)}, u32[]{:S(2)}) copy-start(bf16[128,2048]{1,0:T(8,128)(2,1)} %copy-done.2) | copy-start | bytes 1572868
  42.2 10.4 %collective-permute-start.9 = (bf16[128,1024]{1,0:T(8,128)(2,1)S(1)}, bf16[128,1024]{1,0:T(8,128)(2,1)S(1)}, u32[]{:S(2)}, u32[]{:S(2)}) collective-permute-start(bf16[128,1024]{1,0:T(8,128)(2,1)S(1)} %get-tuple-element.45), channel_id=1, source_target_pairs={{0,2},{1,3},{2,4},{3,5},{4,6},{5,7},{6,0},{7,1},{8,10},{9,11},{10,... | collective-permute-start | bytes 786440 | tf_op jit(solution)/shard_map/ppermute | solution.py:356
  44.4 8.2 %collective-permute-start.11 = (bf16[128,1024]{1,0:T(8,128)(2,1)S(1)}, bf16[128,1024]{1,0:T(8,128)(2,1)S(1)}, u32[]{:S(2)}, u32[]{:S(2)}) collective-permute-start(bf16[128,1024]{1,0:T(8,128)(2,1)S(1)} %far_product.1), channel_id=1, source_target_pairs={{0,4},{1,5},{2,6},{3,7},{4,0},{5,1},{6,2},{7,3},{8,12},{9,13},{10,... | collective-permute-start | bytes 786440 | tf_op jit(solution)/shard_map/ppermute | solution.py:356
  46.2 23.1 %collective-permute-start.3 = (bf16[128,1024]{1,0:T(8,128)(2,1)S(1)}, bf16[128,1024]{1,0:T(8,128)(2,1)S(1)}, u32[]{:S(2)}, u32[]{:S(2)}) collective-permute-start(bf16[128,1024]{1,0:T(8,128)(2,1)S(1)} %copy-done.7), channel_id=1, source_target_pairs={{0,16},{16,0},{32,48},{48,32},{64,80},{80,64},{96,112},{112,96},{1... | collective-permute-start | bytes 786440 | tf_op jit(solution)/shard_map/ppermute | solution.py:350
  46.9 5.7 %copy-start.5 = (f32[1024]{0:T(1024)S(1)}, f32[1024]{0:T(1024)}, u32[]{:S(2)}) copy-start(f32[1024]{0:T(1024)} %param.9) | copy-start | bytes 12292
  53.0 4.5 %collective-permute-start.12 = (bf16[128,256]{1,0:T(8,128)(2,1)S(1)}, bf16[128,256]{1,0:T(8,128)(2,1)S(1)}, u32[]{:S(2)}, u32[]{:S(2)}) collective-permute-start(bf16[128,256]{1,0:T(8,128)(2,1)S(1)} %get-tuple-element.48), channel_id=1, source_target_pairs={{0,16},{16,0},{32,48},{48,32},{64,80},{80,64},{96,112},{112,96},{1... | collective-permute-start | bytes 196616 | tf_op jit(solution)/shard_map/ppermute | solution.py:361
  53.9 4.3 %collective-permute-start.13 = (bf16[128,256]{1,0:T(8,128)(2,1)S(1)}, bf16[128,256]{1,0:T(8,128)(2,1)S(1)}, u32[]{:S(2)}, u32[]{:S(2)}) collective-permute-start(bf16[128,256]{1,0:T(8,128)(2,1)S(1)} %get-tuple-element.49), channel_id=1, source_target_pairs={{0,128},{16,144},{32,160},{48,176},{64,192},{80,208},{96,224},{112... | collective-permute-start | bytes 196616 | tf_op jit(solution)/shard_map/ppermute | solution.py:361
  54.9 5.2 %collective-permute-start.14 = (bf16[128,256]{1,0:T(8,128)(2,1)S(1)}, bf16[128,256]{1,0:T(8,128)(2,1)S(1)}, u32[]{:S(2)}, u32[]{:S(2)}) collective-permute-start(bf16[128,256]{1,0:T(8,128)(2,1)S(1)} %get-tuple-element.50), channel_id=1, source_target_pairs={{0,144},{16,128},{32,176},{48,160},{64,208},{80,192},{96,240},{112... | collective-permute-start | bytes 196616 | tf_op jit(solution)/shard_map/ppermute | solution.py:361
  60.1 15.6 %collective-permute-start.17 = (bf16[512,256]{1,0:T(8,128)(2,1)S(1)}, bf16[512,256]{1,0:T(8,128)(2,1)S(1)}, u32[]{:S(2)}, u32[]{:S(2)}) collective-permute-start(bf16[512,256]{1,0:T(8,128)(2,1)S(1)} %constant_dynamic-update-slice_fusion.kv_ref), channel_id=1, source_target_pairs={{0,96},{16,112},{32,0},{48,16},{64,32},{80,48},{96,64},{112,80},{1... | collective-permute-start | bytes 786440 | tf_op jit(solution)/shard_map/ppermute | solution.py:364
  69.2 13.2 %collective-permute-start.15 = (bf16[512,256]{1,0:T(8,128)(2,1)S(1)}, bf16[512,256]{1,0:T(8,128)(2,1)S(1)}, u32[]{:S(2)}, u32[]{:S(2)}) collective-permute-start(bf16[512,256]{1,0:T(8,128)(2,1)S(1)} %constant_dynamic-update-slice_fusion.kv_ref), channel_id=1, source_target_pairs={{0,32},{16,48},{32,64},{48,80},{64,96},{80,112},{96,0},{112,16},{1... | collective-permute-start | bytes 786440 | tf_op jit(solution)/shard_map/ppermute | solution.py:363
  75.7 10.1 %collective-permute-start.18 = (bf16[256,256]{1,0:T(8,128)(2,1)S(1)}, bf16[256,256]{1,0:T(8,128)(2,1)S(1)}, u32[]{:S(2)}, u32[]{:S(2)}) collective-permute-start(bf16[256,256]{1,0:T(8,128)(2,1)S(1)} %slice.13), channel_id=1, source_target_pairs={{0,96},{16,112},{32,0},{48,16},{64,32},{80,48},{96,64},{112,80},{1... | collective-permute-start | bytes 393224 | tf_op jit(solution)/shard_map/ppermute | solution.py:366
  82.4 8.2 %collective-permute-start.16 = (bf16[256,256]{1,0:T(8,128)(2,1)S(1)}, bf16[256,256]{1,0:T(8,128)(2,1)S(1)}, u32[]{:S(2)}, u32[]{:S(2)}) collective-permute-start(bf16[256,256]{1,0:T(8,128)(2,1)S(1)} %slice.12), channel_id=1, source_target_pairs={{0,32},{16,48},{32,64},{48,80},{64,96},{80,112},{96,0},{112,16},{1... | collective-permute-start | bytes 393224 | tf_op jit(solution)/shard_map/ppermute | solution.py:365
  93.6 6.5 %collective-permute-start.21 = (bf16[128,1024]{1,0:T(8,128)(2,1)S(1)}, bf16[128,1024]{1,0:T(8,128)(2,1)S(1)}, u32[]{:S(2)}, u32[]{:S(2)}) collective-permute-start(bf16[128,1024]{1,0:T(8,128)(2,1)S(1)} %get-tuple-element.60), channel_id=1, source_target_pairs={{0,16},{16,0},{32,48},{48,32},{64,80},{80,64},{96,112},{112,96},{1... | collective-permute-start | bytes 786440 | tf_op jit(solution)/shard_map/ppermute | solution.py:396
  95.3 9.2 %collective-permute-start.20 = (bf16[128,1024]{1,0:T(8,128)(2,1)S(1)}, bf16[128,1024]{1,0:T(8,128)(2,1)S(1)}, u32[]{:S(2)}, u32[]{:S(2)}) collective-permute-start(bf16[128,1024]{1,0:T(8,128)(2,1)S(1)} %get-tuple-element.56), channel_id=1, source_target_pairs={{0,128},{16,144},{32,160},{48,176},{64,192},{80,208},{96,224},{112... | collective-permute-start | bytes 786440 | tf_op jit(solution)/shard_map/ppermute | solution.py:396
  95.9 9.3 %collective-permute-start.19 = (bf16[128,1024]{1,0:T(8,128)(2,1)S(1)}, bf16[128,1024]{1,0:T(8,128)(2,1)S(1)}, u32[]{:S(2)}, u32[]{:S(2)}) collective-permute-start(bf16[128,1024]{1,0:T(8,128)(2,1)S(1)} %get-tuple-element.55), channel_id=1, source_target_pairs={{0,144},{16,128},{32,176},{48,160},{64,208},{80,192},{96,240},{112... | collective-permute-start | bytes 786440 | tf_op jit(solution)/shard_map/ppermute | solution.py:396
